TPU v7x, 32 devices: a whole 2x2x4 slice. The times are simulated.
32 devices in a mesh: blk: 8 (over z, y), req: 4 (over x, core).
Axes of the slice: x: 2, y: 2, z: 4, core: 2. Of those that a mesh axis runs over, the one named last changes fastest.
Arguments:
- tokens_in: bfloat16 [4, 1024, 1792], P('req', 'blk'), may hold values from -6 to 6
- query_weight: bfloat16 [1792, 256], replicated, may hold values from -0.125 to 0.125
- key_weight: bfloat16 [1792, 256], replicated, may hold values from -0.125 to 0.125
- value_weight: bfloat16 [1792, 1792], replicated, may hold values from -0.125 to 0.125
- conv_weight: float32 [3, 1792], replicated, may hold values from -3 to 3
- prompt_lengths: int32 [4], P('req'), may hold values from 512 to 1024, as said below
- decode_map: int32 [4], P('req'), may hold values from 0 to 3, each once
Outputs:
- mixed: bfloat16 [4, 1024, 1792], P('req', 'blk')
- decode_state: float32 [4, 273, 1792], P('req', None, 'blk')
- decode_norm: float32 [4, 273, 16], P('req')
Inputs may be any that keep to these rules, and one draw needn't show every extreme that they name: `prompt_lengths`: some prompt has exactly 1024 live tokens. `decode_map`: each decode slot receives exactly one prompt.
All inputs are finite; a program needn't handle non-finite values.
Results may differ from a plain program's by a relative error of at most 0.0057.
Values may be sent and summed in bfloat16 or wider, within the bound.
No kernel may reach another device: no remote copies, remote signals or barrier semaphores. Data moves between devices by JAX's collectives and lax.ppermute only.
A program may use at most 384 MiB of HBM per device.

v0:
```python
import math

import jax
import jax.numpy as jnp
from jax import lax
from jax.sharding import PartitionSpec as P

HEADS = 16
FEAT = 16
CONV = 3


def from_behind(array, axis, by):
    devices = lax.axis_size(axis)
    pairs = [(i, i + by) for i in range(devices) if 0 <= i + by < devices]
    return lax.ppermute(array, axis, pairs)


def entering(part, axis, combine, identity):
    place = lax.axis_index(axis)
    gathered = jax.tree.map(lambda a: lax.all_gather(a, axis), part)
    state = jax.tree.map(lambda a, e: jnp.zeros_like(a) + jnp.asarray(e, a.dtype), part, identity)

    def one(turn, state):
        return combine(
            state, jax.tree.map(lambda a: lax.dynamic_index_in_dim(a, turn, 0, False), gathered)
        )

    return lax.fori_loop(0, place, one, state)


def features_last(x):
    half = x * FEAT ** (-0.25)
    outer = half[:, :, None, :] * half[:, None, :, :]
    flat = outer.reshape(half.shape[0], FEAT * FEAT, half.shape[2]) * math.sqrt(0.5)
    ones = jnp.ones((half.shape[0], 1, half.shape[2]), jnp.float32)
    return jnp.concatenate([ones, half, flat], 1)


def add_pair(earlier, later):
    return (earlier[0] + later[0], earlier[1] + later[1])


def route_slot(pair, decode_map):
    groups = lax.axis_size("req")
    slots = (jnp.arange(groups, dtype=jnp.int32) == decode_map[0]).astype(jnp.float32)
    sent = (slots[:, None, None] * pair[0][None], slots[:, None, None] * pair[1][None])
    got = (
        lax.all_to_all(sent[0], "req", split_axis=0, concat_axis=0, tiled=True),
        lax.all_to_all(sent[1], "req", split_axis=0, concat_axis=0, tiled=True),
    )
    return (jnp.sum(got[0], 0), jnp.sum(got[1], 0))


def reduce_blocks(pair):
    return (
        lax.psum_scatter(pair[0], "blk", scatter_dimension=1, tiled=True),
        lax.psum_scatter(pair[1], "blk", scatter_dimension=1, tiled=True),
    )


def on_device(
    tokens_in, query_weight, key_weight, value_weight, conv_weight, prompt_lengths, decode_map
):
    rows = tokens_in.shape[1]
    width = tokens_in.shape[2]
    blocks = lax.axis_size("blk")
    head_size = width // HEADS
    hi = lax.Precision.HIGHEST
    inputs = tokens_in[0]
    queries = jnp.einsum(
        "dk,td->kt", query_weight, inputs, preferred_element_type=jnp.float32
    ).reshape(HEADS, FEAT, rows)
    keys = jnp.einsum("dk,td->kt", key_weight, inputs, preferred_element_type=jnp.float32).reshape(
        HEADS, FEAT, rows
    )
    values = jnp.dot(inputs, value_weight, preferred_element_type=jnp.float32).astype(jnp.bfloat16)
    earlier = from_behind(values[rows - (CONV - 1) :], "blk", 1)
    extended = jnp.concatenate([earlier, values], 0).astype(jnp.float32)
    conv = jnp.zeros((rows, width), jnp.float32)
    for tap in range(CONV):
        conv = conv + conv_weight[tap][None, :] * extended[CONV - 1 - tap : CONV - 1 - tap + rows]
    conv_t = conv.astype(jnp.bfloat16).astype(jnp.float32).T.reshape(HEADS, head_size, rows)
    start = lax.axis_index("blk") * rows
    live = (start + jnp.arange(rows, dtype=jnp.int32) < prompt_lengths[0]).astype(jnp.float32)
    feat_q = features_last(queries)
    feat_k = features_last(keys) * live[None, None, :]
    own_state = jnp.einsum("hft,hct->hfc", feat_k, conv_t, precision=hi)
    own_norm = jnp.sum(feat_k, 2)
    zero_state = jnp.zeros_like(own_state)
    zero_norm = jnp.zeros_like(own_norm)
    prior_state, prior_norm = entering(
        (own_state, own_norm), "blk", add_pair, (zero_state, zero_norm)
    )
    causal = (jnp.arange(rows)[:, None] >= jnp.arange(rows)[None, :]).astype(jnp.float32)
    scores = jnp.einsum("hft,hfs->hts", feat_q, feat_k, precision=hi) * causal[None]
    num = jnp.einsum("hts,hcs->hct", scores, conv_t, precision=hi) + jnp.einsum(
        "hft,hfc->hct", feat_q, prior_state, precision=hi
    )
    den = (
        jnp.sum(scores, -1)
        + jnp.einsum("hft,hf->ht", feat_q, prior_norm, precision=hi)
        + (1.0 - live)[None, :]
    )
    result = jnp.where(live[None, None, :] > 0, num / den[:, None, :], 0.0)
    mixed = result.reshape(width, rows).T.reshape(1, rows, width).astype(jnp.bfloat16)
    state_flat = jnp.transpose(own_state, (1, 0, 2)).reshape(own_state.shape[1], width)
    pair = (state_flat, jnp.tile(own_norm.T, (1, blocks)))
    final = route_slot(reduce_blocks(pair), decode_map)
    return (mixed, final[0][None], final[1][None])


def solution(mesh):
    return jax.shard_map(
        on_device,
        mesh=mesh,
        in_specs=(P("req", "blk", None), P(), P(), P(), P(), P("req"), P("req")),
        out_specs=(P("req", "blk", None), P("req", None, "blk"), P("req", None, None)),
        check_vma=False,
    )
```

profile of v0, /device:TPU:31, one launch (start us, length us, event | category | flops | bytes accessed | tf_op | source)
XLA Modules:
  0.0 540.5 jit_solution(6186318176620303270)
XLA Ops:
  8.2 3.8 convolution_convert_fusion
  19.7 3.7 fusion.22
  23.4 2.2 copy.56
  25.7 1.9 copy.45
  30.0 26.4 %all-gather.1 = f32[128,273]{1,0:T(8,128)} all-gather(f32[16,273]{1,0:T(8,128)S(1)} %fusion.21), channel_id=3, replica_groups=mesh['blk'=8,'req'=4] {'blk'}, dimensions={0}, use_global_device_ids=true | all-gather | bytes 157248 | tf_op jit(solution)/shard_map/all_gather | solution.py:21
  56.9 20.2 %reduce-scatter.5.cloned.1.call-done = f32[273,16]{0,1:T(8,128)} async-done(((f32[273,128]{0,1:T(8,128)}), f32[273,16]{0,1:T(8,128)}) %reduce-scatter.5.cloned.1.call-update) | async-done | bytes 17488 | tf_op jit(solution)/shard_map/reduce_scatter | solution.py:58
  77.0 1.5 broadcast_multiply_fusion.1
  78.5 5.8 %all-to-all-start.1 = ((f32[4,273,16]{1,2,0:T(8,128)}), f32[4,273,16]{1,2,0:T(8,128)S(1)}, u32[]{:S(2)}, u32[]{:S(2)}) async-start(f32[4,273,16]{1,2,0:T(8,128)} %broadcast_multiply_fusion.1), calls=%async_computation.2 | async-start | bytes 196608 | tf_op jit(solution)/shard_map/all_to_all | solution.py:50
  84.3 67.7 %reduce-scatter.7.cloned.1.call-done = f32[224,273]{1,0:T(8,128)} async-done(((f32[1792,273]{1,0:T(8,128)}), f32[224,273]{1,0:T(8,128)}) %reduce-scatter.7.cloned.1.call-update) | async-done | bytes 244624
  154.3 5.5 %all-to-all-start = ((f32[4,273,224]{2,1,0:T(8,128)}), f32[4,273,224]{2,1,0:T(8,128)}, u32[]{:S(2)}, u32[]{:S(2)}) async-start(f32[4,273,224]{2,1,0:T(8,128)} %broadcast_multiply_fusion), calls=%async_computation | async-start | bytes 2293760 | tf_op jit(solution)/shard_map/all_to_all | solution.py:49
  161.4 6.5 %fusion.23 = (f32[16,128]{1,0:T(8,128)S(1)}, f32[16,128,128]{1,2,0:T(8,128)}) fusion(f32[128,128]{0,1:T(8,128)S(1)} %fusion.16, f32[16,256,128]{2,1,0:T(8,128)S(1)} %bitcast.62, f32[16,16,128]{2,1,0:T(8,128)S(1)} %convolution_multiply_fusion.1, f32[273]{0:T(512)S(1)} %pad.3.clone, f32[128]{0:T(128)S(1)} %get-tuple-element.79, ...), kind=kOutput, calls=%fused_computation.50 | convolution fusion | flops 862101504 | bytes 5580356 | tf_op jit(solution)/shard_map/hft,hfs->hts/dot_general | solution.py:96
  168.6 4.9 all-to-all-done
  173.4 1.4 reduce_sum.38
  175.8 322.3 %all-gather.4.cloned.1.call-done = f32[128,273,112]{2,0,1:T(8,128)} async-done(((f32[16,273,112]{2,0,1:T(8,128)}), f32[128,273,112]{2,0,1:T(8,128)}) %all-gather.4.cloned.1.call-update) | async-done | bytes 15654928 | tf_op jit(solution)/shard_map/all_gather | solution.py:21
  498.2 25.2 %while.12 = (s32[]{:T(128)}, f32[16,273,112]{2,1,0:T(8,128)S(1)}, f32[16,273]{1,0:T(8,128)S(1)}, s32[]{:T(128)}, f32[8,16,273,112]{3,1,0,2:T(8,128)}, /*index=5*...) while((s32[]{:T(128)}, f32[16,273,112]{2,1,0:T(8,128)S(1)}, f32[16,273]{1,0:T(8,128)S(1)}, s32[]{:T(128)}, ...), condition=%wide.region_2.3_spmd, body=%wide.region_1.2_spmd.sunk | while | flops 493589 | bytes 9836871 | solution.py:29
  498.3 1.8 constant_dynamic-slice_fusion.2
  501.9 1.8 constant_dynamic-slice_fusion.2
  505.5 1.8 constant_dynamic-slice_fusion.2
  509.1 1.8 constant_dynamic-slice_fusion.2
  512.7 1.8 constant_dynamic-slice_fusion.2
  516.3 1.8 constant_dynamic-slice_fusion.2
  519.9 1.8 constant_dynamic-slice_fusion.2
  523.5 3.5 fusion.4
  527.0 5.2 fusion.5
  (68 shorter events, 30.1 us)
Async XLA Ops:
  7.2 1.0 copy-start
  7.2 6.2 %copy-start.5 = (bf16[1792,256]{1,0:T(8,128)(2,1)S(1)}, bf16[1792,256]{1,0:T(8,128)(2,1)}, u32[]{:S(2)}) copy-start(bf16[1792,256]{1,0:T(8,128)(2,1)} %param.11) | copy-start | bytes 2752516
  7.2 69.8 %reduce-scatter.5.cloned.1.call-start = ((), (), s32[]{:S(2)}) async-start(), calls=%async_computation.4 | async-start | bytes 221184 | tf_op jit(solution)/shard_map/reduce_scatter | solution.py:58
  12.1 5.2 collective-permute-start
  14.4 2.8 copy-start.7
  14.7 3.8 copy-start.1
  17.2 134.8 %reduce-scatter.7.cloned.1.call-start = ((), (), s32[]{:S(2)}) async-start(), calls=%async_computation.6 | async-start | bytes 3096576
  25.7 472.4 %all-gather.4.cloned.1.call-start = ((), (), s32[]{:S(2)}) async-start(), calls=%async_computation.5 | async-start | bytes 20127744 | tf_op jit(solution)/shard_map/all_gather | solution.py:21
  27.6 1.2 copy-start.6
  78.5 75.8 %all-to-all-start.1 = ((f32[4,273,16]{1,2,0:T(8,128)}), f32[4,273,16]{1,2,0:T(8,128)S(1)}, u32[]{:S(2)}, u32[]{:S(2)}) async-start(f32[4,273,16]{1,2,0:T(8,128)} %broadcast_multiply_fusion.1), calls=%async_computation.2 | async-start | bytes 196608 | tf_op jit(solution)/shard_map/all_to_all | solution.py:50
  154.3 7.1 %copy-start.2 = (f32[16,16,16,128]{3,2,1,0:T(8,128)S(1)}, f32[16,16,16,128]{3,2,1,0:T(8,128)}, u32[]{:S(2)}) copy-start(f32[16,16,16,128]{3,2,1,0:T(8,128)} %copy-done.1) | copy-start | bytes 6291460
  154.3 19.1 %all-to-all-start = ((f32[4,273,224]{2,1,0:T(8,128)}), f32[4,273,224]{2,1,0:T(8,128)}, u32[]{:S(2)}, u32[]{:S(2)}) async-start(f32[4,273,224]{2,1,0:T(8,128)} %broadcast_multiply_fusion), calls=%async_computation | async-start | bytes 2293760 | tf_op jit(solution)/shard_map/all_to_all | solution.py:49
  160.1 1.3 copy-start.3
  523.5 3.5 copy-start.4
  527.0 5.2 copy-start.8
Sparse Core Ops, SparseCore 0:
  17.3 59.7 reduce-scatter.4
  80.6 71.3 reduce-scatter.6
  153.5 344.4 all-gather.3
where the time goes:
time: 542 us; the launch traced here: 540 us
  waiting for transfers between devices  415 us (77%)
  local copies, waits for them, and re-layouts  26.7 us (5%)
  blocking collectives  26.4 us (5%)
  matrix products  24.2 us (4%)
  other arithmetic  19.9 us (4%)
  between operations  15.3 us (3%)
  starting transfers between devices  12.7 us (2%)
    all_gather x1, waiting for transfers between devices, entering(): gathered = jax.tree.map(lambda a: lax.all_gather(a, axis), part)  322 us
    unnamed x4, waiting for transfers between devices  67.8 us
    all_gather x1, blocking collectives, entering(): gathered = jax.tree.map(lambda a: lax.all_gather(a, axis), part)  26.4 us
    reduce_scatter x1, waiting for transfers between devices, reduce_blocks(): lax.psum_scatter(pair[1], 'blk', scatter_dimension=1, tiled=True)  20.2 us
    dynamic_slice x7, local copies, waits for them, and re-layouts, one(): lax.dynamic_index_in_dim(a, turn, 0, False)  12.7 us
    add x14, other arithmetic, add_pair(): return (earlier[0] + later[0], earlier[1] + later[1])  12.5 us
  transfers between devices with their start and end apart: 6, of which 4 were waited for; matrix products, arithmetic and copies ran while one was open for 5% of the time, Pallas kernels for 0%

commit v1 on v0

--- a/solution.py
+++ b/solution.py
@@ -1,13 +1,428 @@
+import functools
 import math
 
 import jax
 import jax.numpy as jnp
+import numpy as np
 from jax import lax
+from jax.experimental import pallas as pl
+from jax.experimental.pallas import tpu as pltpu
 from jax.sharding import PartitionSpec as P
 
 HEADS = 16
 FEAT = 16
 CONV = 3
+
+GROUP = 4
+SYM = 160
+LANES = 128
+SUMS = 48
+INFO = 34
+f32 = jnp.float32
+bf16 = jnp.bfloat16
+NT = (((1,), (1,)), ((), ()))
+NN = (((1,), (0,)), ((), ()))
+
+
+def dot(a, b, dims=NN):
+    return lax.dot_general(a, b, dims, preferred_element_type=f32)
+
+
+def iota(shape, axis):
+    return lax.broadcasted_iota(jnp.int32, shape, axis)
+
+
+def symmetric(y, scale_square):
+    twice = jnp.concatenate([y, y], 0)
+    rows = [y * y * scale_square] + [y * twice[o : o + FEAT] for o in range(1, 8)]
+    rest = jnp.where(iota((8, y.shape[1]), 0) == 0, 1.0, 0.0)
+    return jnp.concatenate(rows + [y, y[:8] * y[8:], rest], 0)
+
+
+def project_kernel(
+    length, x, wq, wk, wv, conv, o0, o1, o2, o3, taps, wv_v, wqk_v, vt, qkt, taps_v, sems
+):
+    rows = x.shape[0]
+    width = wv.shape[1]
+    keyed = wq.shape[1]
+    tile = 256
+    copies = [
+        pltpu.make_async_copy(wk, wqk_v.at[1], sems.at[0]),
+        pltpu.make_async_copy(wq, wqk_v.at[0], sems.at[1]),
+    ]
+    for j in range(width // tile):
+        cut = pl.ds(j * tile, tile)
+        copies.append(pltpu.make_async_copy(wv.at[:, cut], wv_v.at[:, cut], sems.at[2 + j]))
+    for copy in copies:
+        copy.start()
+    place = lax.axis_index("blk")
+    mine = lax.rem(place, GROUP)
+    padded = jnp.concatenate([conv[...], jnp.zeros((8 - CONV, width), f32)], 0)
+    for j in range(width // LANES):
+        taps_v[j * LANES : (j + 1) * LANES, :] = padded[:, j * LANES : (j + 1) * LANES].T
+    half = width // 2
+    slab = half // GROUP
+    taps[0:slab, :] = taps_v[pl.ds(pl.multiple_of(slab * mine, 32), slab), :]
+    taps[slab : 2 * slab, :] = taps_v[pl.ds(pl.multiple_of(half + slab * mine, 32), slab), :]
+    inputs = x[...]
+    for j, copy in enumerate(copies):
+        copy.wait()
+        if j < 2:
+            got = dot(inputs, wqk_v[1 - j])
+            qkt[1 - j] = got.T.astype(bf16)
+        else:
+            at = (j - 2) * tile
+            got = dot(inputs, wv_v[:, at : at + tile])
+            vt[at : at + tile, :] = got.T.astype(bf16)
+    alive = (place * rows + iota((1, rows), 1) < length[0]).astype(f32)
+    keys = (qkt[1].astype(f32) * alive).astype(bf16)
+    gram = dot(keys, keys, NT)
+    same = iota((keyed, keyed), 0) // FEAT == iota((keyed, keyed), 1) // FEAT
+    pick = (lax.rem(iota((FEAT, keyed), 1), FEAT) == iota((FEAT, keyed), 0)).astype(bf16)
+    folded = dot(pick, jnp.where(same, gram, 0.0).astype(bf16))
+    plain = dot(jnp.ones((8, rows), bf16), keys, NT)
+    third = jnp.concatenate(
+        [plain[0:1, :LANES], plain[0:1, LANES:], jnp.zeros((FEAT - 2, LANES), f32)], 0
+    )
+    sums = jnp.concatenate([folded[:, :LANES], folded[:, LANES:], third], 0).astype(bf16)
+    part = keyed // 2 // GROUP
+    for s, out in enumerate((o0, o1, o2, o3)):
+        dest = mine ^ s
+        out[0:slab, :] = vt[pl.ds(pl.multiple_of(slab * dest, 32), slab), :]
+        out[slab : 2 * slab, :] = vt[pl.ds(pl.multiple_of(half + slab * dest, 32), slab), :]
+        at = 2 * slab
+        for which in (1, 0):
+            for base in (0, keyed // 2):
+                start = pl.multiple_of(base + part * dest, 32)
+                out[at : at + part, :] = qkt[which, pl.ds(start, part), :]
+                at += part
+        out[at : at + SUMS, :] = sums
+
+
+def project(length, x, wq, wk, wv, conv):
+    rows, width = x.shape
+    keyed = wq.shape[1]
+    total = (width + 2 * keyed) // GROUP + SUMS
+    payload = jax.ShapeDtypeStruct((total, rows), bf16)
+    taps = jax.ShapeDtypeStruct((width // GROUP, 8), f32)
+    vmem = pl.BlockSpec(memory_space=pltpu.VMEM)
+    hbm = pl.BlockSpec(memory_space=pl.ANY)
+    return pl.pallas_call(
+        project_kernel,
+        out_shape=[payload] * 4 + [taps],
+        in_specs=[pl.BlockSpec(memory_space=pltpu.SMEM), vmem, hbm, hbm, hbm, vmem],
+        out_specs=[vmem] * 5,
+        scratch_shapes=[
+            pltpu.VMEM((width, width), bf16),
+            pltpu.VMEM((2, width, keyed), bf16),
+            pltpu.VMEM((width, rows), bf16),
+            pltpu.VMEM((2, keyed, rows), bf16),
+            pltpu.VMEM((width, 8), f32),
+            pltpu.SemaphoreType.DMA((2 + width // 256,)),
+        ],
+        compiler_params=pltpu.CompilerParams(vmem_limit_bytes=40 * 2**20),
+        cost_estimate=pl.CostEstimate(
+            flops=2 * rows * width * (width + 2 * keyed),
+            bytes_accessed=2 * width * (width + 2 * keyed),
+            transcendentals=0,
+        ),
+    )(length, x, wq, wk, wv, conv)
+
+
+def state_kernel(length, p0, p1, p2, p3, taps, aug, qk, state, held):
+    rows = p0.shape[1]
+    place = lax.axis_index("blk")
+    mine, group = lax.rem(place, GROUP), place // GROUP
+    values = p0.shape[0] - SUMS - 2 * HEADS // GROUP * FEAT
+    local = HEADS // GROUP
+    size = values // local
+    tokens = GROUP * rows
+    for s, ref in enumerate((p0, p1, p2, p3)):
+        held[mine ^ s] = ref[0 : held.shape[1], :]
+    sums = p0[held.shape[1] :, :].astype(f32) + p1[held.shape[1] :, :].astype(f32)
+    sums += p2[held.shape[1] :, :].astype(f32) + p3[held.shape[1] :, :].astype(f32)
+    state[local * SYM :, :] = sums.astype(bf16)
+    for b in range(GROUP):
+        qk[:, b * rows : (b + 1) * rows] = held[b, values:, :]
+    alive = (group * tokens + iota((1, tokens), 1) < length[0]).astype(f32)
+    token = iota((FEAT, tokens), 1)
+    row = iota((FEAT, tokens), 0)
+    marks = (row == 0) | ((row == 1) & (token == 0)) | ((row == 2) & (token == 1))
+    marks = jnp.where(marks, alive, 0.0).astype(bf16)
+    lane = iota((size, rows), 1)
+    last = iota((FEAT, rows), 0)
+    ends = iota((FEAT, rows), 1)
+    ends = ((last == 9) & (ends == rows - 1)) | ((last == 10) & (ends == rows - 2))
+    ends = ends.astype(bf16)
+    for h in range(local):
+        cut = slice(h * size, (h + 1) * size)
+        tap = [jnp.broadcast_to(taps[cut, t : t + 1], (size, rows)) for t in range(CONV)]
+        before = [jnp.zeros((size, rows), f32)] * 2
+        pieces = []
+        for b in range(GROUP):
+            now = held[b, cut, :].astype(f32)
+            rolled = [pltpu.roll(now, 1, 1), pltpu.roll(now, 2, 1)]
+            one = jnp.where(lane < 1, before[0], rolled[0])
+            two = jnp.where(lane < 2, before[1], rolled[1])
+            before = rolled
+            mixed = tap[0] * now + tap[1] * one + tap[2] * two
+            live = alive[:, b * rows : (b + 1) * rows]
+            pieces.append(jnp.where(live > 0, mixed, 0.0).astype(bf16))
+        aug_h = jnp.concatenate([jnp.concatenate(pieces, 1), marks], 0)
+        aug[h] = aug_h
+        y = qk[h * FEAT : (h + 1) * FEAT, :].astype(f32) * FEAT ** (-0.25)
+        own = dot(symmetric(y, 1.0).astype(bf16), aug_h, NT)
+        edge = dot(ends, held[GROUP - 1, h * size : h * size + LANES, :], NT)
+        state[h * SYM : h * SYM + 144, :] = own[:144].astype(bf16)
+        state[h * SYM + 144 : (h + 1) * SYM, :] = (own[144:] + edge).astype(bf16)
+
+
+def group_state(length, payloads, taps):
+    total, rows = payloads[0].shape
+    local = HEADS // GROUP
+    vmem = pl.BlockSpec(memory_space=pltpu.VMEM)
+    tokens = GROUP * rows
+    return pl.pallas_call(
+        state_kernel,
+        out_shape=[
+            jax.ShapeDtypeStruct((local, LANES, tokens), bf16),
+            jax.ShapeDtypeStruct((2 * local * FEAT, tokens), bf16),
+            jax.ShapeDtypeStruct((local * SYM + SUMS, LANES), bf16),
+        ],
+        in_specs=[pl.BlockSpec(memory_space=pltpu.SMEM)] + [vmem] * 5,
+        out_specs=[vmem] * 3,
+        scratch_shapes=[pltpu.VMEM((GROUP, total - SUMS, rows), bf16)],
+        compiler_params=pltpu.CompilerParams(vmem_limit_bytes=32 * 2**20),
+        cost_estimate=pl.CostEstimate(flops=200_000_000, bytes_accessed=2_000_000, transcendentals=0),
+    )(length, *payloads, taps)
+
+
+def local_kernel(aug, qk, num):
+    local, _, tokens = aug.shape
+    keyed = local * FEAT
+    half = tokens // 2
+    keys = qk[0:keyed, :].astype(f32).T.astype(bf16)
+    queries = qk[keyed:, :]
+    head = iota((keyed, tokens), 0) // FEAT
+    causal = iota((half, half), 0) <= iota((half, half), 1)
+
+    def scores(d):
+        return 1.0 + d * (0.25 + d * 0.03125)
+
+    for h in range(local):
+        only = jnp.where(head == h, queries, jnp.zeros_like(queries))
+        first = scores(dot(keys[:half], only[:, :half]))
+        first = jnp.where(causal, first, 0.0).astype(bf16)
+        num[h, :, 0:half] = dot(aug[h, :, 0:half], first)
+        lower = scores(dot(keys[half:], only[:, half:]))
+        lower = jnp.where(causal, lower, 0.0).astype(bf16)
+        upper = scores(dot(keys[:half], only[:, half:])).astype(bf16)
+        num[h, :, half:] = dot(aug[h, :, 0:half], upper) + dot(aug[h, :, half:], lower)
+
+
+def local_part(aug, qk):
+    local, _, tokens = aug.shape
+    vmem = pl.BlockSpec(memory_space=pltpu.VMEM)
+    return pl.pallas_call(
+        local_kernel,
+        out_shape=jax.ShapeDtypeStruct(aug.shape, f32),
+        in_specs=[vmem] * 2,
+        out_specs=vmem,
+        compiler_params=pltpu.CompilerParams(vmem_limit_bytes=32 * 2**20),
+        cost_estimate=pl.CostEstimate(
+            flops=4 * local * tokens * tokens * LANES, bytes_accessed=2_000_000, transcendentals=0
+        ),
+    )(aug, qk)
+
+
+def finish_kernel(length, slot, num, own, got, qk, taps, r0, r1, r2, r3, route, scr, tot):
+    local, _, tokens = num.shape
+    rows = tokens // GROUP
+    size = taps.shape[0] // local
+    keyed = local * FEAT
+    place = lax.axis_index("blk")
+    mine, group = lax.rem(place, GROUP), place // GROUP
+    upper = group == 1
+    weight = jnp.where(upper, 1.0, 0.0)
+    alive = group * tokens + iota((1, tokens), 1) < length[0]
+    first = (iota((size, LANES), 1) == 0) & upper
+    aux = iota((LANES - size, SYM), 0)
+    for h in range(local):
+        here = own[h * SYM : (h + 1) * SYM, :].astype(f32).T
+        there = got[h * SYM : (h + 1) * SYM, :].astype(f32).T
+        low = jnp.where(upper, there, here)
+        high = jnp.where(upper, here, there)
+        tap = taps[h * size : (h + 1) * size, :]
+        last, second = low[:size, 153:154], low[:size, 154:155]
+        change0 = tap[:, 1:2] * last + tap[:, 2:3] * second
+        change1 = tap[:, 2:3] * last
+        key0, key1 = high[size + 1 : size + 2, :], high[size + 2 : size + 3, :]
+        body = low[:size] + change0 * key0 + change1 * key1
+        tail = jnp.where(aux == 2, key1, low[size:])
+        prior = jnp.concatenate([body, tail], 0)
+        tot[h] = jnp.concatenate([body + high[:size], low[size:] + high[size:]], 0)
+        y = qk[keyed + h * FEAT : keyed + (h + 1) * FEAT, :].astype(f32) * FEAT ** (-0.25)
+        feats = symmetric(y, 0.5).astype(bf16)
+        all_num = num[h] + weight * dot(prior.astype(bf16), feats)
+        den = jnp.where(alive, all_num[size : size + 1, :], 1.0)
+        inverse = jnp.where(alive, 1.0 / den, 0.0)
+        top = all_num[:size]
+        extra = all_num[size + 2 : size + 3, 0:1]
+        edge = top[:, :LANES] - jnp.where(first, change1 * extra, 0.0)
+        top = jnp.concatenate([edge, top[:, LANES:]], 1)
+        result = (top * inverse).astype(bf16)
+        for b in range(GROUP):
+            scr[b, h * size : (h + 1) * size, :] = result[:, b * rows : (b + 1) * rows]
+    for s, out in enumerate((r0, r1, r2, r3)):
+        out[...] = scr[mine ^ s]
+    chosen = local // 2
+    for c in range(chosen):
+        final = jnp.where(upper, tot[chosen + c], tot[c])
+        route[c * SYM : (c + 1) * SYM, :] = final.T.astype(bf16)
+    sums = own[local * SYM :, :].astype(f32) + got[local * SYM :, :].astype(f32)
+    r, c = iota(sums.shape, 0), iota(sums.shape, 1)
+    count = length[0]
+    sums = jnp.where((r == INFO) & (c == 0), slot[0].astype(f32), sums)
+    sums = jnp.where((r == INFO) & (c == 1), (count // 256).astype(f32), sums)
+    sums = jnp.where((r == INFO) & (c == 2), lax.rem(count, 256).astype(f32), sums)
+    route[chosen * SYM :, :] = sums.astype(bf16)
+
+
+def finish(length, slot, num, own, got, qk, taps):
+    local, _, tokens = num.shape
+    rows = tokens // GROUP
+    width = taps.shape[0]
+    vmem = pl.BlockSpec(memory_space=pltpu.VMEM)
+    smem = pl.BlockSpec(memory_space=pltpu.SMEM)
+    result = jax.ShapeDtypeStruct((width, rows), bf16)
+    return pl.pallas_call(
+        finish_kernel,
+        out_shape=[result] * 4 + [jax.ShapeDtypeStruct((local // 2 * SYM + SUMS, LANES), bf16)],
+        in_specs=[smem, smem] + [vmem] * 5,
+        out_specs=[vmem] * 5,
+        scratch_shapes=[
+            pltpu.VMEM((GROUP, width, rows), bf16),
+            pltpu.VMEM((local, LANES, SYM), f32),
+        ],
+        compiler_params=pltpu.CompilerParams(vmem_limit_bytes=32 * 2**20),
+        cost_estimate=pl.CostEstimate(flops=100_000_000, bytes_accessed=2_000_000, transcendentals=0),
+    )(length, slot, num, own, got, qk, taps)
+
+
+def place_kernel(r0, r1, r2, r3, mixed, scr):
+    width = scr.shape[0]
+    mine = lax.rem(lax.axis_index("blk"), GROUP)
+    half = width // 2
+    slab = half // GROUP
+    for s, ref in enumerate((r0, r1, r2, r3)):
+        dest = mine ^ s
+        scr[pl.ds(pl.multiple_of(slab * dest, 32), slab), :] = ref[0:slab, :]
+        scr[pl.ds(pl.multiple_of(half + slab * dest, 32), slab), :] = ref[slab:, :]
+    for j in range(width // LANES):
+        cut = slice(j * LANES, (j + 1) * LANES)
+        mixed[0, :, cut] = scr[cut, :].astype(f32).T.astype(bf16)
+
+
+def place_tokens(results):
+    part, rows = results[0].shape
+    width = part * GROUP
+    vmem = pl.BlockSpec(memory_space=pltpu.VMEM)
+    return pl.pallas_call(
+        place_kernel,
+        out_shape=jax.ShapeDtypeStruct((1, rows, width), bf16),
+        in_specs=[vmem] * 4,
+        out_specs=vmem,
+        scratch_shapes=[pltpu.VMEM((width, rows), bf16)],
+        compiler_params=pltpu.CompilerParams(vmem_limit_bytes=32 * 2**20),
+        cost_estimate=pl.CostEstimate(flops=1000, bytes_accessed=1_000_000, transcendentals=0),
+    )(*results)
+
+
+def expand_kernel(near, far, spread, state, norm):
+    me = lax.axis_index("req").astype(f32)
+    heads = (near.shape[1] - SUMS) // SYM
+    info = heads * SYM + INFO
+    kept = jnp.zeros(near.shape[1:], f32)
+    for ref in (near, far):
+        for c in range(2):
+            kept += jnp.where(ref[c, info : info + 1, 0:1].astype(f32) == me, ref[c].astype(f32), 0.0)
+    size = state.shape[2] // heads
+    expand = state.shape[1]
+    scale = jnp.where(iota((expand, LANES), 0) > FEAT, math.sqrt(0.5), 1.0)
+    for c in range(heads):
+        whole = dot(spread[...], kept[c * SYM : (c + 1) * SYM].astype(bf16)) * scale
+        state[0, :, c * size : (c + 1) * size] = whole[:, :size]
+    sums = kept[heads * SYM :]
+    keyed = HEADS * FEAT
+    products = jnp.concatenate([sums[:FEAT], sums[FEAT : 2 * FEAT]], 1)
+    plain = jnp.concatenate([sums[2 * FEAT : 2 * FEAT + 1], sums[2 * FEAT + 1 : 2 * FEAT + 2]], 1)
+    big = jnp.concatenate(
+        [jnp.broadcast_to(plain * FEAT ** (-0.25), (FEAT, keyed))]
+        + [products * FEAT ** (-0.5)] * FEAT,
+        0,
+    )
+    r, j = iota(big.shape, 0), iota(big.shape, 1)
+    entry = jnp.where(r < FEAT, r, r // FEAT - 1)
+    big = jnp.where(lax.rem(j, FEAT) == entry, big, 0.0)
+    gather = (iota((keyed, HEADS), 0) // FEAT == iota((keyed, HEADS), 1)).astype(bf16)
+    rest = dot(big.astype(bf16), gather)
+    rest = rest * jnp.where(iota(rest.shape, 0) >= FEAT, math.sqrt(0.5), 1.0)
+    count = sums[INFO : INFO + 1, 1:2] * 256.0 + sums[INFO : INFO + 1, 2:3]
+    norm[0, 0:1, :] = jnp.broadcast_to(count, (1, HEADS))
+    norm[0, 1:expand, :] = rest
+
+
+def spread_rows():
+    table = np.zeros((1 + FEAT + FEAT * FEAT, SYM), np.float32)
+    table[0, 152] = 1
+    for a in range(FEAT):
+        table[1 + a, 128 + a] = 1
+        for b in range(FEAT):
+            o = (b - a) % FEAT
+            at = o * FEAT + a if o < 8 else (144 + min(a, b) if o == 8 else (FEAT - o) * FEAT + b)
+            table[1 + FEAT + a * FEAT + b, at] = 1
+    return table
+
+
+def expand_state(near, far, columns):
+    vmem = pl.BlockSpec(memory_space=pltpu.VMEM)
+    spread = jnp.asarray(spread_rows(), bf16)
+    expand = spread.shape[0]
+    return pl.pallas_call(
+        expand_kernel,
+        out_shape=[
+            jax.ShapeDtypeStruct((1, expand, columns), f32),
+            jax.ShapeDtypeStruct((1, expand, HEADS), f32),
+        ],
+        in_specs=[vmem] * 3,
+        out_specs=[vmem] * 2,
+        compiler_params=pltpu.CompilerParams(vmem_limit_bytes=32 * 2**20),
+        cost_estimate=pl.CostEstimate(flops=40_000_000, bytes_accessed=1_000_000, transcendentals=0),
+    )(near, far, spread)
+
+
+def swap(array, axis, by):
+    return lax.ppermute(array, axis, [(i, i ^ by) for i in range(lax.axis_size(axis))])
+
+
+def two_groups(
+    tokens_in, query_weight, key_weight, value_weight, conv_weight, prompt_lengths, decode_map
+):
+    width = tokens_in.shape[2]
+    *payloads, taps = project(
+        prompt_lengths, tokens_in[0], query_weight, key_weight, value_weight, conv_weight
+    )
+    payloads = [payloads[0]] + [swap(payloads[s], "blk", s) for s in (1, 2, 3)]
+    aug, qk, own = group_state(prompt_lengths, payloads, taps)
+    got = swap(own, "blk", GROUP)
+    num = local_part(aug, qk)
+    *results, route = finish(prompt_lengths, decode_map, num, own, got, qk, taps)
+    results = [results[0]] + [swap(results[s], "blk", s) for s in (1, 2, 3)]
+    near = jnp.stack([route, swap(route, "req", 2)])
+    far = swap(near, "req", 1)
+    mixed = place_tokens(results)
+    state, norm = expand_state(near, far, width // lax.axis_size("blk"))
+    return (mixed, state, norm)
 
 
 def from_behind(array, axis, by):
@@ -59,7 +474,7 @@
     )
 
 
-def on_device(
+def any_blocks(
     tokens_in, query_weight, key_weight, value_weight, conv_weight, prompt_lengths, decode_map
 ):
     rows = tokens_in.shape[1]
@@ -111,6 +526,12 @@
 
 
 def solution(mesh):
+    def on_device(*args):
+        rows = args[0].shape[1]
+        if mesh.shape["blk"] == 2 * GROUP and mesh.shape["req"] == 4 and rows == LANES:
+            return two_groups(*args)
+        return any_blocks(*args)
+
     return jax.shard_map(
         on_device,
         mesh=mesh,

time: 542 us -> 55.7 us (0.10)
  the two profiles are of different devices: /device:TPU:31 before, /device:TPU:0 now
where the time goes in v1:
time: 55.7 us; the launch traced here: 55.3 us
  waiting for transfers between devices  21.3 us (38%)
  starting transfers between devices  12.6 us (23%)
  Pallas kernels  10.8 us (19%)
  local copies, waits for them, and re-layouts  8.65 us (16%)
  between operations  1.99 us (4%)
    ppermute x9, waiting for transfers between devices, swap(): lax.ppermute(array, axis, [(i, i ^ by) for i in range(lax.axis_size(axis))])  21.3 us
    ppermute x9, starting transfers between devices, swap(): lax.ppermute(array, axis, [(i, i ^ by) for i in range(lax.axis_size(axis))])  12.6 us
    unnamed x14, local copies, waits for them, and re-layouts  8.65 us
    pallas_call x1, Pallas kernels, project(): pl.pallas_call(project_kernel, out_shape=[payload] * 4 + [taps], in_specs...  5.37 us
    pallas_call x1, Pallas kernels, finish(): pl.pallas_call(finish_kernel, out_shape=[result] * 4 + [jax.ShapeDtypeStr...  1.57 us
    pallas_call x1, Pallas kernels, local_part(): pl.pallas_call(local_kernel, out_shape=jax.ShapeDtypeStruct(aug.shape, f3...  1.51 us
  transfers between devices with their start and end apart: 9, of which 8 were waited for; matrix products, arithmetic and copies ran while one was open for 0% of the time, Pallas kernels for 5%

profile of v1, /device:TPU:0, one launch (start us, length us, event | category | flops | bytes accessed | tf_op | source)
XLA Modules:
  0.0 55.3 jit_solution(8579468437794203649)
XLA Ops:
  1.3 2.8 %copy-done = bf16[1792,1792]{1,0:T(8,128)(2,1)S(1)} copy-done((bf16[1792,1792]{1,0:T(8,128)(2,1)S(1)}, bf16[1792,1792]{1,0:T(8,128)(2,1)}, u32[]{:S(2)}) %copy-start) | copy-done | bytes 6422552
  4.1 1.2 %copy-done.1 = bf16[1792,256]{1,0:T(8,128)(2,1)S(1)} copy-done((bf16[1792,256]{1,0:T(8,128)(2,1)S(1)}, bf16[1792,256]{1,0:T(8,128)(2,1)}, u32[]{:S(2)}) %copy-start.1) | copy-done | bytes 917528
  5.3 1.2 %copy-done.2 = bf16[1792,256]{1,0:T(8,128)(2,1)S(1)} copy-done((bf16[1792,256]{1,0:T(8,128)(2,1)S(1)}, bf16[1792,256]{1,0:T(8,128)(2,1)}, u32[]{:S(2)}) %copy-start.2) | copy-done | bytes 917528
  6.5 1.0 %copy-done.3 = bf16[1,128,1792]{2,1,0:T(8,128)(2,1)S(1)} copy-done((bf16[1,128,1792]{2,1,0:T(8,128)(2,1)S(1)}, bf16[1,128,1792]{2,1,0:T(8,128)(2,1)}, u32[]{:S(2)}) %copy-start.3) | copy-done | bytes 458776
  8.2 5.4 %shard_map.103 = (bf16[624,128]{1,0:T(8,128)(2,1)S(1)}, bf16[624,128]{1,0:T(8,128)(2,1)S(1)}, bf16[624,128]{1,0:T(8,128)(2,1)S(1)}, bf16[624,128]{1,0:T(8,128)(2,1)S(1)}, f32[448,8]{1,0:T(8,128)S(1)}) custom-call(s32[1]{0:T(128)S(6)} %copy.13.length, bf16[128,1792]{1,0:T(8,128)(2,1)S(1)} %bitcast.3, bf16[1792,256]{1,0:T(8,128)(2,1)S(1)} %copy-done.1, ...), custom_call_target="tpu_custom_call" | custom-call | flops 1056964608 | bytes 8257536 | tf_op jit(solution)/shard_map/pallas_call | solution.py:110
  13.6 3.0 %collective-permute-start = (bf16[624,128]{1,0:T(8,128)(2,1)S(1)}, bf16[624,128]{1,0:T(8,128)(2,1)S(1)}, u32[]{:S(2)}, u32[]{:S(2)}) collective-permute-start(bf16[624,128]{1,0:T(8,128)(2,1)S(1)} %get-tuple-element.19), channel_id=1, source_target_pairs={{0,4},{4,0},{8,12},{12,8},{16,20},{20,16},{24,28},{28,24},{1,5},{5... | collective-permute-start | bytes 479240 | tf_op jit(solution)/shard_map/ppermute | solution.py:405
  16.6 1.6 %collective-permute-start.1 = (bf16[624,128]{1,0:T(8,128)(2,1)S(1)}, bf16[624,128]{1,0:T(8,128)(2,1)S(1)}, u32[]{:S(2)}, u32[]{:S(2)}) collective-permute-start(bf16[624,128]{1,0:T(8,128)(2,1)S(1)} %get-tuple-element.20), channel_id=1, source_target_pairs={{0,8},{4,12},{8,0},{12,4},{16,24},{20,28},{24,16},{28,20},{1,9},{5... | collective-permute-start | bytes 479240 | tf_op jit(solution)/shard_map/ppermute | solution.py:405
  18.3 2.5 %collective-permute-done.p1 = bf16[624,128]{1,0:T(8,128)(2,1)S(1)} collective-permute-done((bf16[624,128]{1,0:T(8,128)(2,1)S(1)}, bf16[624,128]{1,0:T(8,128)(2,1)S(1)}, u32[]{:S(2)}, u32[]{:S(2)}) %collective-permute-start) | collective-permute-done | bytes 159776 | tf_op jit(solution)/shard_map/ppermute | solution.py:405
  20.8 2.9 %collective-permute-done.1.p2 = bf16[624,128]{1,0:T(8,128)(2,1)S(1)} collective-permute-done((bf16[624,128]{1,0:T(8,128)(2,1)S(1)}, bf16[624,128]{1,0:T(8,128)(2,1)S(1)}, u32[]{:S(2)}, u32[]{:S(2)}) %collective-permute-start.1) | collective-permute-done | bytes 159776 | tf_op jit(solution)/shard_map/ppermute | solution.py:405
  23.7 1.8 %collective-permute-done.2.p3 = bf16[624,128]{1,0:T(8,128)(2,1)S(1)} collective-permute-done((bf16[624,128]{1,0:T(8,128)(2,1)S(1)}, bf16[624,128]{1,0:T(8,128)(2,1)S(1)}, u32[]{:S(2)}, u32[]{:S(2)}) %collective-permute-start.2) | collective-permute-done | bytes 159776 | tf_op jit(solution)/shard_map/ppermute | solution.py:405
  25.4 0.9 %shard_map.104 = (bf16[4,128,512]{2,1,0:T(8,128)(2,1)S(1)}, bf16[128,512]{1,0:T(8,128)(2,1)S(1)}, bf16[688,128]{1,0:T(8,128)(2,1)S(1)}) custom-call(s32[1]{0:T(128)S(6)} %copy.13.length, bf16[624,128]{1,0:T(8,128)(2,1)S(1)} %get-tuple-element.18.p0, bf16[624,128]{1,0:T(8,128)(2,1)S(1)} %collective-permute-done.p1, ...), custom_call_target="tpu_custom_call" | custom-call | flops 200000000 | bytes 2000000 | tf_op jit(solution)/shard_map/pallas_call | solution.py:185
  26.4 2.8 %collective-permute-start.3 = (bf16[688,128]{1,0:T(8,128)(2,1)S(1)}, bf16[688,128]{1,0:T(8,128)(2,1)S(1)}, u32[]{:S(2)}, u32[]{:S(2)}) collective-permute-start(bf16[688,128]{1,0:T(8,128)(2,1)S(1)} %get-tuple-element.25.own), channel_id=1, source_target_pairs={{0,16},{4,20},{8,24},{12,28},{16,0},{20,4},{24,8},{28,12},{1,17},{... | collective-permute-start | bytes 528392 | tf_op jit(solution)/shard_map/ppermute | solution.py:405
  29.8 1.5 %shard_map.105.num = f32[4,128,512]{2,1,0:T(8,128)S(1)} custom-call(bf16[4,128,512]{2,1,0:T(8,128)(2,1)S(1)} %get-tuple-element.23.aug, bf16[128,512]{1,0:T(8,128)(2,1)S(1)} %get-tuple-element.24.qk), custom_call_target="tpu_custom_call" | custom-call | flops 536870912 | bytes 2000000 | tf_op jit(solution)/shard_map/pallas_call | solution.py:226
  31.3 5.3 %collective-permute-done.3.got = bf16[688,128]{1,0:T(8,128)(2,1)S(1)} collective-permute-done((bf16[688,128]{1,0:T(8,128)(2,1)S(1)}, bf16[688,128]{1,0:T(8,128)(2,1)S(1)}, u32[]{:S(2)}, u32[]{:S(2)}) %collective-permute-start.3) | collective-permute-done | bytes 176160 | tf_op jit(solution)/shard_map/ppermute | solution.py:405
  36.6 1.6 %shard_map.106 = (bf16[448,128]{1,0:T(8,128)(2,1)S(1)}, bf16[448,128]{1,0:T(8,128)(2,1)S(1)}, bf16[448,128]{1,0:T(8,128)(2,1)S(1)}, bf16[448,128]{1,0:T(8,128)(2,1)S(1)}, bf16[368,128]{1,0:T(8,128)(2,1)S(1)}) custom-call(s32[1]{0:T(128)S(6)} %copy.13.length, s32[1]{0:T(128)S(6)} %copy.14.slot, f32[4,128,512]{2,1,0:T(8,128)S(1)} %shard_map.105.num, ...), custom_call_target="tpu_custom_call" | custom-call | flops 100000000 | bytes 2000000 | tf_op jit(solution)/shard_map/pallas_call | solution.py:298
  38.2 1.5 %collective-permute-start.7 = (bf16[368,128]{1,0:T(8,128)(2,1)S(1)}, bf16[368,128]{1,0:T(8,128)(2,1)S(1)}, u32[]{:S(2)}, u32[]{:S(2)}) collective-permute-start(bf16[368,128]{1,0:T(8,128)(2,1)S(1)} %get-tuple-element.30), channel_id=1, source_target_pairs={{0,2},{1,3},{2,0},{3,1},{4,6},{5,7},{6,4},{7,5},{8,10},{9,11},{10,... | collective-permute-start | bytes 282632 | tf_op jit(solution)/shard_map/ppermute | solution.py:405
  39.7 3.1 %collective-permute-done.7 = bf16[368,128]{1,0:T(8,128)(2,1)S(1)} collective-permute-done((bf16[368,128]{1,0:T(8,128)(2,1)S(1)}, bf16[368,128]{1,0:T(8,128)(2,1)S(1)}, u32[]{:S(2)}, u32[]{:S(2)}) %collective-permute-start.7) | collective-permute-done | bytes 94240 | tf_op jit(solution)/shard_map/ppermute | solution.py:405
  43.0 1.2 %collective-permute-start.4 = (bf16[448,128]{1,0:T(8,128)(2,1)S(1)}, bf16[448,128]{1,0:T(8,128)(2,1)S(1)}, u32[]{:S(2)}, u32[]{:S(2)}) collective-permute-start(bf16[448,128]{1,0:T(8,128)(2,1)S(1)} %get-tuple-element.27), channel_id=1, source_target_pairs={{0,4},{4,0},{8,12},{12,8},{16,20},{20,16},{24,28},{28,24},{1,5},{5... | collective-permute-start | bytes 344072 | tf_op jit(solution)/shard_map/ppermute | solution.py:405
  44.8 1.7 %collective-permute-start.6 = (bf16[448,128]{1,0:T(8,128)(2,1)S(1)}, bf16[448,128]{1,0:T(8,128)(2,1)S(1)}, u32[]{:S(2)}, u32[]{:S(2)}) collective-permute-start(bf16[448,128]{1,0:T(8,128)(2,1)S(1)} %get-tuple-element.29), channel_id=1, source_target_pairs={{0,12},{4,8},{8,4},{12,0},{16,28},{20,24},{24,20},{28,16},{1,13},{... | collective-permute-start | bytes 344072 | tf_op jit(solution)/shard_map/ppermute | solution.py:405
  46.5 2.0 %collective-permute-done.4.r1 = bf16[448,128]{1,0:T(8,128)(2,1)S(1)} collective-permute-done((bf16[448,128]{1,0:T(8,128)(2,1)S(1)}, bf16[448,128]{1,0:T(8,128)(2,1)S(1)}, u32[]{:S(2)}, u32[]{:S(2)}) %collective-permute-start.4) | collective-permute-done | bytes 114720 | tf_op jit(solution)/shard_map/ppermute | solution.py:405
  48.5 1.6 %collective-permute-done.5.r2 = bf16[448,128]{1,0:T(8,128)(2,1)S(1)} collective-permute-done((bf16[448,128]{1,0:T(8,128)(2,1)S(1)}, bf16[448,128]{1,0:T(8,128)(2,1)S(1)}, u32[]{:S(2)}, u32[]{:S(2)}) %collective-permute-start.5) | collective-permute-done | bytes 114720 | tf_op jit(solution)/shard_map/ppermute | solution.py:405
  50.1 2.0 %collective-permute-done.6.r3 = bf16[448,128]{1,0:T(8,128)(2,1)S(1)} collective-permute-done((bf16[448,128]{1,0:T(8,128)(2,1)S(1)}, bf16[448,128]{1,0:T(8,128)(2,1)S(1)}, u32[]{:S(2)}, u32[]{:S(2)}) %collective-permute-start.6) | collective-permute-done | bytes 114720 | tf_op jit(solution)/shard_map/ppermute | solution.py:405
  52.2 1.0 %shard_map.107 = bf16[1,128,1792]{2,1,0:T(8,128)(2,1)} custom-call(bf16[448,128]{1,0:T(8,128)(2,1)S(1)} %get-tuple-element.26.r0, bf16[448,128]{1,0:T(8,128)(2,1)S(1)} %collective-permute-done.4.r1, bf16[448,128]{1,0:T(8,128)(2,1)S(1)} %collective-permute-done.5.r2, bf16[448,128]{1,0:T(8,128)(2,1)S(1)} %collective-permute-done.6.r3), custom_call_target="tpu_custom_call" | custom-call | flops 1000 | bytes 1000000 | tf_op jit(solution)/shard_map/pallas_call | solution.py:330
  53.6 1.0 %copy.11 = f32[1,273,224]{2,0,1:T(1,128)} copy(f32[1,273,224]{2,1,0:T(8,128)S(1)} %get-tuple-element.34) | data formatting | bytes 489216
  (15 shorter events, 2.6 us)
Async XLA Ops:
  1.3 2.8 %copy-start = (bf16[1792,1792]{1,0:T(8,128)(2,1)S(1)}, bf16[1792,1792]{1,0:T(8,128)(2,1)}, u32[]{:S(2)}) copy-start(bf16[1792,1792]{1,0:T(8,128)(2,1)} %wv.1) | copy-start | bytes 19267588
  4.1 1.2 %copy-start.1 = (bf16[1792,256]{1,0:T(8,128)(2,1)S(1)}, bf16[1792,256]{1,0:T(8,128)(2,1)}, u32[]{:S(2)}) copy-start(bf16[1792,256]{1,0:T(8,128)(2,1)} %wq.1) | copy-start | bytes 2752516
  5.3 1.2 %copy-start.2 = (bf16[1792,256]{1,0:T(8,128)(2,1)S(1)}, bf16[1792,256]{1,0:T(8,128)(2,1)}, u32[]{:S(2)}) copy-start(bf16[1792,256]{1,0:T(8,128)(2,1)} %wk.1) | copy-start | bytes 2752516
  6.5 1.0 %copy-start.3 = (bf16[1,128,1792]{2,1,0:T(8,128)(2,1)S(1)}, bf16[1,128,1792]{2,1,0:T(8,128)(2,1)}, u32[]{:S(2)}) copy-start(bf16[1,128,1792]{2,1,0:T(8,128)(2,1)} %param.8) | copy-start | bytes 1376260
  7.5 0.7 %copy-start.5 = (f32[3,1792]{1,0:T(4,128)S(1)}, f32[3,1792]{1,0:T(4,128)}, u32[]{:S(2)}) copy-start(f32[3,1792]{1,0:T(4,128)} %conv.1) | copy-start | bytes 64516
  8.2 44.9 %copy-start.4 = (bf16[273,160]{1,0:T(8,128)(2,1)S(1)}, bf16[273,160]{1,0:T(8,128)(2,1)}, u32[]{:S(2)}) copy-start(bf16[273,160]{1,0:T(8,128)(2,1)} %constant.2.clone.spread) | copy-start | bytes 262084
  13.6 7.1 %collective-permute-start = (bf16[624,128]{1,0:T(8,128)(2,1)S(1)}, bf16[624,128]{1,0:T(8,128)(2,1)S(1)}, u32[]{:S(2)}, u32[]{:S(2)}) collective-permute-start(bf16[624,128]{1,0:T(8,128)(2,1)S(1)} %get-tuple-element.19), channel_id=1, source_target_pairs={{0,4},{4,0},{8,12},{12,8},{16,20},{20,16},{24,28},{28,24},{1,5},{5... | collective-permute-start | bytes 479240 | tf_op jit(solution)/shard_map/ppermute | solution.py:405
  16.6 7.0 %collective-permute-start.1 = (bf16[624,128]{1,0:T(8,128)(2,1)S(1)}, bf16[624,128]{1,0:T(8,128)(2,1)S(1)}, u32[]{:S(2)}, u32[]{:S(2)}) collective-permute-start(bf16[624,128]{1,0:T(8,128)(2,1)S(1)} %get-tuple-element.20), channel_id=1, source_target_pairs={{0,8},{4,12},{8,0},{12,4},{16,24},{20,28},{24,16},{28,20},{1,9},{5... | collective-permute-start | bytes 479240 | tf_op jit(solution)/shard_map/ppermute | solution.py:405
  18.3 7.2 %collective-permute-start.2 = (bf16[624,128]{1,0:T(8,128)(2,1)S(1)}, bf16[624,128]{1,0:T(8,128)(2,1)S(1)}, u32[]{:S(2)}, u32[]{:S(2)}) collective-permute-start(bf16[624,128]{1,0:T(8,128)(2,1)S(1)} %get-tuple-element.21), channel_id=1, source_target_pairs={{0,12},{4,8},{8,4},{12,0},{16,28},{20,24},{24,20},{28,16},{1,13},{... | collective-permute-start | bytes 479240 | tf_op jit(solution)/shard_map/ppermute | solution.py:405
  26.4 10.3 %collective-permute-start.3 = (bf16[688,128]{1,0:T(8,128)(2,1)S(1)}, bf16[688,128]{1,0:T(8,128)(2,1)S(1)}, u32[]{:S(2)}, u32[]{:S(2)}) collective-permute-start(bf16[688,128]{1,0:T(8,128)(2,1)S(1)} %get-tuple-element.25.own), channel_id=1, source_target_pairs={{0,16},{4,20},{8,24},{12,28},{16,0},{20,4},{24,8},{28,12},{1,17},{... | collective-permute-start | bytes 528392 | tf_op jit(solution)/shard_map/ppermute | solution.py:405
  38.2 4.6 %collective-permute-start.7 = (bf16[368,128]{1,0:T(8,128)(2,1)S(1)}, bf16[368,128]{1,0:T(8,128)(2,1)S(1)}, u32[]{:S(2)}, u32[]{:S(2)}) collective-permute-start(bf16[368,128]{1,0:T(8,128)(2,1)S(1)} %get-tuple-element.30), channel_id=1, source_target_pairs={{0,2},{1,3},{2,0},{3,1},{4,6},{5,7},{6,4},{7,5},{8,10},{9,11},{10,... | collective-permute-start | bytes 282632 | tf_op jit(solution)/shard_map/ppermute | solution.py:405
  42.9 10.3 %collective-permute-start.8 = (bf16[2,368,128]{2,1,0:T(8,128)(2,1)S(1)}, bf16[2,368,128]{2,1,0:T(8,128)(2,1)S(1)}, u32[]{:S(2)}, u32[]{:S(2)}) collective-permute-start(bf16[2,368,128]{2,1,0:T(8,128)(2,1)S(1)} %pad_maximum_fusion.near), channel_id=1, source_target_pairs={{0,1},{1,0},{2,3},{3,2},{4,5},{5,4},{6,7},{7,6},{8,9},{9,8},{10,11... | collective-permute-start | bytes 565256 | tf_op jit(solution)/shard_map/ppermute | solution.py:405
  43.0 5.6 %collective-permute-start.4 = (bf16[448,128]{1,0:T(8,128)(2,1)S(1)}, bf16[448,128]{1,0:T(8,128)(2,1)S(1)}, u32[]{:S(2)}, u32[]{:S(2)}) collective-permute-start(bf16[448,128]{1,0:T(8,128)(2,1)S(1)} %get-tuple-element.27), channel_id=1, source_target_pairs={{0,4},{4,0},{8,12},{12,8},{16,20},{20,16},{24,28},{28,24},{1,5},{5... | collective-permute-start | bytes 344072 | tf_op jit(solution)/shard_map/ppermute | solution.py:405
  44.2 6.0 %collective-permute-start.5 = (bf16[448,128]{1,0:T(8,128)(2,1)S(1)}, bf16[448,128]{1,0:T(8,128)(2,1)S(1)}, u32[]{:S(2)}, u32[]{:S(2)}) collective-permute-start(bf16[448,128]{1,0:T(8,128)(2,1)S(1)} %get-tuple-element.28), channel_id=1, source_target_pairs={{0,8},{4,12},{8,0},{12,4},{16,24},{20,28},{24,16},{28,20},{1,9},{5... | collective-permute-start | bytes 344072 | tf_op jit(solution)/shard_map/ppermute | solution.py:405
  44.8 7.3 %collective-permute-start.6 = (bf16[448,128]{1,0:T(8,128)(2,1)S(1)}, bf16[448,128]{1,0:T(8,128)(2,1)S(1)}, u32[]{:S(2)}, u32[]{:S(2)}) collective-permute-start(bf16[448,128]{1,0:T(8,128)(2,1)S(1)} %get-tuple-element.29), channel_id=1, source_target_pairs={{0,12},{4,8},{8,4},{12,0},{16,28},{20,24},{24,20},{28,16},{1,13},{... | collective-permute-start | bytes 344072 | tf_op jit(solution)/shard_map/ppermute | solution.py:405

commit v2 on v0

--- a/solution.py
+++ b/solution.py
@@ -1,13 +1,473 @@
+import functools
 import math
 
 import jax
 import jax.numpy as jnp
+import numpy as np
 from jax import lax
+from jax.experimental import pallas as pl
+from jax.experimental.pallas import tpu as pltpu
 from jax.sharding import PartitionSpec as P
 
 HEADS = 16
 FEAT = 16
 CONV = 3
+
+GROUP = 4
+SYM = 160
+LANES = 128
+INFO = 159
+LOCAL = HEADS // GROUP // 2
+f32 = jnp.float32
+bf16 = jnp.bfloat16
+NT = (((1,), (1,)), ((), ()))
+NN = (((1,), (0,)), ((), ()))
+
+
+def dot(a, b, dims=NN):
+    return lax.dot_general(a, b, dims, preferred_element_type=f32)
+
+
+def iota(shape, axis):
+    return lax.broadcasted_iota(jnp.int32, shape, axis)
+
+
+def symmetric(y, scale_square):
+    twice = jnp.concatenate([y, y], 0)
+    rows = [y * y * scale_square] + [y * twice[o : o + FEAT] for o in range(1, 8)]
+    rest = jnp.where(iota((8, y.shape[1]), 0) == 0, 1.0, 0.0)
+    return jnp.concatenate(rows + [y, y[:8] * y[8:], rest], 0)
+
+
+def call(kernel, outs, scratch, limit, flops, moved, args, spaces=(), after=()):
+    vmem = pl.BlockSpec(memory_space=pltpu.VMEM)
+    given = [pl.BlockSpec(memory_space=space) for space in spaces]
+    if after:
+        body, plain = kernel, len(args)
+
+        def kernel(*refs):
+            body(*refs[:plain], *refs[plain + len(after) :])
+
+    return pl.pallas_call(
+        kernel,
+        out_shape=[jax.ShapeDtypeStruct(shape, dtype) for shape, dtype in outs],
+        in_specs=given
+        + [vmem] * (len(args) - len(given))
+        + [pl.BlockSpec(memory_space=pl.ANY)] * len(after),
+        out_specs=[vmem] * len(outs),
+        scratch_shapes=scratch,
+        compiler_params=pltpu.CompilerParams(vmem_limit_bytes=int(limit * 2**20)),
+        cost_estimate=pl.CostEstimate(flops=flops, bytes_accessed=moved, transcendentals=0),
+    )(*args, *after)
+
+
+TILES = (384, 512)
+
+
+def key_sums(keys):
+    keyed, rows = keys.shape
+    gram = dot(keys, keys, NT)
+    same = iota((keyed, keyed), 0) // FEAT == iota((keyed, keyed), 1) // FEAT
+    entry, lane = iota((FEAT, keyed), 0), iota((FEAT, keyed), 1)
+    pick = (lax.rem(lane, FEAT) == entry).astype(bf16)
+    folded = dot(pick, jnp.where(same, gram, 0.0).astype(bf16))
+    plain = dot(jnp.ones((8, rows), bf16), keys, NT)
+    mirror = lax.rem(entry - lax.rem(lane, FEAT) + FEAT, FEAT) == 9
+    return jnp.where(mirror, plain[0:1], folded).astype(bf16)
+
+
+def project_kernel(half, *refs):
+    x, wq, wk, wv = refs[:4]
+    refs = refs[4:]
+    if half:
+        length, early, o0, o1, o2, o3 = refs[:6]
+        refs = refs[6:]
+    else:
+        o0, o1, o2, o3, early = refs[:5]
+        refs = refs[5:]
+    x_v, wqk_v, wv_v, vt, qkt, sems = refs[:6]
+    rows = x.shape[1]
+    width = wv.shape[1] // 2
+    keyed = wq.shape[1] // 2
+    get_x = pltpu.make_async_copy(x.at[0], x_v, sems.at[0])
+    keyed_cut = pl.ds(half * keyed, keyed)
+    get_k = pltpu.make_async_copy(wk.at[:, keyed_cut], wqk_v.at[:, pl.ds(0, keyed)], sems.at[1])
+    get_q = pltpu.make_async_copy(wq.at[:, keyed_cut], wqk_v.at[:, pl.ds(keyed, keyed)], sems.at[2])
+    copies, at = [], 0
+    for j, tile in enumerate(TILES):
+        source = wv.at[:, pl.ds(half * width + at, tile)]
+        copies.append(pltpu.make_async_copy(source, wv_v.at[:, pl.ds(at, tile)], sems.at[3 + j]))
+        at += tile
+    for copy in (get_x, get_k, get_q, *copies):
+        copy.start()
+    place = lax.axis_index("blk")
+    mine = lax.rem(place, GROUP)
+    slab = width // GROUP
+    get_x.wait()
+    get_k.wait()
+    get_q.wait()
+    inputs = x_v[...]
+    qkt[...] = dot(inputs, wqk_v[...]).T.astype(bf16)
+    at = 0
+    for tile, copy in zip(TILES, copies):
+        copy.wait()
+        vt[at : at + tile, :] = dot(inputs, wv_v[:, at : at + tile]).T.astype(bf16)
+        at += tile
+    part = keyed // GROUP
+    for s, out in enumerate((o0, o1, o2, o3)):
+        dest = mine ^ s
+        out[0:slab, :] = vt[pl.ds(pl.multiple_of(slab * dest, 32), slab), :]
+        for base, at in ((0, slab), (keyed, slab + part)):
+            start = pl.multiple_of(base + part * dest, 32)
+            out[at : at + part, :] = qkt[pl.ds(start, part), :]
+    if not half:
+        early[...] = qkt[0:keyed, :]
+        return
+    alive = place * rows + iota((1, rows), 1) < length[...]
+    alive = jnp.where(alive, 1.0, 0.0).astype(bf16)
+    sums = [key_sums(early[...] * alive), key_sums(qkt[0:keyed, :] * alive)]
+    for out in (o0, o1, o2, o3):
+        out[slab + 2 * part :, :] = jnp.concatenate(sums, 0)
+
+
+def project(half, x, wq, wk, wv, *others):
+    _, rows, width = x.shape
+    keyed = wq.shape[1]
+    total = (width + 2 * keyed) // GROUP // 2 + (2 * FEAT if half else 0)
+    outs = [((total, rows), bf16)] * GROUP
+    scratch = [
+        pltpu.VMEM((rows, width), bf16),
+        pltpu.VMEM((width, keyed), bf16),
+        pltpu.VMEM((width, width // 2), bf16),
+        pltpu.VMEM((width // 2, rows), bf16),
+        pltpu.VMEM((keyed, rows), bf16),
+        pltpu.SemaphoreType.DMA((3 + len(TILES),)),
+    ]
+    if not half:
+        outs.append(((keyed // 2, rows), bf16))
+    flops = rows * width * (width + 2 * keyed)
+    kernel = functools.partial(project_kernel, half)
+    limit = LIMIT_B if half else LIMIT_A
+    args = [x, wq, wk, wv, *others]
+    return call(kernel, outs, scratch, limit, flops, flops // rows, args, [pltpu.HBM] * 4)
+
+
+LIMIT_A = 53.6
+LIMIT_B = 16
+
+
+def own_taps(conv, mine, taps, taps_v):
+    full = conv.shape[1]
+    padded = jnp.concatenate([conv[...], jnp.zeros((8 - CONV, full), f32)], 0)
+    for j in range(full // LANES):
+        taps_v[j * LANES : (j + 1) * LANES, :] = padded[:, j * LANES : (j + 1) * LANES].T
+    slab = full // 2 // GROUP
+    for half in range(2):
+        start = pl.multiple_of(full // 2 * half + slab * mine, 32)
+        taps[half * slab : (half + 1) * slab, :] = taps_v[pl.ds(start, slab), :]
+
+
+def state_kernel(half, *refs):
+    length, p0, p1, p2, p3 = refs[:5]
+    if half:
+        taps, aug, qk, state, held = refs[5:]
+    else:
+        conv, aug, qk, state, taps, held, taps_v = refs[5:]
+        own_taps(conv, lax.rem(lax.axis_index("blk"), GROUP), taps, taps_v)
+    rows = p0.shape[1]
+    place = lax.axis_index("blk")
+    mine, group = lax.rem(place, GROUP), place // GROUP
+    kept = held.shape[1]
+    size = kept // LOCAL - 2 * FEAT
+    values = LOCAL * size
+    tokens = GROUP * rows
+    for s, ref in enumerate((p0, p1, p2, p3)):
+        held[mine ^ s] = ref[0:kept, :]
+    if half:
+        sums = p0[kept:, :].astype(f32) + p1[kept:, :].astype(f32)
+        sums += p2[kept:, :].astype(f32) + p3[kept:, :].astype(f32)
+        state[LOCAL * SYM :, :] = sums.astype(bf16)
+    for b in range(GROUP):
+        qk[:, b * rows : (b + 1) * rows] = held[b, values:, :]
+    alive = (group * tokens + iota((1, tokens), 1) < length[...]).astype(f32)
+    token = iota((FEAT, tokens), 1)
+    row = iota((FEAT, tokens), 0)
+    marks = (row == 0) | ((row == 1) & (token == 0)) | ((row == 2) & (token == 1))
+    marks = jnp.where(marks, alive, 0.0).astype(bf16)
+    lane = iota((size, rows), 1)
+    last = iota((FEAT, rows), 0)
+    ends = iota((FEAT, rows), 1)
+    ends = ((last == 9) & (ends == rows - 1)) | ((last == 10) & (ends == rows - 2))
+    ends = ends.astype(bf16)
+    for h in range(LOCAL):
+        cut = slice(h * size, (h + 1) * size)
+        first = (half * LOCAL + h) * size
+        tap = taps[first : first + size, :]
+        tap = [jnp.broadcast_to(tap[:, t : t + 1], (size, rows)) for t in range(CONV)]
+        before = [jnp.zeros((size, rows), f32)] * 2
+        pieces = []
+        for b in range(GROUP):
+            now = held[b, cut, :].astype(f32)
+            rolled = [pltpu.roll(now, 1, 1), pltpu.roll(now, 2, 1)]
+            one = jnp.where(lane < 1, before[0], rolled[0])
+            two = jnp.where(lane < 2, before[1], rolled[1])
+            before = rolled
+            mixed = tap[0] * now + tap[1] * one + tap[2] * two
+            live = alive[:, b * rows : (b + 1) * rows]
+            pieces.append(jnp.where(live > 0, mixed, 0.0).astype(bf16))
+        aug_h = jnp.concatenate([jnp.concatenate(pieces, 1), marks], 0)
+        aug[h] = aug_h
+        y = qk[h * FEAT : (h + 1) * FEAT, :].astype(f32) * FEAT ** (-0.25)
+        own = dot(symmetric(y, 1.0).astype(bf16), aug_h, NT)
+        edge = dot(ends, held[GROUP - 1, h * size : h * size + LANES, :], NT)
+        state[h * SYM : h * SYM + 144, :] = own[:144].astype(bf16)
+        state[h * SYM + 144 : (h + 1) * SYM, :] = (own[144:] + edge).astype(bf16)
+
+
+def group_state(half, length, payloads, taps, after):
+    total, rows = payloads[0].shape
+    tokens = GROUP * rows
+    extra = 2 * FEAT if half else 0
+    outs = [
+        ((LOCAL, LANES, tokens), bf16),
+        ((2 * LOCAL * FEAT, tokens), bf16),
+        ((LOCAL * SYM + extra, LANES), bf16),
+    ]
+    scratch = [pltpu.VMEM((GROUP, total - extra, rows), bf16)]
+    if not half:
+        width = taps.shape[1]
+        outs.append(((width // GROUP, 8), f32))
+        scratch.append(pltpu.VMEM((width, 8), f32))
+    kernel = functools.partial(state_kernel, half)
+    args = [length, *payloads, taps]
+    return call(kernel, outs, scratch, 32, 100_000_000, 1_000_000, args, after=after)
+
+
+def local_kernel(aug, qk, num):
+    _, _, tokens = aug.shape
+    keyed = LOCAL * FEAT
+    half = tokens // 2
+    keys = qk[0:keyed, :].astype(f32).T.astype(bf16)
+    queries = qk[keyed:, :]
+    head = iota((keyed, tokens), 0) // FEAT
+    causal = iota((half, half), 0) <= iota((half, half), 1)
+
+    def scores(d):
+        return 1.0 + d * (0.25 + d * 0.03125)
+
+    for h in range(LOCAL):
+        only = jnp.where(head == h, queries, jnp.zeros_like(queries))
+        first = scores(dot(keys[:half], only[:, :half]))
+        first = jnp.where(causal, first, 0.0).astype(bf16)
+        num[h, :, 0:half] = dot(aug[h, :, 0:half], first)
+        lower = scores(dot(keys[half:], only[:, half:]))
+        lower = jnp.where(causal, lower, 0.0).astype(bf16)
+        upper = scores(dot(keys[:half], only[:, half:])).astype(bf16)
+        num[h, :, half:] = dot(aug[h, :, 0:half], upper) + dot(aug[h, :, half:], lower)
+
+
+def local_part(aug, qk, flops, after):
+    _, _, tokens = aug.shape
+    return call(local_kernel, [(aug.shape, f32)], [], 32, flops, 1000, [aug, qk], after=after)[0]
+
+
+def finish_kernel(half, *refs):
+    length, slot, num, own, got, qk, taps = refs[:7]
+    refs = refs[7:]
+    if half:
+        other, *firsts = refs[:5]
+        refs = refs[5:]
+    r0, r1, r2, r3, route, scr = refs
+    _, _, tokens = num.shape
+    rows = tokens // GROUP
+    size = taps.shape[0] // 2 // LOCAL
+    keyed = LOCAL * FEAT
+    place = lax.axis_index("blk")
+    mine, group = lax.rem(place, GROUP), place // GROUP
+    upper = group == 1
+    weight = jnp.where(upper, 1.0, 0.0)
+    alive = group * tokens + iota((1, tokens), 1) < length[...]
+    first = (iota((size, LANES), 1) == 0) & upper
+    aux = iota((LANES - size, SYM), 0)
+    finals = []
+    for h in range(LOCAL):
+        here = own[h * SYM : (h + 1) * SYM, :].astype(f32).T
+        there = got[h * SYM : (h + 1) * SYM, :].astype(f32).T
+        low = jnp.where(upper, there, here)
+        high = jnp.where(upper, here, there)
+        at = (half * LOCAL + h) * size
+        tap = taps[at : at + size, :]
+        last, second = low[:size, 153:154], low[:size, 154:155]
+        change0 = tap[:, 1:2] * last + tap[:, 2:3] * second
+        change1 = tap[:, 2:3] * last
+        key0, key1 = high[size + 1 : size + 2, :], high[size + 2 : size + 3, :]
+        body = low[:size] + change0 * key0 + change1 * key1
+        tail = jnp.where(aux == 2, key1, low[size:])
+        prior = jnp.concatenate([body, tail], 0)
+        finals.append(jnp.concatenate([body + high[:size], low[size:] + high[size:]], 0))
+        y = qk[keyed + h * FEAT : keyed + (h + 1) * FEAT, :].astype(f32) * FEAT ** (-0.25)
+        feats = symmetric(y, 0.5).astype(bf16)
+        all_num = num[h] + weight * dot(prior.astype(bf16), feats)
+        den = jnp.where(alive, all_num[size : size + 1, :], 1.0)
+        inverse = jnp.where(alive, 1.0 / den, 0.0)
+        top = all_num[:size]
+        extra = all_num[size + 2 : size + 3, 0:1]
+        edge = top[:, :LANES] - jnp.where(first, change1 * extra, 0.0)
+        top = jnp.concatenate([edge, top[:, LANES:]], 1)
+        result = (top * inverse).astype(bf16)
+        for b in range(GROUP):
+            scr[b, h * size : (h + 1) * size, :] = result[:, b * rows : (b + 1) * rows]
+    for s, out in enumerate((r0, r1, r2, r3)):
+        if half:
+            out[0 : LOCAL * size, :] = firsts[s][...]
+        out[half * LOCAL * size :, :] = scr[mine ^ s]
+    if not half:
+        for c in range(LOCAL):
+            route[c * SYM : (c + 1) * SYM, :] = finals[c].T.astype(bf16)
+        return
+    count = length[...]
+    for c in range(LOCAL):
+        final = jnp.where(upper, finals[c].T, other[c * SYM : (c + 1) * SYM, :].astype(f32))
+        if c == 0:
+            row, lane = iota(final.shape, 0), iota(final.shape, 1)
+            info = (slot[...], lax.shift_right_logical(count, 8), count & 255)
+            for at, value in enumerate(info):
+                final = jnp.where((row == INFO) & (lane == at), value.astype(f32), final)
+        route[c * SYM : (c + 1) * SYM, :] = final.astype(bf16)
+    sums = own[LOCAL * SYM :, :].astype(f32) + got[LOCAL * SYM :, :].astype(f32)
+    route[LOCAL * SYM :, :] = sums.astype(bf16)
+
+
+def finish(half, length, slot, num, own, got, qk, taps, other):
+    _, _, tokens = num.shape
+    rows = tokens // GROUP
+    width = taps.shape[0] // 2
+    outs = [(((1 + half) * width, rows), bf16)] * GROUP + [(own.shape, bf16)]
+    scratch = [pltpu.VMEM((GROUP, width, rows), bf16)]
+    args = [length, slot, num, own, got, qk, taps] + other
+    kernel = functools.partial(finish_kernel, half)
+    return call(kernel, outs, scratch, 32, 50_000_000, 20_000_000, args)
+
+
+def place_kernel(r0, r1, r2, r3, mixed, scr):
+    width = scr.shape[0]
+    mine = lax.rem(lax.axis_index("blk"), GROUP)
+    half = width // 2
+    slab = half // GROUP
+    for s, ref in enumerate((r0, r1, r2, r3)):
+        start = pl.multiple_of(slab * (mine ^ s), 32)
+        scr[pl.ds(start, slab), :] = ref[0:slab, :]
+        scr[pl.ds(pl.multiple_of(half + start, 32), slab), :] = ref[slab:, :]
+    for j in range(width // LANES):
+        cut = slice(j * LANES, (j + 1) * LANES)
+        mixed[0, :, cut] = scr[cut, :].astype(f32).T.astype(bf16)
+
+
+def place_tokens(results, after):
+    part, rows = results[0].shape
+    width = part * GROUP
+    outs = [((1, rows, width), bf16)]
+    scratch = [pltpu.VMEM((width, rows), bf16)]
+    return call(place_kernel, outs, scratch, 32, 1000, 1_000_000, results, after=after)[0]
+
+
+def hand_on_kernel(own, got, out):
+    other = (lax.axis_index("req") ^ 1).astype(f32)
+    kept = jnp.zeros(out.shape, f32)
+    for ref in (own, got):
+        here = ref[INFO : INFO + 1, 0:1].astype(f32) == other
+        kept += jnp.where(here, ref[...].astype(f32), 0.0)
+    out[...] = kept.astype(bf16)
+
+
+def hand_on(own, got, after):
+    args = [own, got]
+    return call(hand_on_kernel, [(own.shape, bf16)], [], 32, 1000, 300_000, args, after=after)[0]
+
+
+def expand_kernel(c0, c1, c2, spread, state, norm):
+    me = lax.axis_index("req").astype(f32)
+    kept = jnp.zeros(c0.shape, f32)
+    for ref in (c0, c1, c2):
+        here = ref[INFO : INFO + 1, 0:1].astype(f32) == me
+        kept += jnp.where(here, ref[...].astype(f32), 0.0)
+    size = state.shape[2] // LOCAL
+    expand = state.shape[0]
+    scale = jnp.where(iota((expand, LANES), 0) > FEAT, math.sqrt(0.5), 1.0)
+    wholes = []
+    for c in range(LOCAL):
+        whole = dot(spread[...], kept[c * SYM : (c + 1) * SYM].astype(bf16)) * scale
+        wholes.append(whole[:, :size])
+    state[...] = jnp.concatenate(wholes, 1).reshape(state.shape)
+    sums = kept[LOCAL * SYM :]
+    keyed = HEADS * FEAT
+    sums = jnp.concatenate([sums[:FEAT], sums[FEAT:]], 1)
+    plain = jnp.concatenate([sums[9:], sums[:9]], 0) * FEAT ** (-0.25)
+    products = sums * FEAT ** (-0.5)
+    b = iota((FEAT, keyed), 0)
+    entry = lax.rem(iota((FEAT, keyed), 1), FEAT)
+    big = [jnp.where(entry == b, plain, 0.0)]
+    for a in range(FEAT):
+        mirror = b == (a + 9) % FEAT
+        row = jnp.where(mirror, products[a : a + 1], products)
+        big.append(jnp.where(entry == jnp.where(mirror, b, a), row, 0.0))
+    big = jnp.concatenate(big, 0)
+    gather = (iota((keyed, HEADS), 0) // FEAT == iota((keyed, HEADS), 1)).astype(bf16)
+    rest = dot(big.astype(bf16), gather)
+    rest = rest * jnp.where(iota(rest.shape, 0) >= FEAT, math.sqrt(0.5), 1.0)
+    info = kept[INFO : INFO + 1]
+    count = info[:, 1:2] * 256.0 + info[:, 2:3]
+    norm[0] = jnp.concatenate([jnp.broadcast_to(count, (1, HEADS)), rest], 0).T
+
+
+def spread_rows():
+    table = np.zeros((1 + FEAT + FEAT * FEAT, SYM), np.float32)
+    table[0, 152] = 1
+    for a in range(FEAT):
+        table[1 + a, 128 + a] = 1
+        for b in range(FEAT):
+            o = (b - a) % FEAT
+            at = o * FEAT + a if o < 8 else (144 + min(a, b) if o == 8 else (FEAT - o) * FEAT + b)
+            table[1 + FEAT + a * FEAT + b, at] = 1
+    return table
+
+
+def expand_state(candidates, columns):
+    spread = jnp.asarray(spread_rows(), bf16)
+    expand = spread.shape[0]
+    outs = [((expand, 1, columns), f32), ((1, HEADS, expand), f32)]
+    return call(expand_kernel, outs, [], 32, 40_000_000, 1_000_000, [*candidates, spread])
+
+
+def swap(array, axis, by):
+    return lax.ppermute(array, axis, [(i, i ^ by) for i in range(lax.axis_size(axis))])
+
+
+def two_groups(
+    tokens_in, query_weight, key_weight, value_weight, conv_weight, prompt_lengths, decode_map
+):
+    width = tokens_in.shape[2]
+    length, slot = prompt_lengths.reshape(1, 1), decode_map.reshape(1, 1)
+    given = (tokens_in, query_weight, key_weight, value_weight)
+    *parts, early = project(0, *given)
+    sent = [[parts[0]] + [swap(parts[s], "blk", s) for s in (1, 2, 3)]]
+    parts = project(1, *given, length, early)
+    sent.append([parts[0]] + [swap(parts[s], "blk", s) for s in (1, 2, 3)])
+    *first, taps = group_state(0, length, sent[0], conv_weight, [])
+    second = group_state(1, length, sent[1], taps, [first[2]])
+    got = [swap(held[2], "blk", GROUP) for held in (first, second)]
+    aug, qk, own = first
+    num = local_part(aug, qk, 1000, [second[2]])
+    early = finish(0, length, slot, num, own, got[0], qk, taps, [])
+    aug, qk, own = second
+    num = local_part(aug, qk, 5_000_000_000, [early[4]])
+    *parts, total = finish(1, length, slot, num, own, got[1], qk, taps, [early[4], *early[:4]])
+    results = [parts[0]] + [swap(parts[s], "blk", s) for s in (1, 2, 3)]
+    beside = swap(total, "req", 2)
+    theirs = swap(hand_on(total, beside, results[1:2]), "req", 1)
+    state, norm = expand_state([total, beside, theirs], width // lax.axis_size("blk"))
+    mixed = place_tokens(results, [theirs])
+    return (mixed, jnp.swapaxes(state, 0, 1), jnp.swapaxes(norm, 1, 2))
 
 
 def from_behind(array, axis, by):
@@ -59,7 +519,7 @@
     )
 
 
-def on_device(
+def any_blocks(
     tokens_in, query_weight, key_weight, value_weight, conv_weight, prompt_lengths, decode_map
 ):
     rows = tokens_in.shape[1]
@@ -111,6 +571,12 @@
 
 
 def solution(mesh):
+    def on_device(*args):
+        rows = args[0].shape[1]
+        if mesh.shape["blk"] == 2 * GROUP and mesh.shape["req"] == 4 and rows == LANES:
+            return two_groups(*args)
+        return any_blocks(*args)
+
     return jax.shard_map(
         on_device,
         mesh=mesh,

time: 542 us -> 39.1 us (0.07)
  the two profiles are of different devices: /device:TPU:31 before, /device:TPU:0 now
where the time goes in v2:
time: 39.1 us; the launch traced here: 38.9 us
  starting transfers between devices  18.7 us (48%)
  Pallas kernels  12.9 us (33%)
  waiting for transfers between devices  5.16 us (13%)
  between operations  2.13 us (5%)
    ppermute x13, starting transfers between devices, swap(): lax.ppermute(array, axis, [(i, i ^ by) for i in range(lax.axis_size(axis))])  18.7 us
    pallas_call x11, Pallas kernels, call(): pl.pallas_call(kernel, out_shape=[jax.ShapeDtypeStruct(shape, dtype) for...  12.9 us
    ppermute x13, waiting for transfers between devices, swap(): lax.ppermute(array, axis, [(i, i ^ by) for i in range(lax.axis_size(axis))])  5.16 us
  transfers between devices with their start and end apart: 13, of which 5 were waited for; matrix products, arithmetic and copies ran while one was open for 0% of the time, Pallas kernels for 20%

profile of v2, /device:TPU:0, one launch (start us, length us, event | category | flops | bytes accessed | tf_op | source)
XLA Modules:
  0.0 38.9 jit_solution(1795582054230541246)
XLA Ops:
  0.7 3.0 %shard_map.103 = (bf16[288,128]{1,0:T(8,128)(2,1)S(1)}, bf16[288,128]{1,0:T(8,128)(2,1)S(1)}, bf16[288,128]{1,0:T(8,128)(2,1)S(1)}, bf16[288,128]{1,0:T(8,128)(2,1)S(1)}, bf16[128,128]{1,0:T(8,128)(2,1)S(1)}) custom-call(bf16[1,128,1792]{2,1,0:T(8,128)(2,1)} %refs_0_.3, bf16[1792,256]{1,0:T(8,128)(2,1)} %refs_1_.3, bf16[1792,256]{1,0:T(8,128)(2,1)} %refs_2_.3, ...), custom_call_target="tpu_custom_call" | custom-call | flops 528482304 | bytes 4128768 | tf_op jit(solution)/shard_map/pallas_call | solution.py:51
  3.7 3.0 %collective-permute-start.3 = (bf16[288,128]{1,0:T(8,128)(2,1)S(1)}, bf16[288,128]{1,0:T(8,128)(2,1)S(1)}, u32[]{:S(2)}, u32[]{:S(2)}) collective-permute-start(bf16[288,128]{1,0:T(8,128)(2,1)S(1)} %get-tuple-element.37), channel_id=1, source_target_pairs={{0,4},{4,0},{8,12},{12,8},{16,20},{20,16},{24,28},{28,24},{1,5},{5... | collective-permute-start | bytes 221192 | tf_op jit(solution)/shard_map/ppermute | solution.py:443
  6.8 1.6 %collective-permute-start.4 = (bf16[288,128]{1,0:T(8,128)(2,1)S(1)}, bf16[288,128]{1,0:T(8,128)(2,1)S(1)}, u32[]{:S(2)}, u32[]{:S(2)}) collective-permute-start(bf16[288,128]{1,0:T(8,128)(2,1)S(1)} %get-tuple-element.38), channel_id=1, source_target_pairs={{0,8},{4,12},{8,0},{12,4},{16,24},{20,28},{24,16},{28,20},{1,9},{5... | collective-permute-start | bytes 221192 | tf_op jit(solution)/shard_map/ppermute | solution.py:443
  9.0 2.5 %shard_map.104 = (bf16[320,128]{1,0:T(8,128)(2,1)S(1)}, bf16[320,128]{1,0:T(8,128)(2,1)S(1)}, bf16[320,128]{1,0:T(8,128)(2,1)S(1)}, bf16[320,128]{1,0:T(8,128)(2,1)S(1)}) custom-call(bf16[1,128,1792]{2,1,0:T(8,128)(2,1)S(1)} %copy-done.3, bf16[1792,256]{1,0:T(8,128)(2,1)S(1)} %copy-done.1, bf16[1792,256]{1,0:T(8,128)(2,1)S(1)} %copy-done.2, ...), custom_call_target="tpu_custom_call" | custom-call | flops 528482304 | bytes 4128768 | tf_op jit(solution)/shard_map/pallas_call | solution.py:51
  11.6 2.0 %collective-permute-start = (bf16[320,128]{1,0:T(8,128)(2,1)S(1)}, bf16[320,128]{1,0:T(8,128)(2,1)S(1)}, u32[]{:S(2)}, u32[]{:S(2)}) collective-permute-start(bf16[320,128]{1,0:T(8,128)(2,1)S(1)} %get-tuple-element.33), channel_id=1, source_target_pairs={{0,4},{4,0},{8,12},{12,8},{16,20},{20,16},{24,28},{28,24},{1,5},{5... | collective-permute-start | bytes 245768 | tf_op jit(solution)/shard_map/ppermute | solution.py:443
  13.5 1.6 %collective-permute-start.1 = (bf16[320,128]{1,0:T(8,128)(2,1)S(1)}, bf16[320,128]{1,0:T(8,128)(2,1)S(1)}, u32[]{:S(2)}, u32[]{:S(2)}) collective-permute-start(bf16[320,128]{1,0:T(8,128)(2,1)S(1)} %get-tuple-element.34), channel_id=1, source_target_pairs={{0,8},{4,12},{8,0},{12,4},{16,24},{20,28},{24,16},{28,20},{1,9},{5... | collective-permute-start | bytes 245768 | tf_op jit(solution)/shard_map/ppermute | solution.py:443
  15.1 0.9 %shard_map.105 = (bf16[2,128,512]{2,1,0:T(8,128)(2,1)S(1)}, bf16[64,512]{1,0:T(8,128)(2,1)S(1)}, bf16[320,128]{1,0:T(8,128)(2,1)S(1)}, f32[448,8]{1,0:T(8,128)S(1)}) custom-call(s32[1,1]{1,0:T(1,128)} %bitcast.5.refs_0_, bf16[288,128]{1,0:T(8,128)(2,1)S(1)} %get-tuple-element.36.refs_1_, bf16[288,128]{1,0:T(8,128)(2,1)S(1)} %collective-permute-done.3.refs_2_, ...), custom_call_target="tpu_custom_call" | custom-call | flops 100000000 | bytes 1000000 | tf_op jit(solution)/shard_map/pallas_call | solution.py:51
  16.0 3.0 %collective-permute-start.6 = (bf16[320,128]{1,0:T(8,128)(2,1)S(1)}, bf16[320,128]{1,0:T(8,128)(2,1)S(1)}, u32[]{:S(2)}, u32[]{:S(2)}) collective-permute-start(bf16[320,128]{1,0:T(8,128)(2,1)S(1)} %get-tuple-element.41.refs_6_.refs_3_), channel_id=1, source_target_pairs={{0,16},{4,20},{8,24},{12,28},{16,0},{20,4},{24,8},{28,12},{1,17},{... | collective-permute-start | bytes 245768 | tf_op jit(solution)/shard_map/ppermute | solution.py:443
  19.7 1.1 %collective-permute-done.2.refs_4_ = bf16[320,128]{1,0:T(8,128)(2,1)S(1)} collective-permute-done((bf16[320,128]{1,0:T(8,128)(2,1)S(1)}, bf16[320,128]{1,0:T(8,128)(2,1)S(1)}, u32[]{:S(2)}, u32[]{:S(2)}) %collective-permute-start.2) | collective-permute-done | bytes 81952 | tf_op jit(solution)/shard_map/ppermute | solution.py:443
  20.8 0.6 %shard_map.106 = (bf16[2,128,512]{2,1,0:T(8,128)(2,1)S(1)}, bf16[64,512]{1,0:T(8,128)(2,1)S(1)}, bf16[352,128]{1,0:T(8,128)(2,1)S(1)}) custom-call(s32[1,1]{1,0:T(1,128)} %bitcast.6.refs_0_, bf16[320,128]{1,0:T(8,128)(2,1)S(1)} %get-tuple-element.32.refs_1_, bf16[320,128]{1,0:T(8,128)(2,1)S(1)} %collective-permute-done.refs_2_, ...), custom_call_target="tpu_custom_call" | custom-call | flops 100000000 | bytes 1000000 | tf_op jit(solution)/shard_map/pallas_call | solution.py:51
  21.4 2.4 %collective-permute-start.7 = (bf16[352,128]{1,0:T(8,128)(2,1)S(1)}, bf16[352,128]{1,0:T(8,128)(2,1)S(1)}, u32[]{:S(2)}, u32[]{:S(2)}) collective-permute-start(bf16[352,128]{1,0:T(8,128)(2,1)S(1)} %get-tuple-element.46.refs_2_.refs_3_), channel_id=1, source_target_pairs={{0,16},{4,20},{8,24},{12,28},{16,0},{20,4},{24,8},{28,12},{1,17},{... | collective-permute-start | bytes 270344 | tf_op jit(solution)/shard_map/ppermute | solution.py:443
  23.8 0.9 %shard_map.107.refs_2_ = f32[2,128,512]{2,1,0:T(8,128)S(1)} custom-call(bf16[2,128,512]{2,1,0:T(8,128)(2,1)S(1)} %get-tuple-element.44.refs_0_, bf16[64,512]{1,0:T(8,128)(2,1)S(1)} %get-tuple-element.45.refs_1_.refs_5_, bf16[352,128]{1,0:T(8,128)(2,1)S(1)} %get-tuple-element.46.refs_2_.refs_3_), custom_call_target="tpu_custom_call" | custom-call | flops 1000 | bytes 1000 | tf_op jit(solution)/shard_map/pallas_call | solution.py:51
  24.7 0.8 %shard_map.108 = (bf16[224,128]{1,0:T(8,128)(2,1)S(1)}, bf16[224,128]{1,0:T(8,128)(2,1)S(1)}, bf16[224,128]{1,0:T(8,128)(2,1)S(1)}, bf16[224,128]{1,0:T(8,128)(2,1)S(1)}, bf16[320,128]{1,0:T(8,128)(2,1)S(1)}) custom-call(s32[1,1]{1,0:T(1,128)} %bitcast.7.refs_0_, s32[1,1]{1,0:T(1,128)} %bitcast.9.refs_1_, f32[2,128,512]{2,1,0:T(8,128)S(1)} %shard_map.107.refs_2_, ...), custom_call_target="tpu_custom_call" | custom-call | flops 50000000 | bytes 20000000 | tf_op jit(solution)/shard_map/pallas_call | solution.py:51
  25.5 0.9 %shard_map.109.refs_2_ = f32[2,128,512]{2,1,0:T(8,128)S(1)} custom-call(bf16[2,128,512]{2,1,0:T(8,128)(2,1)S(1)} %get-tuple-element.42.refs_0_, bf16[64,512]{1,0:T(8,128)(2,1)S(1)} %get-tuple-element.43.refs_1_.refs_5_, bf16[320,128]{1,0:T(8,128)(2,1)S(1)} %get-tuple-element.47.refs_2_.refs_7_), custom_call_target="tpu_custom_call" | custom-call | flops 5000000000 | bytes 1000 | tf_op jit(solution)/shard_map/pallas_call | solution.py:51
  26.5 1.4 %collective-permute-done.7.refs_4_ = bf16[352,128]{1,0:T(8,128)(2,1)S(1)} collective-permute-done((bf16[352,128]{1,0:T(8,128)(2,1)S(1)}, bf16[352,128]{1,0:T(8,128)(2,1)S(1)}, u32[]{:S(2)}, u32[]{:S(2)}) %collective-permute-start.7) | collective-permute-done | bytes 90144 | tf_op jit(solution)/shard_map/ppermute | solution.py:443
  27.8 1.0 %shard_map.110 = (bf16[448,128]{1,0:T(8,128)(2,1)S(1)}, bf16[448,128]{1,0:T(8,128)(2,1)S(1)}, bf16[448,128]{1,0:T(8,128)(2,1)S(1)}, bf16[448,128]{1,0:T(8,128)(2,1)S(1)}, bf16[352,128]{1,0:T(8,128)(2,1)S(1)}) custom-call(s32[1,1]{1,0:T(1,128)} %bitcast.8.refs_0_, s32[1,1]{1,0:T(1,128)} %bitcast.10.refs_1_, f32[2,128,512]{2,1,0:T(8,128)S(1)} %shard_map.109.refs_2_, ...), custom_call_target="tpu_custom_call" | custom-call | flops 50000000 | bytes 20000000 | tf_op jit(solution)/shard_map/pallas_call | solution.py:51
  28.9 1.6 %collective-permute-start.11 = (bf16[352,128]{1,0:T(8,128)(2,1)S(1)}, bf16[352,128]{1,0:T(8,128)(2,1)S(1)}, u32[]{:S(2)}, u32[]{:S(2)}) collective-permute-start(bf16[352,128]{1,0:T(8,128)(2,1)S(1)} %get-tuple-element.56.refs_0_.c0), channel_id=1, source_target_pairs={{0,2},{1,3},{2,0},{3,1},{4,6},{5,7},{6,4},{7,5},{8,10},{9,11},{10,... | collective-permute-start | bytes 270344 | tf_op jit(solution)/shard_map/ppermute | solution.py:443
  30.5 1.0 %collective-permute-start.9 = (bf16[448,128]{1,0:T(8,128)(2,1)S(1)}, bf16[448,128]{1,0:T(8,128)(2,1)S(1)}, u32[]{:S(2)}, u32[]{:S(2)}) collective-permute-start(bf16[448,128]{1,0:T(8,128)(2,1)S(1)} %get-tuple-element.54), channel_id=1, source_target_pairs={{0,8},{4,12},{8,0},{12,4},{16,24},{20,28},{24,16},{28,20},{1,9},{5... | collective-permute-start | bytes 344072 | tf_op jit(solution)/shard_map/ppermute | solution.py:443
  31.5 2.4 %collective-permute-start.10 = (bf16[448,128]{1,0:T(8,128)(2,1)S(1)}, bf16[448,128]{1,0:T(8,128)(2,1)S(1)}, u32[]{:S(2)}, u32[]{:S(2)}) collective-permute-start(bf16[448,128]{1,0:T(8,128)(2,1)S(1)} %get-tuple-element.55), channel_id=1, source_target_pairs={{0,12},{4,8},{8,4},{12,0},{16,28},{20,24},{24,20},{28,16},{1,13},{... | collective-permute-start | bytes 344072 | tf_op jit(solution)/shard_map/ppermute | solution.py:443
  33.9 0.5 %collective-permute-done.8.refs_2_.refs_1_ = bf16[448,128]{1,0:T(8,128)(2,1)S(1)} collective-permute-done((bf16[448,128]{1,0:T(8,128)(2,1)S(1)}, bf16[448,128]{1,0:T(8,128)(2,1)S(1)}, u32[]{:S(2)}, u32[]{:S(2)}) %collective-permute-start.8) | collective-permute-done | bytes 114720 | tf_op jit(solution)/shard_map/ppermute | solution.py:443
  34.5 1.3 %collective-permute-done.12.refs_4_.c2 = bf16[352,128]{1,0:T(8,128)(2,1)S(1)} collective-permute-done((bf16[352,128]{1,0:T(8,128)(2,1)S(1)}, bf16[352,128]{1,0:T(8,128)(2,1)S(1)}, u32[]{:S(2)}, u32[]{:S(2)}) %collective-permute-start.12) | collective-permute-done | bytes 90144 | tf_op jit(solution)/shard_map/ppermute | solution.py:443
  35.8 1.1 %shard_map.113 = (f32[273,1,224]{2,1,0:T(1,128)}, f32[1,16,273]{2,1,0:T(8,128)}) custom-call(bf16[352,128]{1,0:T(8,128)(2,1)S(1)} %get-tuple-element.56.refs_0_.c0, bf16[352,128]{1,0:T(8,128)(2,1)S(1)} %collective-permute-done.11.refs_1_.c1, bf16[352,128]{1,0:T(8,128)(2,1)S(1)} %collective-permute-done.12.refs_4_.c2, bf16[273,160]{1,0:T(8,128)(2,1)S(1)} %copy-done.4), custom_call_target="tpu_custom_call" | custom-call | flops 40000000 | bytes 1000000 | tf_op jit(solution)/shard_map/pallas_call | solution.py:51
  36.9 1.0 %collective-permute-done.10.refs_3_ = bf16[448,128]{1,0:T(8,128)(2,1)S(1)} collective-permute-done((bf16[448,128]{1,0:T(8,128)(2,1)S(1)}, bf16[448,128]{1,0:T(8,128)(2,1)S(1)}, u32[]{:S(2)}, u32[]{:S(2)}) %collective-permute-start.10) | collective-permute-done | bytes 114720 | tf_op jit(solution)/shard_map/ppermute | solution.py:443
  37.9 1.0 %shard_map.112 = bf16[1,128,1792]{2,1,0:T(8,128)(2,1)} custom-call(bf16[448,128]{1,0:T(8,128)(2,1)S(1)} %get-tuple-element.52.refs_0_, bf16[448,128]{1,0:T(8,128)(2,1)S(1)} %collective-permute-done.8.refs_2_.refs_1_, bf16[448,128]{1,0:T(8,128)(2,1)S(1)} %collective-permute-done.9.refs_2_, bf16[448,128]{1,0:T(8,128)(2,1)S(1)} %collective-permute-done.10.refs_3_, ...), custom_call_target="tpu_custom_call" | custom-call | flops 1000 | bytes 1000000 | tf_op jit(solution)/shard_map/pallas_call | solution.py:51
  (25 shorter events, 0.3 us)
Async XLA Ops:
  0.6 8.4 %copy-start = (bf16[1792,1792]{1,0:T(8,128)(2,1)S(1)}, bf16[1792,1792]{1,0:T(8,128)(2,1)}, u32[]{:S(2)}) copy-start(bf16[1792,1792]{1,0:T(8,128)(2,1)} %refs_3_.3) | copy-start | bytes 19267588
  0.6 8.4 %copy-start.2 = (bf16[1792,256]{1,0:T(8,128)(2,1)S(1)}, bf16[1792,256]{1,0:T(8,128)(2,1)}, u32[]{:S(2)}) copy-start(bf16[1792,256]{1,0:T(8,128)(2,1)} %refs_2_.3) | copy-start | bytes 2752516
  0.7 8.4 %copy-start.1 = (bf16[1792,256]{1,0:T(8,128)(2,1)S(1)}, bf16[1792,256]{1,0:T(8,128)(2,1)}, u32[]{:S(2)}) copy-start(bf16[1792,256]{1,0:T(8,128)(2,1)} %refs_1_.3) | copy-start | bytes 2752516
  0.7 8.4 %copy-start.3 = (bf16[1,128,1792]{2,1,0:T(8,128)(2,1)S(1)}, bf16[1,128,1792]{2,1,0:T(8,128)(2,1)}, u32[]{:S(2)}) copy-start(bf16[1,128,1792]{2,1,0:T(8,128)(2,1)} %refs_0_.3) | copy-start | bytes 1376260
  3.7 11.4 %copy-start.5 = (f32[3,1792]{1,0:T(4,128)S(1)}, f32[3,1792]{1,0:T(4,128)}, u32[]{:S(2)}) copy-start(f32[3,1792]{1,0:T(4,128)} %refs_5_.1) | copy-start | bytes 64516
  3.7 11.4 %collective-permute-start.3 = (bf16[288,128]{1,0:T(8,128)(2,1)S(1)}, bf16[288,128]{1,0:T(8,128)(2,1)S(1)}, u32[]{:S(2)}, u32[]{:S(2)}) collective-permute-start(bf16[288,128]{1,0:T(8,128)(2,1)S(1)} %get-tuple-element.37), channel_id=1, source_target_pairs={{0,4},{4,0},{8,12},{12,8},{16,20},{20,16},{24,28},{28,24},{1,5},{5... | collective-permute-start | bytes 221192 | tf_op jit(solution)/shard_map/ppermute | solution.py:443
  6.8 8.3 %collective-permute-start.4 = (bf16[288,128]{1,0:T(8,128)(2,1)S(1)}, bf16[288,128]{1,0:T(8,128)(2,1)S(1)}, u32[]{:S(2)}, u32[]{:S(2)}) collective-permute-start(bf16[288,128]{1,0:T(8,128)(2,1)S(1)} %get-tuple-element.38), channel_id=1, source_target_pairs={{0,8},{4,12},{8,0},{12,4},{16,24},{20,28},{24,16},{28,20},{1,9},{5... | collective-permute-start | bytes 221192 | tf_op jit(solution)/shard_map/ppermute | solution.py:443
  8.4 6.8 %collective-permute-start.5 = (bf16[288,128]{1,0:T(8,128)(2,1)S(1)}, bf16[288,128]{1,0:T(8,128)(2,1)S(1)}, u32[]{:S(2)}, u32[]{:S(2)}) collective-permute-start(bf16[288,128]{1,0:T(8,128)(2,1)S(1)} %get-tuple-element.39), channel_id=1, source_target_pairs={{0,12},{4,8},{8,4},{12,0},{16,28},{20,24},{24,20},{28,16},{1,13},{... | collective-permute-start | bytes 221192 | tf_op jit(solution)/shard_map/ppermute | solution.py:443
  11.6 8.2 %collective-permute-start = (bf16[320,128]{1,0:T(8,128)(2,1)S(1)}, bf16[320,128]{1,0:T(8,128)(2,1)S(1)}, u32[]{:S(2)}, u32[]{:S(2)}) collective-permute-start(bf16[320,128]{1,0:T(8,128)(2,1)S(1)} %get-tuple-element.33), channel_id=1, source_target_pairs={{0,4},{4,0},{8,12},{12,8},{16,20},{20,16},{24,28},{28,24},{1,5},{5... | collective-permute-start | bytes 245768 | tf_op jit(solution)/shard_map/ppermute | solution.py:443
  13.5 6.2 %collective-permute-start.1 = (bf16[320,128]{1,0:T(8,128)(2,1)S(1)}, bf16[320,128]{1,0:T(8,128)(2,1)S(1)}, u32[]{:S(2)}, u32[]{:S(2)}) collective-permute-start(bf16[320,128]{1,0:T(8,128)(2,1)S(1)} %get-tuple-element.34), channel_id=1, source_target_pairs={{0,8},{4,12},{8,0},{12,4},{16,24},{20,28},{24,16},{28,20},{1,9},{5... | collective-permute-start | bytes 245768 | tf_op jit(solution)/shard_map/ppermute | solution.py:443
  15.1 5.7 %collective-permute-start.2 = (bf16[320,128]{1,0:T(8,128)(2,1)S(1)}, bf16[320,128]{1,0:T(8,128)(2,1)S(1)}, u32[]{:S(2)}, u32[]{:S(2)}) collective-permute-start(bf16[320,128]{1,0:T(8,128)(2,1)S(1)} %get-tuple-element.35), channel_id=1, source_target_pairs={{0,12},{4,8},{8,4},{12,0},{16,28},{20,24},{24,20},{28,16},{1,13},{... | collective-permute-start | bytes 245768 | tf_op jit(solution)/shard_map/ppermute | solution.py:443
  16.0 8.7 %collective-permute-start.6 = (bf16[320,128]{1,0:T(8,128)(2,1)S(1)}, bf16[320,128]{1,0:T(8,128)(2,1)S(1)}, u32[]{:S(2)}, u32[]{:S(2)}) collective-permute-start(bf16[320,128]{1,0:T(8,128)(2,1)S(1)} %get-tuple-element.41.refs_6_.refs_3_), channel_id=1, source_target_pairs={{0,16},{4,20},{8,24},{12,28},{16,0},{20,4},{24,8},{28,12},{1,17},{... | collective-permute-start | bytes 245768 | tf_op jit(solution)/shard_map/ppermute | solution.py:443
  21.4 6.4 %collective-permute-start.7 = (bf16[352,128]{1,0:T(8,128)(2,1)S(1)}, bf16[352,128]{1,0:T(8,128)(2,1)S(1)}, u32[]{:S(2)}, u32[]{:S(2)}) collective-permute-start(bf16[352,128]{1,0:T(8,128)(2,1)S(1)} %get-tuple-element.46.refs_2_.refs_3_), channel_id=1, source_target_pairs={{0,16},{4,20},{8,24},{12,28},{16,0},{20,4},{24,8},{28,12},{1,17},{... | collective-permute-start | bytes 270344 | tf_op jit(solution)/shard_map/ppermute | solution.py:443
  25.5 10.3 %copy-start.4 = (bf16[273,160]{1,0:T(8,128)(2,1)S(1)}, bf16[273,160]{1,0:T(8,128)(2,1)}, u32[]{:S(2)}) copy-start(bf16[273,160]{1,0:T(8,128)(2,1)} %constant.2.clone.spread) | copy-start | bytes 262084
  28.8 5.5 %collective-permute-start.8 = (bf16[448,128]{1,0:T(8,128)(2,1)S(1)}, bf16[448,128]{1,0:T(8,128)(2,1)S(1)}, u32[]{:S(2)}, u32[]{:S(2)}) collective-permute-start(bf16[448,128]{1,0:T(8,128)(2,1)S(1)} %get-tuple-element.53), channel_id=1, source_target_pairs={{0,4},{4,0},{8,12},{12,8},{16,20},{20,16},{24,28},{28,24},{1,5},{5... | collective-permute-start | bytes 344072 | tf_op jit(solution)/shard_map/ppermute | solution.py:443
  28.9 5.0 %collective-permute-start.11 = (bf16[352,128]{1,0:T(8,128)(2,1)S(1)}, bf16[352,128]{1,0:T(8,128)(2,1)S(1)}, u32[]{:S(2)}, u32[]{:S(2)}) collective-permute-start(bf16[352,128]{1,0:T(8,128)(2,1)S(1)} %get-tuple-element.56.refs_0_.c0), channel_id=1, source_target_pairs={{0,2},{1,3},{2,0},{3,1},{4,6},{5,7},{6,4},{7,5},{8,10},{9,11},{10,... | collective-permute-start | bytes 270344 | tf_op jit(solution)/shard_map/ppermute | solution.py:443
  30.5 6.4 %collective-permute-start.9 = (bf16[448,128]{1,0:T(8,128)(2,1)S(1)}, bf16[448,128]{1,0:T(8,128)(2,1)S(1)}, u32[]{:S(2)}, u32[]{:S(2)}) collective-permute-start(bf16[448,128]{1,0:T(8,128)(2,1)S(1)} %get-tuple-element.54), channel_id=1, source_target_pairs={{0,8},{4,12},{8,0},{12,4},{16,24},{20,28},{24,16},{28,20},{1,9},{5... | collective-permute-start | bytes 344072 | tf_op jit(solution)/shard_map/ppermute | solution.py:443
  31.5 6.4 %collective-permute-start.10 = (bf16[448,128]{1,0:T(8,128)(2,1)S(1)}, bf16[448,128]{1,0:T(8,128)(2,1)S(1)}, u32[]{:S(2)}, u32[]{:S(2)}) collective-permute-start(bf16[448,128]{1,0:T(8,128)(2,1)S(1)} %get-tuple-element.55), channel_id=1, source_target_pairs={{0,12},{4,8},{8,4},{12,0},{16,28},{20,24},{24,20},{28,16},{1,13},{... | collective-permute-start | bytes 344072 | tf_op jit(solution)/shard_map/ppermute | solution.py:443
  34.4 1.4 %collective-permute-start.12 = (bf16[352,128]{1,0:T(8,128)(2,1)S(1)}, bf16[352,128]{1,0:T(8,128)(2,1)S(1)}, u32[]{:S(2)}, u32[]{:S(2)}) collective-permute-start(bf16[352,128]{1,0:T(8,128)(2,1)S(1)} %shard_map.111), channel_id=1, source_target_pairs={{0,1},{1,0},{2,3},{3,2},{4,5},{5,4},{6,7},{7,6},{8,9},{9,8},{10,11... | collective-permute-start | bytes 270344 | tf_op jit(solution)/shard_map/ppermute | solution.py:443

commit v3 on v2

--- a/solution.py
+++ b/solution.py
@@ -18,6 +18,7 @@
 LANES = 128
 INFO = 159
 LOCAL = HEADS // GROUP // 2
+ORDER = (0, 3, 2, 1)
 f32 = jnp.float32
 bf16 = jnp.bfloat16
 NT = (((1,), (1,)), ((), ()))
@@ -114,7 +115,7 @@
         vt[at : at + tile, :] = dot(inputs, wv_v[:, at : at + tile]).T.astype(bf16)
         at += tile
     part = keyed // GROUP
-    for s, out in enumerate((o0, o1, o2, o3)):
+    for s, out in zip(ORDER, (o0, o1, o2, o3)):
         dest = mine ^ s
         out[0:slab, :] = vt[pl.ds(pl.multiple_of(slab * dest, 32), slab), :]
         for base, at in ((0, slab), (keyed, slab + part)):
@@ -157,14 +158,18 @@
 
 
 def own_taps(conv, mine, taps, taps_v):
-    full = conv.shape[1]
-    padded = jnp.concatenate([conv[...], jnp.zeros((8 - CONV, full), f32)], 0)
-    for j in range(full // LANES):
-        taps_v[j * LANES : (j + 1) * LANES, :] = padded[:, j * LANES : (j + 1) * LANES].T
-    slab = full // 2 // GROUP
-    for half in range(2):
-        start = pl.multiple_of(full // 2 * half + slab * mine, 32)
-        taps[half * slab : (half + 1) * slab, :] = taps_v[pl.ds(start, slab), :]
+    half = conv.shape[1] // 2
+    slab = half // GROUP
+    wide = taps_v.shape[0]
+    start = jnp.minimum(slab * mine // LANES * LANES, half - wide)
+    inside = pl.multiple_of(slab * mine - start, 32)
+    for h in range(2):
+        cut = conv[:, pl.ds(pl.multiple_of(half * h + start, LANES), wide)]
+        padded = jnp.concatenate([cut, jnp.zeros((8 - CONV, wide), f32)], 0)
+        for j in range(wide // LANES):
+            rows = slice(j * LANES, (j + 1) * LANES)
+            taps_v[rows, :] = padded[:, rows].T
+        taps[h * slab : (h + 1) * slab, :] = taps_v[pl.ds(inside, slab), :]
 
 
 def state_kernel(half, *refs):
@@ -181,7 +186,7 @@
     size = kept // LOCAL - 2 * FEAT
     values = LOCAL * size
     tokens = GROUP * rows
-    for s, ref in enumerate((p0, p1, p2, p3)):
+    for s, ref in zip(ORDER, (p0, p1, p2, p3)):
         held[mine ^ s] = ref[0:kept, :]
     if half:
         sums = p0[kept:, :].astype(f32) + p1[kept:, :].astype(f32)
@@ -235,9 +240,9 @@
     ]
     scratch = [pltpu.VMEM((GROUP, total - extra, rows), bf16)]
     if not half:
-        width = taps.shape[1]
-        outs.append(((width // GROUP, 8), f32))
-        scratch.append(pltpu.VMEM((width, 8), f32))
+        slab = taps.shape[1] // GROUP
+        outs.append(((slab, 8), f32))
+        scratch.append(pltpu.VMEM(((slab // 2 // LANES + 2) * LANES, 8), f32))
     kernel = functools.partial(state_kernel, half)
     args = [length, *payloads, taps]
     return call(kernel, outs, scratch, 32, 100_000_000, 1_000_000, args, after=after)
@@ -317,9 +322,9 @@
         result = (top * inverse).astype(bf16)
         for b in range(GROUP):
             scr[b, h * size : (h + 1) * size, :] = result[:, b * rows : (b + 1) * rows]
-    for s, out in enumerate((r0, r1, r2, r3)):
+    for j, (s, out) in enumerate(zip(ORDER, (r0, r1, r2, r3))):
         if half:
-            out[0 : LOCAL * size, :] = firsts[s][...]
+            out[0 : LOCAL * size, :] = firsts[j][...]
         out[half * LOCAL * size :, :] = scr[mine ^ s]
     if not half:
         for c in range(LOCAL):
@@ -330,8 +335,8 @@
         final = jnp.where(upper, finals[c].T, other[c * SYM : (c + 1) * SYM, :].astype(f32))
         if c == 0:
             row, lane = iota(final.shape, 0), iota(final.shape, 1)
-            info = (slot[...], lax.shift_right_logical(count, 8), count & 255)
-            for at, value in enumerate(info):
+            values = (slot[...], lax.shift_right_logical(count, 8), count & 255)
+            for at, value in enumerate(values):
                 final = jnp.where((row == INFO) & (lane == at), value.astype(f32), final)
         route[c * SYM : (c + 1) * SYM, :] = final.astype(bf16)
     sums = own[LOCAL * SYM :, :].astype(f32) + got[LOCAL * SYM :, :].astype(f32)
@@ -354,13 +359,13 @@
     mine = lax.rem(lax.axis_index("blk"), GROUP)
     half = width // 2
     slab = half // GROUP
-    for s, ref in enumerate((r0, r1, r2, r3)):
+    for s, ref in zip(ORDER, (r0, r1, r2, r3)):
         start = pl.multiple_of(slab * (mine ^ s), 32)
         scr[pl.ds(start, slab), :] = ref[0:slab, :]
         scr[pl.ds(pl.multiple_of(half + start, 32), slab), :] = ref[slab:, :]
     for j in range(width // LANES):
         cut = slice(j * LANES, (j + 1) * LANES)
-        mixed[0, :, cut] = scr[cut, :].astype(f32).T.astype(bf16)
+        mixed[0, :, cut] = scr[cut, :].T
 
 
 def place_tokens(results, after):
@@ -371,8 +376,11 @@
     return call(place_kernel, outs, scratch, 32, 1000, 1_000_000, results, after=after)[0]
 
 
+ROUTE = (2, 1)
+
+
 def hand_on_kernel(own, got, out):
-    other = (lax.axis_index("req") ^ 1).astype(f32)
+    other = (lax.axis_index("req") ^ ROUTE[1]).astype(f32)
     kept = jnp.zeros(out.shape, f32)
     for ref in (own, got):
         here = ref[INFO : INFO + 1, 0:1].astype(f32) == other
@@ -439,6 +447,10 @@
     return call(expand_kernel, outs, [], 32, 40_000_000, 1_000_000, [*candidates, spread])
 
 
+def across(arrays):
+    return [swap(array, "blk", s) if s else array for s, array in zip(ORDER, arrays)]
+
+
 def swap(array, axis, by):
     return lax.ppermute(array, axis, [(i, i ^ by) for i in range(lax.axis_size(axis))])
 
@@ -447,12 +459,12 @@
     tokens_in, query_weight, key_weight, value_weight, conv_weight, prompt_lengths, decode_map
 ):
     width = tokens_in.shape[2]
+    given = (tokens_in, query_weight, key_weight, value_weight)
     length, slot = prompt_lengths.reshape(1, 1), decode_map.reshape(1, 1)
-    given = (tokens_in, query_weight, key_weight, value_weight)
     *parts, early = project(0, *given)
-    sent = [[parts[0]] + [swap(parts[s], "blk", s) for s in (1, 2, 3)]]
+    sent = [across(parts)]
     parts = project(1, *given, length, early)
-    sent.append([parts[0]] + [swap(parts[s], "blk", s) for s in (1, 2, 3)])
+    sent.append(across(parts))
     *first, taps = group_state(0, length, sent[0], conv_weight, [])
     second = group_state(1, length, sent[1], taps, [first[2]])
     got = [swap(held[2], "blk", GROUP) for held in (first, second)]
@@ -462,9 +474,9 @@
     aug, qk, own = second
     num = local_part(aug, qk, 5_000_000_000, [early[4]])
     *parts, total = finish(1, length, slot, num, own, got[1], qk, taps, [early[4], *early[:4]])
-    results = [parts[0]] + [swap(parts[s], "blk", s) for s in (1, 2, 3)]
-    beside = swap(total, "req", 2)
-    theirs = swap(hand_on(total, beside, results[1:2]), "req", 1)
+    results = across(parts)
+    beside = swap(total, "req", ROUTE[0])
+    theirs = swap(hand_on(total, beside, results[1:2]), "req", ROUTE[1])
     state, norm = expand_state([total, beside, theirs], width // lax.axis_size("blk"))
     mixed = place_tokens(results, [theirs])
     return (mixed, jnp.swapaxes(state, 0, 1), jnp.swapaxes(norm, 1, 2))

time: 39.1 us -> 37.6 us (0.962)
  waiting for transfers between devices: 5.16 us -> 3.81 us
    ppermute x13, waiting for transfers between devices: 5.16 us -> 3.81 us  [swap(): lax.ppermute(array, axis, [(i, i ^ by) for i in range(lax.axis_size(axis))])]
  transfers between devices with their start and end apart: 13 -> 13, of which waited for: 5 -> 4; matrix products, arithmetic and copies ran while one was open for 0% -> 0% of each run, Pallas kernels for 20% -> 21%
where the time goes in v3:
time: 37.6 us; the launch traced here: 37.4 us
  starting transfers between devices  18.7 us (50%)
  Pallas kernels  12.7 us (34%)
  waiting for transfers between devices  3.81 us (10%)
  between operations  2.1 us (6%)
    ppermute x13, starting transfers between devices, swap(): lax.ppermute(array, axis, [(i, i ^ by) for i in range(lax.axis_size(axis))])  18.7 us
    pallas_call x11, Pallas kernels, call(): pl.pallas_call(kernel, out_shape=[jax.ShapeDtypeStruct(shape, dtype) for...  12.7 us
    ppermute x13, waiting for transfers between devices, swap(): lax.ppermute(array, axis, [(i, i ^ by) for i in range(lax.axis_size(axis))])  3.81 us
  transfers between devices with their start and end apart: 13, of which 4 were waited for; matrix products, arithmetic and copies ran while one was open for 0% of the time, Pallas kernels for 21%

profile of v3, /device:TPU:0, one launch (start us, length us, event | category | flops | bytes accessed | tf_op | source)
XLA Modules:
  0.0 37.4 jit_solution(15481312475687907717)
XLA Ops:
  0.7 3.0 %shard_map.103 = (bf16[288,128]{1,0:T(8,128)(2,1)S(1)}, bf16[288,128]{1,0:T(8,128)(2,1)S(1)}, bf16[288,128]{1,0:T(8,128)(2,1)S(1)}, bf16[288,128]{1,0:T(8,128)(2,1)S(1)}, bf16[128,128]{1,0:T(8,128)(2,1)S(1)}) custom-call(bf16[1,128,1792]{2,1,0:T(8,128)(2,1)} %refs_0_.3, bf16[1792,256]{1,0:T(8,128)(2,1)} %refs_1_.3, bf16[1792,256]{1,0:T(8,128)(2,1)} %refs_2_.3, ...), custom_call_target="tpu_custom_call" | custom-call | flops 528482304 | bytes 4128768 | tf_op jit(solution)/shard_map/pallas_call | solution.py:52
  3.7 4.1 %collective-permute-start.3 = (bf16[288,128]{1,0:T(8,128)(2,1)S(1)}, bf16[288,128]{1,0:T(8,128)(2,1)S(1)}, u32[]{:S(2)}, u32[]{:S(2)}) collective-permute-start(bf16[288,128]{1,0:T(8,128)(2,1)S(1)} %get-tuple-element.37), channel_id=1, source_target_pairs={{0,12},{4,8},{8,4},{12,0},{16,28},{20,24},{24,20},{28,16},{1,13},{... | collective-permute-start | bytes 221192 | tf_op jit(solution)/shard_map/ppermute | solution.py:455
  7.8 0.4 %collective-permute-start.4 = (bf16[288,128]{1,0:T(8,128)(2,1)S(1)}, bf16[288,128]{1,0:T(8,128)(2,1)S(1)}, u32[]{:S(2)}, u32[]{:S(2)}) collective-permute-start(bf16[288,128]{1,0:T(8,128)(2,1)S(1)} %get-tuple-element.38), channel_id=1, source_target_pairs={{0,8},{4,12},{8,0},{12,4},{16,24},{20,28},{24,16},{28,20},{1,9},{5... | collective-permute-start | bytes 221192 | tf_op jit(solution)/shard_map/ppermute | solution.py:455
  9.1 2.5 %shard_map.104 = (bf16[320,128]{1,0:T(8,128)(2,1)S(1)}, bf16[320,128]{1,0:T(8,128)(2,1)S(1)}, bf16[320,128]{1,0:T(8,128)(2,1)S(1)}, bf16[320,128]{1,0:T(8,128)(2,1)S(1)}) custom-call(bf16[1,128,1792]{2,1,0:T(8,128)(2,1)S(1)} %copy-done.3, bf16[1792,256]{1,0:T(8,128)(2,1)S(1)} %copy-done.1, bf16[1792,256]{1,0:T(8,128)(2,1)S(1)} %copy-done.2, ...), custom_call_target="tpu_custom_call" | custom-call | flops 528482304 | bytes 4128768 | tf_op jit(solution)/shard_map/pallas_call | solution.py:52
  11.6 2.9 %collective-permute-start = (bf16[320,128]{1,0:T(8,128)(2,1)S(1)}, bf16[320,128]{1,0:T(8,128)(2,1)S(1)}, u32[]{:S(2)}, u32[]{:S(2)}) collective-permute-start(bf16[320,128]{1,0:T(8,128)(2,1)S(1)} %get-tuple-element.33), channel_id=1, source_target_pairs={{0,12},{4,8},{8,4},{12,0},{16,28},{20,24},{24,20},{28,16},{1,13},{... | collective-permute-start | bytes 245768 | tf_op jit(solution)/shard_map/ppermute | solution.py:455
  14.5 0.4 %collective-permute-start.1 = (bf16[320,128]{1,0:T(8,128)(2,1)S(1)}, bf16[320,128]{1,0:T(8,128)(2,1)S(1)}, u32[]{:S(2)}, u32[]{:S(2)}) collective-permute-start(bf16[320,128]{1,0:T(8,128)(2,1)S(1)} %get-tuple-element.34), channel_id=1, source_target_pairs={{0,8},{4,12},{8,0},{12,4},{16,24},{20,28},{24,16},{28,20},{1,9},{5... | collective-permute-start | bytes 245768 | tf_op jit(solution)/shard_map/ppermute | solution.py:455
  15.0 0.2 collective-permute-start.2
  15.2 0.8 %shard_map.105 = (bf16[2,128,512]{2,1,0:T(8,128)(2,1)S(1)}, bf16[64,512]{1,0:T(8,128)(2,1)S(1)}, bf16[320,128]{1,0:T(8,128)(2,1)S(1)}, f32[448,8]{1,0:T(8,128)S(1)}) custom-call(s32[1,1]{1,0:T(1,128)} %bitcast.5.refs_0_, bf16[288,128]{1,0:T(8,128)(2,1)S(1)} %get-tuple-element.36.refs_1_, bf16[288,128]{1,0:T(8,128)(2,1)S(1)} %collective-permute-done.3.refs_2_, ...), custom_call_target="tpu_custom_call" | custom-call | flops 100000000 | bytes 1000000 | tf_op jit(solution)/shard_map/pallas_call | solution.py:52
  16.0 3.0 %collective-permute-start.6 = (bf16[320,128]{1,0:T(8,128)(2,1)S(1)}, bf16[320,128]{1,0:T(8,128)(2,1)S(1)}, u32[]{:S(2)}, u32[]{:S(2)}) collective-permute-start(bf16[320,128]{1,0:T(8,128)(2,1)S(1)} %get-tuple-element.41.refs_6_.refs_3_), channel_id=1, source_target_pairs={{0,16},{4,20},{8,24},{12,28},{16,0},{20,4},{24,8},{28,12},{1,17},{... | collective-permute-start | bytes 245768 | tf_op jit(solution)/shard_map/ppermute | solution.py:455
  19.7 0.6 %shard_map.106 = (bf16[2,128,512]{2,1,0:T(8,128)(2,1)S(1)}, bf16[64,512]{1,0:T(8,128)(2,1)S(1)}, bf16[352,128]{1,0:T(8,128)(2,1)S(1)}) custom-call(s32[1,1]{1,0:T(1,128)} %bitcast.6.refs_0_, bf16[320,128]{1,0:T(8,128)(2,1)S(1)} %get-tuple-element.32.refs_1_, bf16[320,128]{1,0:T(8,128)(2,1)S(1)} %collective-permute-done.refs_2_, ...), custom_call_target="tpu_custom_call" | custom-call | flops 100000000 | bytes 1000000 | tf_op jit(solution)/shard_map/pallas_call | solution.py:52
  20.3 2.4 %collective-permute-start.7 = (bf16[352,128]{1,0:T(8,128)(2,1)S(1)}, bf16[352,128]{1,0:T(8,128)(2,1)S(1)}, u32[]{:S(2)}, u32[]{:S(2)}) collective-permute-start(bf16[352,128]{1,0:T(8,128)(2,1)S(1)} %get-tuple-element.46.refs_2_.refs_3_), channel_id=1, source_target_pairs={{0,16},{4,20},{8,24},{12,28},{16,0},{20,4},{24,8},{28,12},{1,17},{... | collective-permute-start | bytes 270344 | tf_op jit(solution)/shard_map/ppermute | solution.py:455
  22.7 0.9 %shard_map.107.refs_2_ = f32[2,128,512]{2,1,0:T(8,128)S(1)} custom-call(bf16[2,128,512]{2,1,0:T(8,128)(2,1)S(1)} %get-tuple-element.44.refs_0_, bf16[64,512]{1,0:T(8,128)(2,1)S(1)} %get-tuple-element.45.refs_1_.refs_5_, bf16[352,128]{1,0:T(8,128)(2,1)S(1)} %get-tuple-element.46.refs_2_.refs_3_), custom_call_target="tpu_custom_call" | custom-call | flops 1000 | bytes 1000 | tf_op jit(solution)/shard_map/pallas_call | solution.py:52
  23.6 0.8 %shard_map.108 = (bf16[224,128]{1,0:T(8,128)(2,1)S(1)}, bf16[224,128]{1,0:T(8,128)(2,1)S(1)}, bf16[224,128]{1,0:T(8,128)(2,1)S(1)}, bf16[224,128]{1,0:T(8,128)(2,1)S(1)}, bf16[320,128]{1,0:T(8,128)(2,1)S(1)}) custom-call(s32[1,1]{1,0:T(1,128)} %bitcast.7.refs_0_, s32[1,1]{1,0:T(1,128)} %bitcast.9.refs_1_, f32[2,128,512]{2,1,0:T(8,128)S(1)} %shard_map.107.refs_2_, ...), custom_call_target="tpu_custom_call" | custom-call | flops 50000000 | bytes 20000000 | tf_op jit(solution)/shard_map/pallas_call | solution.py:52
  24.4 0.9 %shard_map.109.refs_2_ = f32[2,128,512]{2,1,0:T(8,128)S(1)} custom-call(bf16[2,128,512]{2,1,0:T(8,128)(2,1)S(1)} %get-tuple-element.42.refs_0_, bf16[64,512]{1,0:T(8,128)(2,1)S(1)} %get-tuple-element.43.refs_1_.refs_5_, bf16[320,128]{1,0:T(8,128)(2,1)S(1)} %get-tuple-element.47.refs_2_.refs_7_), custom_call_target="tpu_custom_call" | custom-call | flops 5000000000 | bytes 1000 | tf_op jit(solution)/shard_map/pallas_call | solution.py:52
  25.4 0.4 %collective-permute-done.7.refs_4_ = bf16[352,128]{1,0:T(8,128)(2,1)S(1)} collective-permute-done((bf16[352,128]{1,0:T(8,128)(2,1)S(1)}, bf16[352,128]{1,0:T(8,128)(2,1)S(1)}, u32[]{:S(2)}, u32[]{:S(2)}) %collective-permute-start.7) | collective-permute-done | bytes 90144 | tf_op jit(solution)/shard_map/ppermute | solution.py:455
  25.8 1.0 %shard_map.110 = (bf16[448,128]{1,0:T(8,128)(2,1)S(1)}, bf16[448,128]{1,0:T(8,128)(2,1)S(1)}, bf16[448,128]{1,0:T(8,128)(2,1)S(1)}, bf16[448,128]{1,0:T(8,128)(2,1)S(1)}, bf16[352,128]{1,0:T(8,128)(2,1)S(1)}) custom-call(s32[1,1]{1,0:T(1,128)} %bitcast.8.refs_0_, s32[1,1]{1,0:T(1,128)} %bitcast.10.refs_1_, f32[2,128,512]{2,1,0:T(8,128)S(1)} %shard_map.109.refs_2_, ...), custom_call_target="tpu_custom_call" | custom-call | flops 50000000 | bytes 20000000 | tf_op jit(solution)/shard_map/pallas_call | solution.py:52
  26.8 2.5 %collective-permute-start.8 = (bf16[448,128]{1,0:T(8,128)(2,1)S(1)}, bf16[448,128]{1,0:T(8,128)(2,1)S(1)}, u32[]{:S(2)}, u32[]{:S(2)}) collective-permute-start(bf16[448,128]{1,0:T(8,128)(2,1)S(1)} %get-tuple-element.53), channel_id=1, source_target_pairs={{0,12},{4,8},{8,4},{12,0},{16,28},{20,24},{24,20},{28,16},{1,13},{... | collective-permute-start | bytes 344072 | tf_op jit(solution)/shard_map/ppermute | solution.py:455
  29.3 1.5 %collective-permute-start.11 = (bf16[352,128]{1,0:T(8,128)(2,1)S(1)}, bf16[352,128]{1,0:T(8,128)(2,1)S(1)}, u32[]{:S(2)}, u32[]{:S(2)}) collective-permute-start(bf16[352,128]{1,0:T(8,128)(2,1)S(1)} %get-tuple-element.56.refs_0_.c0), channel_id=1, source_target_pairs={{0,2},{1,3},{2,0},{3,1},{4,6},{5,7},{6,4},{7,5},{8,10},{9,11},{10,... | collective-permute-start | bytes 270344 | tf_op jit(solution)/shard_map/ppermute | solution.py:455
  30.8 0.4 %collective-permute-start.9 = (bf16[448,128]{1,0:T(8,128)(2,1)S(1)}, bf16[448,128]{1,0:T(8,128)(2,1)S(1)}, u32[]{:S(2)}, u32[]{:S(2)}) collective-permute-start(bf16[448,128]{1,0:T(8,128)(2,1)S(1)} %get-tuple-element.54), channel_id=1, source_target_pairs={{0,8},{4,12},{8,0},{12,4},{16,24},{20,28},{24,16},{28,20},{1,9},{5... | collective-permute-start | bytes 344072 | tf_op jit(solution)/shard_map/ppermute | solution.py:455
  31.2 0.6 %collective-permute-start.10 = (bf16[448,128]{1,0:T(8,128)(2,1)S(1)}, bf16[448,128]{1,0:T(8,128)(2,1)S(1)}, u32[]{:S(2)}, u32[]{:S(2)}) collective-permute-start(bf16[448,128]{1,0:T(8,128)(2,1)S(1)} %get-tuple-element.55), channel_id=1, source_target_pairs={{0,4},{4,0},{8,12},{12,8},{16,20},{20,16},{24,28},{28,24},{1,5},{5... | collective-permute-start | bytes 344072 | tf_op jit(solution)/shard_map/ppermute | solution.py:455
  31.9 1.9 %collective-permute-done.11.refs_1_.c1 = bf16[352,128]{1,0:T(8,128)(2,1)S(1)} collective-permute-done((bf16[352,128]{1,0:T(8,128)(2,1)S(1)}, bf16[352,128]{1,0:T(8,128)(2,1)S(1)}, u32[]{:S(2)}, u32[]{:S(2)}) %collective-permute-start.11) | collective-permute-done | bytes 90144 | tf_op jit(solution)/shard_map/ppermute | solution.py:455
  34.0 1.3 %collective-permute-done.12.refs_4_.c2 = bf16[352,128]{1,0:T(8,128)(2,1)S(1)} collective-permute-done((bf16[352,128]{1,0:T(8,128)(2,1)S(1)}, bf16[352,128]{1,0:T(8,128)(2,1)S(1)}, u32[]{:S(2)}, u32[]{:S(2)}) %collective-permute-start.12) | collective-permute-done | bytes 90144 | tf_op jit(solution)/shard_map/ppermute | solution.py:455
  35.3 1.1 %shard_map.113 = (f32[273,1,224]{2,1,0:T(1,128)}, f32[1,16,273]{2,1,0:T(8,128)}) custom-call(bf16[352,128]{1,0:T(8,128)(2,1)S(1)} %get-tuple-element.56.refs_0_.c0, bf16[352,128]{1,0:T(8,128)(2,1)S(1)} %collective-permute-done.11.refs_1_.c1, bf16[352,128]{1,0:T(8,128)(2,1)S(1)} %collective-permute-done.12.refs_4_.c2, bf16[273,160]{1,0:T(8,128)(2,1)S(1)} %copy-done.4), custom_call_target="tpu_custom_call" | custom-call | flops 40000000 | bytes 1000000 | tf_op jit(solution)/shard_map/pallas_call | solution.py:52
  36.4 1.0 %shard_map.112 = bf16[1,128,1792]{2,1,0:T(8,128)(2,1)} custom-call(bf16[448,128]{1,0:T(8,128)(2,1)S(1)} %get-tuple-element.52.refs_0_, bf16[448,128]{1,0:T(8,128)(2,1)S(1)} %collective-permute-done.8.refs_2_.refs_1_, bf16[448,128]{1,0:T(8,128)(2,1)S(1)} %collective-permute-done.9.refs_2_, bf16[448,128]{1,0:T(8,128)(2,1)S(1)} %collective-permute-done.10.refs_3_, ...), custom_call_target="tpu_custom_call" | custom-call | flops 1000 | bytes 1000000 | tf_op jit(solution)/shard_map/pallas_call | solution.py:52
  (25 shorter events, 0.5 us)
Async XLA Ops:
  0.6 8.5 %copy-start = (bf16[1792,1792]{1,0:T(8,128)(2,1)S(1)}, bf16[1792,1792]{1,0:T(8,128)(2,1)}, u32[]{:S(2)}) copy-start(bf16[1792,1792]{1,0:T(8,128)(2,1)} %refs_3_.3) | copy-start | bytes 19267588
  0.6 8.5 %copy-start.2 = (bf16[1792,256]{1,0:T(8,128)(2,1)S(1)}, bf16[1792,256]{1,0:T(8,128)(2,1)}, u32[]{:S(2)}) copy-start(bf16[1792,256]{1,0:T(8,128)(2,1)} %refs_2_.3) | copy-start | bytes 2752516
  0.7 8.5 %copy-start.1 = (bf16[1792,256]{1,0:T(8,128)(2,1)S(1)}, bf16[1792,256]{1,0:T(8,128)(2,1)}, u32[]{:S(2)}) copy-start(bf16[1792,256]{1,0:T(8,128)(2,1)} %refs_1_.3) | copy-start | bytes 2752516
  0.7 8.5 %copy-start.3 = (bf16[1,128,1792]{2,1,0:T(8,128)(2,1)S(1)}, bf16[1,128,1792]{2,1,0:T(8,128)(2,1)}, u32[]{:S(2)}) copy-start(bf16[1,128,1792]{2,1,0:T(8,128)(2,1)} %refs_0_.3) | copy-start | bytes 1376260
  3.7 11.5 %copy-start.5 = (f32[3,1792]{1,0:T(4,128)S(1)}, f32[3,1792]{1,0:T(4,128)}, u32[]{:S(2)}) copy-start(f32[3,1792]{1,0:T(4,128)} %refs_5_.1) | copy-start | bytes 64516
  3.7 11.2 %collective-permute-start.3 = (bf16[288,128]{1,0:T(8,128)(2,1)S(1)}, bf16[288,128]{1,0:T(8,128)(2,1)S(1)}, u32[]{:S(2)}, u32[]{:S(2)}) collective-permute-start(bf16[288,128]{1,0:T(8,128)(2,1)S(1)} %get-tuple-element.37), channel_id=1, source_target_pairs={{0,12},{4,8},{8,4},{12,0},{16,28},{20,24},{24,20},{28,16},{1,13},{... | collective-permute-start | bytes 221192 | tf_op jit(solution)/shard_map/ppermute | solution.py:455
  7.8 7.4 %collective-permute-start.4 = (bf16[288,128]{1,0:T(8,128)(2,1)S(1)}, bf16[288,128]{1,0:T(8,128)(2,1)S(1)}, u32[]{:S(2)}, u32[]{:S(2)}) collective-permute-start(bf16[288,128]{1,0:T(8,128)(2,1)S(1)} %get-tuple-element.38), channel_id=1, source_target_pairs={{0,8},{4,12},{8,0},{12,4},{16,24},{20,28},{24,16},{28,20},{1,9},{5... | collective-permute-start | bytes 221192 | tf_op jit(solution)/shard_map/ppermute | solution.py:455
  8.2 7.0 %collective-permute-start.5 = (bf16[288,128]{1,0:T(8,128)(2,1)S(1)}, bf16[288,128]{1,0:T(8,128)(2,1)S(1)}, u32[]{:S(2)}, u32[]{:S(2)}) collective-permute-start(bf16[288,128]{1,0:T(8,128)(2,1)S(1)} %get-tuple-element.39), channel_id=1, source_target_pairs={{0,4},{4,0},{8,12},{12,8},{16,20},{20,16},{24,28},{28,24},{1,5},{5... | collective-permute-start | bytes 221192 | tf_op jit(solution)/shard_map/ppermute | solution.py:455
  11.6 8.0 %collective-permute-start = (bf16[320,128]{1,0:T(8,128)(2,1)S(1)}, bf16[320,128]{1,0:T(8,128)(2,1)S(1)}, u32[]{:S(2)}, u32[]{:S(2)}) collective-permute-start(bf16[320,128]{1,0:T(8,128)(2,1)S(1)} %get-tuple-element.33), channel_id=1, source_target_pairs={{0,12},{4,8},{8,4},{12,0},{16,28},{20,24},{24,20},{28,16},{1,13},{... | collective-permute-start | bytes 245768 | tf_op jit(solution)/shard_map/ppermute | solution.py:455
  14.5 5.2 %collective-permute-start.1 = (bf16[320,128]{1,0:T(8,128)(2,1)S(1)}, bf16[320,128]{1,0:T(8,128)(2,1)S(1)}, u32[]{:S(2)}, u32[]{:S(2)}) collective-permute-start(bf16[320,128]{1,0:T(8,128)(2,1)S(1)} %get-tuple-element.34), channel_id=1, source_target_pairs={{0,8},{4,12},{8,0},{12,4},{16,24},{20,28},{24,16},{28,20},{1,9},{5... | collective-permute-start | bytes 245768 | tf_op jit(solution)/shard_map/ppermute | solution.py:455
  15.0 4.7 %collective-permute-start.2 = (bf16[320,128]{1,0:T(8,128)(2,1)S(1)}, bf16[320,128]{1,0:T(8,128)(2,1)S(1)}, u32[]{:S(2)}, u32[]{:S(2)}) collective-permute-start(bf16[320,128]{1,0:T(8,128)(2,1)S(1)} %get-tuple-element.35), channel_id=1, source_target_pairs={{0,4},{4,0},{8,12},{12,8},{16,20},{20,16},{24,28},{28,24},{1,5},{5... | collective-permute-start | bytes 245768 | tf_op jit(solution)/shard_map/ppermute | solution.py:455
  16.0 7.6 %collective-permute-start.6 = (bf16[320,128]{1,0:T(8,128)(2,1)S(1)}, bf16[320,128]{1,0:T(8,128)(2,1)S(1)}, u32[]{:S(2)}, u32[]{:S(2)}) collective-permute-start(bf16[320,128]{1,0:T(8,128)(2,1)S(1)} %get-tuple-element.41.refs_6_.refs_3_), channel_id=1, source_target_pairs={{0,16},{4,20},{8,24},{12,28},{16,0},{20,4},{24,8},{28,12},{1,17},{... | collective-permute-start | bytes 245768 | tf_op jit(solution)/shard_map/ppermute | solution.py:455
  20.3 5.5 %collective-permute-start.7 = (bf16[352,128]{1,0:T(8,128)(2,1)S(1)}, bf16[352,128]{1,0:T(8,128)(2,1)S(1)}, u32[]{:S(2)}, u32[]{:S(2)}) collective-permute-start(bf16[352,128]{1,0:T(8,128)(2,1)S(1)} %get-tuple-element.46.refs_2_.refs_3_), channel_id=1, source_target_pairs={{0,16},{4,20},{8,24},{12,28},{16,0},{20,4},{24,8},{28,12},{1,17},{... | collective-permute-start | bytes 270344 | tf_op jit(solution)/shard_map/ppermute | solution.py:455
  24.4 10.9 %copy-start.4 = (bf16[273,160]{1,0:T(8,128)(2,1)S(1)}, bf16[273,160]{1,0:T(8,128)(2,1)}, u32[]{:S(2)}) copy-start(bf16[273,160]{1,0:T(8,128)(2,1)} %constant.2.clone.spread) | copy-start | bytes 262084
  26.8 7.0 %collective-permute-start.8 = (bf16[448,128]{1,0:T(8,128)(2,1)S(1)}, bf16[448,128]{1,0:T(8,128)(2,1)S(1)}, u32[]{:S(2)}, u32[]{:S(2)}) collective-permute-start(bf16[448,128]{1,0:T(8,128)(2,1)S(1)} %get-tuple-element.53), channel_id=1, source_target_pairs={{0,12},{4,8},{8,4},{12,0},{16,28},{20,24},{24,20},{28,16},{1,13},{... | collective-permute-start | bytes 344072 | tf_op jit(solution)/shard_map/ppermute | solution.py:455
  29.3 4.5 %collective-permute-start.11 = (bf16[352,128]{1,0:T(8,128)(2,1)S(1)}, bf16[352,128]{1,0:T(8,128)(2,1)S(1)}, u32[]{:S(2)}, u32[]{:S(2)}) collective-permute-start(bf16[352,128]{1,0:T(8,128)(2,1)S(1)} %get-tuple-element.56.refs_0_.c0), channel_id=1, source_target_pairs={{0,2},{1,3},{2,0},{3,1},{4,6},{5,7},{6,4},{7,5},{8,10},{9,11},{10,... | collective-permute-start | bytes 270344 | tf_op jit(solution)/shard_map/ppermute | solution.py:455
  30.8 5.6 %collective-permute-start.9 = (bf16[448,128]{1,0:T(8,128)(2,1)S(1)}, bf16[448,128]{1,0:T(8,128)(2,1)S(1)}, u32[]{:S(2)}, u32[]{:S(2)}) collective-permute-start(bf16[448,128]{1,0:T(8,128)(2,1)S(1)} %get-tuple-element.54), channel_id=1, source_target_pairs={{0,8},{4,12},{8,0},{12,4},{16,24},{20,28},{24,16},{28,20},{1,9},{5... | collective-permute-start | bytes 344072 | tf_op jit(solution)/shard_map/ppermute | solution.py:455
  31.2 5.2 %collective-permute-start.10 = (bf16[448,128]{1,0:T(8,128)(2,1)S(1)}, bf16[448,128]{1,0:T(8,128)(2,1)S(1)}, u32[]{:S(2)}, u32[]{:S(2)}) collective-permute-start(bf16[448,128]{1,0:T(8,128)(2,1)S(1)} %get-tuple-element.55), channel_id=1, source_target_pairs={{0,4},{4,0},{8,12},{12,8},{16,20},{20,16},{24,28},{28,24},{1,5},{5... | collective-permute-start | bytes 344072 | tf_op jit(solution)/shard_map/ppermute | solution.py:455
  33.9 1.4 %collective-permute-start.12 = (bf16[352,128]{1,0:T(8,128)(2,1)S(1)}, bf16[352,128]{1,0:T(8,128)(2,1)S(1)}, u32[]{:S(2)}, u32[]{:S(2)}) collective-permute-start(bf16[352,128]{1,0:T(8,128)(2,1)S(1)} %shard_map.111), channel_id=1, source_target_pairs={{0,1},{1,0},{2,3},{3,2},{4,5},{5,4},{6,7},{7,6},{8,9},{9,8},{10,11... | collective-permute-start | bytes 270344 | tf_op jit(solution)/shard_map/ppermute | solution.py:455

commit v4 on v3

--- a/solution.py
+++ b/solution.py
@@ -16,7 +16,9 @@
 GROUP = 4
 SYM = 160
 LANES = 128
-INFO = 159
+REST = SYM - LANES
+EDGE, KEYS = 25, 27
+INFO = 31
 LOCAL = HEADS // GROUP // 2
 ORDER = (0, 3, 2, 1)
 f32 = jnp.float32
@@ -191,7 +193,7 @@
     if half:
         sums = p0[kept:, :].astype(f32) + p1[kept:, :].astype(f32)
         sums += p2[kept:, :].astype(f32) + p3[kept:, :].astype(f32)
-        state[LOCAL * SYM :, :] = sums.astype(bf16)
+        state[LOCAL * (size + REST) :, :] = sums.astype(bf16)
     for b in range(GROUP):
         qk[:, b * rows : (b + 1) * rows] = held[b, values:, :]
     alive = (group * tokens + iota((1, tokens), 1) < length[...]).astype(f32)
@@ -200,10 +202,11 @@
     marks = (row == 0) | ((row == 1) & (token == 0)) | ((row == 2) & (token == 1))
     marks = jnp.where(marks, alive, 0.0).astype(bf16)
     lane = iota((size, rows), 1)
-    last = iota((FEAT, rows), 0)
-    ends = iota((FEAT, rows), 1)
-    ends = ((last == 9) & (ends == rows - 1)) | ((last == 10) & (ends == rows - 2))
+    last = iota((REST, rows), 0)
+    ends = iota((REST, rows), 1)
+    ends = ((last == EDGE) & (ends == rows - 1)) | ((last == EDGE + 1) & (ends == rows - 2))
     ends = ends.astype(bf16)
+    step = size + REST
     for h in range(LOCAL):
         cut = slice(h * size, (h + 1) * size)
         first = (half * LOCAL + h) * size
@@ -223,10 +226,14 @@
         aug_h = jnp.concatenate([jnp.concatenate(pieces, 1), marks], 0)
         aug[h] = aug_h
         y = qk[h * FEAT : (h + 1) * FEAT, :].astype(f32) * FEAT ** (-0.25)
-        own = dot(symmetric(y, 1.0).astype(bf16), aug_h, NT)
+        feats = symmetric(y, 1.0).astype(bf16)
+        own = dot(aug_h, feats, NT)
+        keys = pltpu.roll(own[size : size + 8, :LANES], KEYS % 8, 0)
+        keys = jnp.concatenate([jnp.zeros((KEYS // 8 * 8, LANES), f32), keys], 0)
         edge = dot(ends, held[GROUP - 1, h * size : h * size + LANES, :], NT)
-        state[h * SYM : h * SYM + 144, :] = own[:144].astype(bf16)
-        state[h * SYM + 144 : (h + 1) * SYM, :] = (own[144:] + edge).astype(bf16)
+        rest = own[:, LANES:].T + edge + keys
+        state[h * step : h * step + size, :] = own[:size, :LANES].astype(bf16)
+        state[h * step + size : (h + 1) * step, :] = rest.astype(bf16)
 
 
 def group_state(half, length, payloads, taps, after):
@@ -236,7 +243,7 @@
     outs = [
         ((LOCAL, LANES, tokens), bf16),
         ((2 * LOCAL * FEAT, tokens), bf16),
-        ((LOCAL * SYM + extra, LANES), bf16),
+        (((total - extra) // LOCAL * LOCAL + extra, LANES), bf16),
     ]
     scratch = [pltpu.VMEM((GROUP, total - extra, rows), bf16)]
     if not half:
@@ -277,8 +284,10 @@
 
 
 def finish_kernel(half, *refs):
-    length, slot, num, own, got, qk, taps = refs[:7]
-    refs = refs[7:]
+    if half:
+        slot, *refs = refs
+    length, num, own, got, qk, taps = refs[:6]
+    refs = refs[6:]
     if half:
         other, *firsts = refs[:5]
         refs = refs[5:]
@@ -294,10 +303,17 @@
     alive = group * tokens + iota((1, tokens), 1) < length[...]
     first = (iota((size, LANES), 1) == 0) & upper
     aux = iota((LANES - size, SYM), 0)
+    step = size + REST
+
+    def whole(ref, h):
+        rest = ref[h * step + size : (h + 1) * step, :].astype(f32)
+        tail = [rest[KEYS : KEYS + 3], jnp.zeros((LANES - size - 3, LANES), f32)]
+        main = [ref[h * step : h * step + size, :].astype(f32), *tail]
+        return jnp.concatenate([jnp.concatenate(main, 0), rest.T], 1)
+
     finals = []
     for h in range(LOCAL):
-        here = own[h * SYM : (h + 1) * SYM, :].astype(f32).T
-        there = got[h * SYM : (h + 1) * SYM, :].astype(f32).T
+        here, there = whole(own, h), whole(got, h)
         low = jnp.where(upper, there, here)
         high = jnp.where(upper, here, there)
         at = (half * LOCAL + h) * size
@@ -328,19 +344,24 @@
         out[half * LOCAL * size :, :] = scr[mine ^ s]
     if not half:
         for c in range(LOCAL):
-            route[c * SYM : (c + 1) * SYM, :] = finals[c].T.astype(bf16)
+            route[c * step : c * step + size, :] = finals[c][:size, :LANES].astype(bf16)
+            route[c * step + size : (c + 1) * step, :] = finals[c][:, LANES:].T.astype(bf16)
         return
     count = length[...]
     for c in range(LOCAL):
-        final = jnp.where(upper, finals[c].T, other[c * SYM : (c + 1) * SYM, :].astype(f32))
+        cut = slice(c * step, c * step + size)
+        final = jnp.where(upper, finals[c][:size, :LANES], other[cut, :].astype(f32))
+        route[cut, :] = final.astype(bf16)
+        cut = slice(c * step + size, (c + 1) * step)
+        final = jnp.where(upper, finals[c][:, LANES:].T, other[cut, :].astype(f32))
         if c == 0:
             row, lane = iota(final.shape, 0), iota(final.shape, 1)
-            values = (slot[...], lax.shift_right_logical(count, 8), count & 255)
+            values = (slot[0], lax.shift_right_logical(count, 8), count & 255)
             for at, value in enumerate(values):
                 final = jnp.where((row == INFO) & (lane == at), value.astype(f32), final)
-        route[c * SYM : (c + 1) * SYM, :] = final.astype(bf16)
-    sums = own[LOCAL * SYM :, :].astype(f32) + got[LOCAL * SYM :, :].astype(f32)
-    route[LOCAL * SYM :, :] = sums.astype(bf16)
+        route[cut, :] = final.astype(bf16)
+    sums = own[LOCAL * step :, :].astype(f32) + got[LOCAL * step :, :].astype(f32)
+    route[LOCAL * step :, :] = sums.astype(bf16)
 
 
 def finish(half, length, slot, num, own, got, qk, taps, other):
@@ -349,12 +370,12 @@
     width = taps.shape[0] // 2
     outs = [(((1 + half) * width, rows), bf16)] * GROUP + [(own.shape, bf16)]
     scratch = [pltpu.VMEM((GROUP, width, rows), bf16)]
-    args = [length, slot, num, own, got, qk, taps] + other
+    args = [slot] * half + [length, num, own, got, qk, taps] + other
     kernel = functools.partial(finish_kernel, half)
-    return call(kernel, outs, scratch, 32, 50_000_000, 20_000_000, args)
-
-
-def place_kernel(r0, r1, r2, r3, mixed, scr):
+    return call(kernel, outs, scratch, 32, 50_000_000, 20_000_000, args, [pltpu.SMEM] * half)
+
+
+def place_kernel(r0, r1, r2, r3, mixed, scr, turned, sems):
     width = scr.shape[0]
     mine = lax.rem(lax.axis_index("blk"), GROUP)
     half = width // 2
@@ -363,17 +384,41 @@
         start = pl.multiple_of(slab * (mine ^ s), 32)
         scr[pl.ds(start, slab), :] = ref[0:slab, :]
         scr[pl.ds(pl.multiple_of(half + start, 32), slab), :] = ref[slab:, :]
+    copies = []
     for j in range(width // LANES):
         cut = slice(j * LANES, (j + 1) * LANES)
-        mixed[0, :, cut] = scr[cut, :].T
+        turned[:, cut] = scr[cut, :].T
+        if j % 2:
+            cut = pl.ds((j - 1) * LANES, 2 * LANES)
+            copies.append(
+                pltpu.make_async_copy(turned.at[:, cut], mixed.at[0, :, cut], sems.at[j // 2])
+            )
+            copies[-1].start()
+    for copy in copies:
+        copy.wait()
 
 
 def place_tokens(results, after):
     part, rows = results[0].shape
     width = part * GROUP
-    outs = [((1, rows, width), bf16)]
-    scratch = [pltpu.VMEM((width, rows), bf16)]
-    return call(place_kernel, outs, scratch, 32, 1000, 1_000_000, results, after=after)[0]
+
+    def kernel(*refs):
+        place_kernel(*refs[:GROUP], *refs[GROUP + len(after) :])
+
+    vmem, hbm = (pl.BlockSpec(memory_space=space) for space in (pltpu.VMEM, pl.ANY))
+    return pl.pallas_call(
+        kernel,
+        out_shape=jax.ShapeDtypeStruct((1, rows, width), bf16),
+        in_specs=[vmem] * GROUP + [hbm] * len(after),
+        out_specs=hbm,
+        scratch_shapes=[
+            pltpu.VMEM((width, rows), bf16),
+            pltpu.VMEM((rows, width), bf16),
+            pltpu.SemaphoreType.DMA((width // LANES // 2,)),
+        ],
+        compiler_params=pltpu.CompilerParams(vmem_limit_bytes=32 * 2**20),
+        cost_estimate=pl.CostEstimate(flops=1000, bytes_accessed=1_000_000, transcendentals=0),
+    )(*results, *after)
 
 
 ROUTE = (2, 1)
@@ -383,7 +428,8 @@
     other = (lax.axis_index("req") ^ ROUTE[1]).astype(f32)
     kept = jnp.zeros(out.shape, f32)
     for ref in (own, got):
-        here = ref[INFO : INFO + 1, 0:1].astype(f32) == other
+        at = (ref.shape[0] - 2 * FEAT) // LOCAL - REST + INFO
+        here = ref[at : at + 1, 0:1].astype(f32) == other
         kept += jnp.where(here, ref[...].astype(f32), 0.0)
     out[...] = kept.astype(bf16)
 
@@ -396,18 +442,22 @@
 def expand_kernel(c0, c1, c2, spread, state, norm):
     me = lax.axis_index("req").astype(f32)
     kept = jnp.zeros(c0.shape, f32)
+    step = (c0.shape[0] - 2 * FEAT) // LOCAL
+    at = step - REST + INFO
     for ref in (c0, c1, c2):
-        here = ref[INFO : INFO + 1, 0:1].astype(f32) == me
+        here = ref[at : at + 1, 0:1].astype(f32) == me
         kept += jnp.where(here, ref[...].astype(f32), 0.0)
     size = state.shape[2] // LOCAL
     expand = state.shape[0]
-    scale = jnp.where(iota((expand, LANES), 0) > FEAT, math.sqrt(0.5), 1.0)
+    scale = jnp.where(iota((expand, size), 0) > FEAT, math.sqrt(0.5), 1.0)
     wholes = []
     for c in range(LOCAL):
-        whole = dot(spread[...], kept[c * SYM : (c + 1) * SYM].astype(bf16)) * scale
-        wholes.append(whole[:, :size])
+        main = kept[c * step : c * step + size].astype(bf16)
+        rest = kept[c * step + size : (c + 1) * step].astype(bf16)
+        whole = dot(spread[:, :LANES], main, NT) + dot(spread[:, LANES:], rest)[:, :size]
+        wholes.append(whole * scale)
     state[...] = jnp.concatenate(wholes, 1).reshape(state.shape)
-    sums = kept[LOCAL * SYM :]
+    sums = kept[LOCAL * step :]
     keyed = HEADS * FEAT
     sums = jnp.concatenate([sums[:FEAT], sums[FEAT:]], 1)
     plain = jnp.concatenate([sums[9:], sums[:9]], 0) * FEAT ** (-0.25)
@@ -423,7 +473,7 @@
     gather = (iota((keyed, HEADS), 0) // FEAT == iota((keyed, HEADS), 1)).astype(bf16)
     rest = dot(big.astype(bf16), gather)
     rest = rest * jnp.where(iota(rest.shape, 0) >= FEAT, math.sqrt(0.5), 1.0)
-    info = kept[INFO : INFO + 1]
+    info = kept[at : at + 1]
     count = info[:, 1:2] * 256.0 + info[:, 2:3]
     norm[0] = jnp.concatenate([jnp.broadcast_to(count, (1, HEADS)), rest], 0).T
 
@@ -460,7 +510,7 @@
 ):
     width = tokens_in.shape[2]
     given = (tokens_in, query_weight, key_weight, value_weight)
-    length, slot = prompt_lengths.reshape(1, 1), decode_map.reshape(1, 1)
+    length, slot = prompt_lengths.reshape(1, 1), decode_map
     *parts, early = project(0, *given)
     sent = [across(parts)]
     parts = project(1, *given, length, early)
@@ -476,7 +526,7 @@
     *parts, total = finish(1, length, slot, num, own, got[1], qk, taps, [early[4], *early[:4]])
     results = across(parts)
     beside = swap(total, "req", ROUTE[0])
-    theirs = swap(hand_on(total, beside, results[1:2]), "req", ROUTE[1])
+    theirs = swap(hand_on(total, beside, []), "req", ROUTE[1])
     state, norm = expand_state([total, beside, theirs], width // lax.axis_size("blk"))
     mixed = place_tokens(results, [theirs])
     return (mixed, jnp.swapaxes(state, 0, 1), jnp.swapaxes(norm, 1, 2))

time: 37.6 us -> 36.8 us (0.979)
  waiting for transfers between devices: 3.81 us -> 3.39 us
    pallas_call x11 -> x10, Pallas kernels: 12.7 us -> 11.5 us  [call(): pl.pallas_call(kernel, out_shape=[jax.ShapeDtypeStruct(shape, dtype) for...]
    pallas_call x0 -> x1, Pallas kernels: none -> 0.93 us  [place_tokens(): pl.pallas_call(kernel, out_shape=jax.ShapeDtypeStruct((1, rows, width), b...]
    ppermute x13, waiting for transfers between devices: 3.81 us -> 3.39 us  [swap(): lax.ppermute(array, axis, [(i, i ^ by) for i in range(lax.axis_size(axis))])]
where the time goes in v4:
time: 36.8 us; the launch traced here: 36.6 us
  starting transfers between devices  18.7 us (51%)
  Pallas kernels  12.4 us (34%)
  waiting for transfers between devices  3.39 us (9%)
  between operations  2.11 us (6%)
    ppermute x13, starting transfers between devices, swap(): lax.ppermute(array, axis, [(i, i ^ by) for i in range(lax.axis_size(axis))])  18.7 us
    pallas_call x10, Pallas kernels, call(): pl.pallas_call(kernel, out_shape=[jax.ShapeDtypeStruct(shape, dtype) for...  11.5 us
    ppermute x13, waiting for transfers between devices, swap(): lax.ppermute(array, axis, [(i, i ^ by) for i in range(lax.axis_size(axis))])  3.39 us
    pallas_call x1, Pallas kernels, place_tokens(): pl.pallas_call(kernel, out_shape=jax.ShapeDtypeStruct((1, rows, width), b...  0.93 us
  transfers between devices with their start and end apart: 13, of which 4 were waited for; matrix products, arithmetic and copies ran while one was open for 0% of the time, Pallas kernels for 21%

profile of v4, /device:TPU:0, one launch (start us, length us, event | category | flops | bytes accessed | tf_op | source)
XLA Modules:
  0.0 36.6 jit_solution(7059432610787938703)
XLA Ops:
  0.7 3.0 %shard_map.103 = (bf16[288,128]{1,0:T(8,128)(2,1)S(1)}, bf16[288,128]{1,0:T(8,128)(2,1)S(1)}, bf16[288,128]{1,0:T(8,128)(2,1)S(1)}, bf16[288,128]{1,0:T(8,128)(2,1)S(1)}, bf16[128,128]{1,0:T(8,128)(2,1)S(1)}) custom-call(bf16[1,128,1792]{2,1,0:T(8,128)(2,1)} %refs_0_.4, bf16[1792,256]{1,0:T(8,128)(2,1)} %refs_1_.3, bf16[1792,256]{1,0:T(8,128)(2,1)} %refs_2_.3, ...), custom_call_target="tpu_custom_call" | custom-call | flops 528482304 | bytes 4128768 | tf_op jit(solution)/shard_map/pallas_call | solution.py:54
  3.7 4.1 %collective-permute-start.3 = (bf16[288,128]{1,0:T(8,128)(2,1)S(1)}, bf16[288,128]{1,0:T(8,128)(2,1)S(1)}, u32[]{:S(2)}, u32[]{:S(2)}) collective-permute-start(bf16[288,128]{1,0:T(8,128)(2,1)S(1)} %get-tuple-element.37), channel_id=1, source_target_pairs={{0,12},{4,8},{8,4},{12,0},{16,28},{20,24},{24,20},{28,16},{1,13},{... | collective-permute-start | bytes 221192 | tf_op jit(solution)/shard_map/ppermute | solution.py:505
  7.8 0.4 %collective-permute-start.4 = (bf16[288,128]{1,0:T(8,128)(2,1)S(1)}, bf16[288,128]{1,0:T(8,128)(2,1)S(1)}, u32[]{:S(2)}, u32[]{:S(2)}) collective-permute-start(bf16[288,128]{1,0:T(8,128)(2,1)S(1)} %get-tuple-element.38), channel_id=1, source_target_pairs={{0,8},{4,12},{8,0},{12,4},{16,24},{20,28},{24,16},{28,20},{1,9},{5... | collective-permute-start | bytes 221192 | tf_op jit(solution)/shard_map/ppermute | solution.py:505
  9.1 2.5 %shard_map.104 = (bf16[320,128]{1,0:T(8,128)(2,1)S(1)}, bf16[320,128]{1,0:T(8,128)(2,1)S(1)}, bf16[320,128]{1,0:T(8,128)(2,1)S(1)}, bf16[320,128]{1,0:T(8,128)(2,1)S(1)}) custom-call(bf16[1,128,1792]{2,1,0:T(8,128)(2,1)S(1)} %copy-done.3, bf16[1792,256]{1,0:T(8,128)(2,1)S(1)} %copy-done.1, bf16[1792,256]{1,0:T(8,128)(2,1)S(1)} %copy-done.2, ...), custom_call_target="tpu_custom_call" | custom-call | flops 528482304 | bytes 4128768 | tf_op jit(solution)/shard_map/pallas_call | solution.py:54
  11.6 2.9 %collective-permute-start = (bf16[320,128]{1,0:T(8,128)(2,1)S(1)}, bf16[320,128]{1,0:T(8,128)(2,1)S(1)}, u32[]{:S(2)}, u32[]{:S(2)}) collective-permute-start(bf16[320,128]{1,0:T(8,128)(2,1)S(1)} %get-tuple-element.33), channel_id=1, source_target_pairs={{0,12},{4,8},{8,4},{12,0},{16,28},{20,24},{24,20},{28,16},{1,13},{... | collective-permute-start | bytes 245768 | tf_op jit(solution)/shard_map/ppermute | solution.py:505
  14.5 0.4 %collective-permute-start.1 = (bf16[320,128]{1,0:T(8,128)(2,1)S(1)}, bf16[320,128]{1,0:T(8,128)(2,1)S(1)}, u32[]{:S(2)}, u32[]{:S(2)}) collective-permute-start(bf16[320,128]{1,0:T(8,128)(2,1)S(1)} %get-tuple-element.34), channel_id=1, source_target_pairs={{0,8},{4,12},{8,0},{12,4},{16,24},{20,28},{24,16},{28,20},{1,9},{5... | collective-permute-start | bytes 245768 | tf_op jit(solution)/shard_map/ppermute | solution.py:505
  15.2 0.8 %shard_map.105 = (bf16[2,128,512]{2,1,0:T(8,128)(2,1)S(1)}, bf16[64,512]{1,0:T(8,128)(2,1)S(1)}, bf16[288,128]{1,0:T(8,128)(2,1)S(1)}, f32[448,8]{1,0:T(8,128)S(1)}) custom-call(s32[1,1]{1,0:T(1,128)} %bitcast.4.refs_0_, bf16[288,128]{1,0:T(8,128)(2,1)S(1)} %get-tuple-element.36.refs_1_, bf16[288,128]{1,0:T(8,128)(2,1)S(1)} %collective-permute-done.3.refs_2_, ...), custom_call_target="tpu_custom_call" | custom-call | flops 100000000 | bytes 1000000 | tf_op jit(solution)/shard_map/pallas_call | solution.py:54
  16.0 3.0 %collective-permute-start.6 = (bf16[288,128]{1,0:T(8,128)(2,1)S(1)}, bf16[288,128]{1,0:T(8,128)(2,1)S(1)}, u32[]{:S(2)}, u32[]{:S(2)}) collective-permute-start(bf16[288,128]{1,0:T(8,128)(2,1)S(1)} %get-tuple-element.41.refs_6_.refs_2_), channel_id=1, source_target_pairs={{0,16},{4,20},{8,24},{12,28},{16,0},{20,4},{24,8},{28,12},{1,17},{... | collective-permute-start | bytes 221192 | tf_op jit(solution)/shard_map/ppermute | solution.py:505
  19.7 0.6 %shard_map.106 = (bf16[2,128,512]{2,1,0:T(8,128)(2,1)S(1)}, bf16[64,512]{1,0:T(8,128)(2,1)S(1)}, bf16[320,128]{1,0:T(8,128)(2,1)S(1)}) custom-call(s32[1,1]{1,0:T(1,128)} %bitcast.5.refs_0_, bf16[320,128]{1,0:T(8,128)(2,1)S(1)} %get-tuple-element.32.refs_1_, bf16[320,128]{1,0:T(8,128)(2,1)S(1)} %collective-permute-done.refs_2_, ...), custom_call_target="tpu_custom_call" | custom-call | flops 100000000 | bytes 1000000 | tf_op jit(solution)/shard_map/pallas_call | solution.py:54
  20.3 2.4 %collective-permute-start.7 = (bf16[320,128]{1,0:T(8,128)(2,1)S(1)}, bf16[320,128]{1,0:T(8,128)(2,1)S(1)}, u32[]{:S(2)}, u32[]{:S(2)}) collective-permute-start(bf16[320,128]{1,0:T(8,128)(2,1)S(1)} %get-tuple-element.46.refs_2_.refs_3_), channel_id=1, source_target_pairs={{0,16},{4,20},{8,24},{12,28},{16,0},{20,4},{24,8},{28,12},{1,17},{... | collective-permute-start | bytes 245768 | tf_op jit(solution)/shard_map/ppermute | solution.py:505
  22.6 0.9 %shard_map.107.refs_1_ = f32[2,128,512]{2,1,0:T(8,128)S(1)} custom-call(bf16[2,128,512]{2,1,0:T(8,128)(2,1)S(1)} %get-tuple-element.44.refs_0_, bf16[64,512]{1,0:T(8,128)(2,1)S(1)} %get-tuple-element.45.refs_1_.refs_4_, bf16[320,128]{1,0:T(8,128)(2,1)S(1)} %get-tuple-element.46.refs_2_.refs_3_), custom_call_target="tpu_custom_call" | custom-call | flops 1000 | bytes 1000 | tf_op jit(solution)/shard_map/pallas_call | solution.py:54
  23.6 0.7 %shard_map.108 = (bf16[224,128]{1,0:T(8,128)(2,1)S(1)}, bf16[224,128]{1,0:T(8,128)(2,1)S(1)}, bf16[224,128]{1,0:T(8,128)(2,1)S(1)}, bf16[224,128]{1,0:T(8,128)(2,1)S(1)}, bf16[288,128]{1,0:T(8,128)(2,1)S(1)}) custom-call(s32[1,1]{1,0:T(1,128)} %bitcast.6.refs_0_, f32[2,128,512]{2,1,0:T(8,128)S(1)} %shard_map.107.refs_1_, ...), custom_call_target="tpu_custom_call" | custom-call | flops 50000000 | bytes 20000000 | tf_op jit(solution)/shard_map/pallas_call | solution.py:54
  24.3 0.9 %shard_map.109.refs_2_ = f32[2,128,512]{2,1,0:T(8,128)S(1)} custom-call(bf16[2,128,512]{2,1,0:T(8,128)(2,1)S(1)} %get-tuple-element.42.refs_0_, bf16[64,512]{1,0:T(8,128)(2,1)S(1)} %get-tuple-element.43.refs_1_.refs_5_, bf16[288,128]{1,0:T(8,128)(2,1)S(1)} %get-tuple-element.47.refs_2_.refs_7_), custom_call_target="tpu_custom_call" | custom-call | flops 5000000000 | bytes 1000 | tf_op jit(solution)/shard_map/pallas_call | solution.py:54
  25.3 0.4 %collective-permute-done.7.refs_4_ = bf16[320,128]{1,0:T(8,128)(2,1)S(1)} collective-permute-done((bf16[320,128]{1,0:T(8,128)(2,1)S(1)}, bf16[320,128]{1,0:T(8,128)(2,1)S(1)}, u32[]{:S(2)}, u32[]{:S(2)}) %collective-permute-start.7) | collective-permute-done | bytes 81952 | tf_op jit(solution)/shard_map/ppermute | solution.py:505
  25.7 0.7 %shard_map.110 = (bf16[448,128]{1,0:T(8,128)(2,1)S(1)}, bf16[448,128]{1,0:T(8,128)(2,1)S(1)}, bf16[448,128]{1,0:T(8,128)(2,1)S(1)}, bf16[448,128]{1,0:T(8,128)(2,1)S(1)}, bf16[320,128]{1,0:T(8,128)(2,1)S(1)}) custom-call(s32[1]{0:T(128)S(6)} %copy.12.refs_0_, s32[1,1]{1,0:T(1,128)} %bitcast.7.refs_1_, f32[2,128,512]{2,1,0:T(8,128)S(1)} %shard_map.109.refs_2_, ...), custom_call_target="tpu_custom_call" | custom-call | flops 50000000 | bytes 20000000 | tf_op jit(solution)/shard_map/pallas_call | solution.py:54
  26.4 1.6 %collective-permute-start.11 = (bf16[320,128]{1,0:T(8,128)(2,1)S(1)}, bf16[320,128]{1,0:T(8,128)(2,1)S(1)}, u32[]{:S(2)}, u32[]{:S(2)}) collective-permute-start(bf16[320,128]{1,0:T(8,128)(2,1)S(1)} %get-tuple-element.56.own.c0), channel_id=1, source_target_pairs={{0,2},{1,3},{2,0},{3,1},{4,6},{5,7},{6,4},{7,5},{8,10},{9,11},{10,... | collective-permute-start | bytes 245768 | tf_op jit(solution)/shard_map/ppermute | solution.py:505
  28.0 2.5 %collective-permute-start.8 = (bf16[448,128]{1,0:T(8,128)(2,1)S(1)}, bf16[448,128]{1,0:T(8,128)(2,1)S(1)}, u32[]{:S(2)}, u32[]{:S(2)}) collective-permute-start(bf16[448,128]{1,0:T(8,128)(2,1)S(1)} %get-tuple-element.53), channel_id=1, source_target_pairs={{0,12},{4,8},{8,4},{12,0},{16,28},{20,24},{24,20},{28,16},{1,13},{... | collective-permute-start | bytes 344072 | tf_op jit(solution)/shard_map/ppermute | solution.py:505
  30.5 0.4 %collective-permute-start.9 = (bf16[448,128]{1,0:T(8,128)(2,1)S(1)}, bf16[448,128]{1,0:T(8,128)(2,1)S(1)}, u32[]{:S(2)}, u32[]{:S(2)}) collective-permute-start(bf16[448,128]{1,0:T(8,128)(2,1)S(1)} %get-tuple-element.54), channel_id=1, source_target_pairs={{0,8},{4,12},{8,0},{12,4},{16,24},{20,28},{24,16},{28,20},{1,9},{5... | collective-permute-start | bytes 344072 | tf_op jit(solution)/shard_map/ppermute | solution.py:505
  30.9 0.5 %collective-permute-start.10 = (bf16[448,128]{1,0:T(8,128)(2,1)S(1)}, bf16[448,128]{1,0:T(8,128)(2,1)S(1)}, u32[]{:S(2)}, u32[]{:S(2)}) collective-permute-start(bf16[448,128]{1,0:T(8,128)(2,1)S(1)} %get-tuple-element.55), channel_id=1, source_target_pairs={{0,4},{4,0},{8,12},{12,8},{16,20},{20,16},{24,28},{28,24},{1,5},{5... | collective-permute-start | bytes 344072 | tf_op jit(solution)/shard_map/ppermute | solution.py:505
  31.6 1.3 %collective-permute-done.12.refs_4_.c2 = bf16[320,128]{1,0:T(8,128)(2,1)S(1)} collective-permute-done((bf16[320,128]{1,0:T(8,128)(2,1)S(1)}, bf16[320,128]{1,0:T(8,128)(2,1)S(1)}, u32[]{:S(2)}, u32[]{:S(2)}) %collective-permute-start.12) | collective-permute-done | bytes 81952 | tf_op jit(solution)/shard_map/ppermute | solution.py:505
  32.9 1.1 %shard_map.113 = (f32[273,1,224]{2,1,0:T(1,128)}, f32[1,16,273]{2,1,0:T(8,128)}) custom-call(bf16[320,128]{1,0:T(8,128)(2,1)S(1)} %get-tuple-element.56.own.c0, bf16[320,128]{1,0:T(8,128)(2,1)S(1)} %collective-permute-done.11.got.c1, bf16[320,128]{1,0:T(8,128)(2,1)S(1)} %collective-permute-done.12.refs_4_.c2, bf16[273,160]{1,0:T(8,128)(2,1)S(1)} %copy-done.4), custom_call_target="tpu_custom_call" | custom-call | flops 40000000 | bytes 1000000 | tf_op jit(solution)/shard_map/pallas_call | solution.py:54
  34.0 1.3 %collective-permute-done.9.refs_2_ = bf16[448,128]{1,0:T(8,128)(2,1)S(1)} collective-permute-done((bf16[448,128]{1,0:T(8,128)(2,1)S(1)}, bf16[448,128]{1,0:T(8,128)(2,1)S(1)}, u32[]{:S(2)}, u32[]{:S(2)}) %collective-permute-start.9) | collective-permute-done | bytes 114720 | tf_op jit(solution)/shard_map/ppermute | solution.py:505
  35.3 0.4 %collective-permute-done.10.refs_3_ = bf16[448,128]{1,0:T(8,128)(2,1)S(1)} collective-permute-done((bf16[448,128]{1,0:T(8,128)(2,1)S(1)}, bf16[448,128]{1,0:T(8,128)(2,1)S(1)}, u32[]{:S(2)}, u32[]{:S(2)}) %collective-permute-start.10) | collective-permute-done | bytes 114720 | tf_op jit(solution)/shard_map/ppermute | solution.py:505
  35.7 0.9 %shard_map.112 = bf16[1,128,1792]{2,1,0:T(8,128)(2,1)} custom-call(bf16[448,128]{1,0:T(8,128)(2,1)S(1)} %get-tuple-element.52.refs_0_, bf16[448,128]{1,0:T(8,128)(2,1)S(1)} %collective-permute-done.8.refs_1_, bf16[448,128]{1,0:T(8,128)(2,1)S(1)} %collective-permute-done.9.refs_2_, bf16[448,128]{1,0:T(8,128)(2,1)S(1)} %collective-permute-done.10.refs_3_, ...), custom_call_target="tpu_custom_call" | custom-call | flops 1000 | bytes 1000000 | tf_op jit(solution)/shard_map/pallas_call | solution.py:409
  (25 shorter events, 0.6 us)
Async XLA Ops:
  0.6 8.5 %copy-start = (bf16[1792,1792]{1,0:T(8,128)(2,1)S(1)}, bf16[1792,1792]{1,0:T(8,128)(2,1)}, u32[]{:S(2)}) copy-start(bf16[1792,1792]{1,0:T(8,128)(2,1)} %refs_3_.3) | copy-start | bytes 19267588
  0.6 8.5 %copy-start.2 = (bf16[1792,256]{1,0:T(8,128)(2,1)S(1)}, bf16[1792,256]{1,0:T(8,128)(2,1)}, u32[]{:S(2)}) copy-start(bf16[1792,256]{1,0:T(8,128)(2,1)} %refs_2_.3) | copy-start | bytes 2752516
  0.7 8.5 %copy-start.1 = (bf16[1792,256]{1,0:T(8,128)(2,1)S(1)}, bf16[1792,256]{1,0:T(8,128)(2,1)}, u32[]{:S(2)}) copy-start(bf16[1792,256]{1,0:T(8,128)(2,1)} %refs_1_.3) | copy-start | bytes 2752516
  0.7 8.5 %copy-start.3 = (bf16[1,128,1792]{2,1,0:T(8,128)(2,1)S(1)}, bf16[1,128,1792]{2,1,0:T(8,128)(2,1)}, u32[]{:S(2)}) copy-start(bf16[1,128,1792]{2,1,0:T(8,128)(2,1)} %refs_0_.4) | copy-start | bytes 1376260
  3.7 11.5 %copy-start.5 = (f32[3,1792]{1,0:T(4,128)S(1)}, f32[3,1792]{1,0:T(4,128)}, u32[]{:S(2)}) copy-start(f32[3,1792]{1,0:T(4,128)} %refs_5_.1) | copy-start | bytes 64516
  3.7 11.2 %collective-permute-start.3 = (bf16[288,128]{1,0:T(8,128)(2,1)S(1)}, bf16[288,128]{1,0:T(8,128)(2,1)S(1)}, u32[]{:S(2)}, u32[]{:S(2)}) collective-permute-start(bf16[288,128]{1,0:T(8,128)(2,1)S(1)} %get-tuple-element.37), channel_id=1, source_target_pairs={{0,12},{4,8},{8,4},{12,0},{16,28},{20,24},{24,20},{28,16},{1,13},{... | collective-permute-start | bytes 221192 | tf_op jit(solution)/shard_map/ppermute | solution.py:505
  7.8 7.4 %collective-permute-start.4 = (bf16[288,128]{1,0:T(8,128)(2,1)S(1)}, bf16[288,128]{1,0:T(8,128)(2,1)S(1)}, u32[]{:S(2)}, u32[]{:S(2)}) collective-permute-start(bf16[288,128]{1,0:T(8,128)(2,1)S(1)} %get-tuple-element.38), channel_id=1, source_target_pairs={{0,8},{4,12},{8,0},{12,4},{16,24},{20,28},{24,16},{28,20},{1,9},{5... | collective-permute-start | bytes 221192 | tf_op jit(solution)/shard_map/ppermute | solution.py:505
  8.2 7.0 %collective-permute-start.5 = (bf16[288,128]{1,0:T(8,128)(2,1)S(1)}, bf16[288,128]{1,0:T(8,128)(2,1)S(1)}, u32[]{:S(2)}, u32[]{:S(2)}) collective-permute-start(bf16[288,128]{1,0:T(8,128)(2,1)S(1)} %get-tuple-element.39), channel_id=1, source_target_pairs={{0,4},{4,0},{8,12},{12,8},{16,20},{20,16},{24,28},{28,24},{1,5},{5... | collective-permute-start | bytes 221192 | tf_op jit(solution)/shard_map/ppermute | solution.py:505
  11.6 8.0 %collective-permute-start = (bf16[320,128]{1,0:T(8,128)(2,1)S(1)}, bf16[320,128]{1,0:T(8,128)(2,1)S(1)}, u32[]{:S(2)}, u32[]{:S(2)}) collective-permute-start(bf16[320,128]{1,0:T(8,128)(2,1)S(1)} %get-tuple-element.33), channel_id=1, source_target_pairs={{0,12},{4,8},{8,4},{12,0},{16,28},{20,24},{24,20},{28,16},{1,13},{... | collective-permute-start | bytes 245768 | tf_op jit(solution)/shard_map/ppermute | solution.py:505
  14.5 5.2 %collective-permute-start.1 = (bf16[320,128]{1,0:T(8,128)(2,1)S(1)}, bf16[320,128]{1,0:T(8,128)(2,1)S(1)}, u32[]{:S(2)}, u32[]{:S(2)}) collective-permute-start(bf16[320,128]{1,0:T(8,128)(2,1)S(1)} %get-tuple-element.34), channel_id=1, source_target_pairs={{0,8},{4,12},{8,0},{12,4},{16,24},{20,28},{24,16},{28,20},{1,9},{5... | collective-permute-start | bytes 245768 | tf_op jit(solution)/shard_map/ppermute | solution.py:505
  15.0 4.7 %collective-permute-start.2 = (bf16[320,128]{1,0:T(8,128)(2,1)S(1)}, bf16[320,128]{1,0:T(8,128)(2,1)S(1)}, u32[]{:S(2)}, u32[]{:S(2)}) collective-permute-start(bf16[320,128]{1,0:T(8,128)(2,1)S(1)} %get-tuple-element.35), channel_id=1, source_target_pairs={{0,4},{4,0},{8,12},{12,8},{16,20},{20,16},{24,28},{28,24},{1,5},{5... | collective-permute-start | bytes 245768 | tf_op jit(solution)/shard_map/ppermute | solution.py:505
  16.0 7.5 %collective-permute-start.6 = (bf16[288,128]{1,0:T(8,128)(2,1)S(1)}, bf16[288,128]{1,0:T(8,128)(2,1)S(1)}, u32[]{:S(2)}, u32[]{:S(2)}) collective-permute-start(bf16[288,128]{1,0:T(8,128)(2,1)S(1)} %get-tuple-element.41.refs_6_.refs_2_), channel_id=1, source_target_pairs={{0,16},{4,20},{8,24},{12,28},{16,0},{20,4},{24,8},{28,12},{1,17},{... | collective-permute-start | bytes 221192 | tf_op jit(solution)/shard_map/ppermute | solution.py:505
  20.3 5.4 %collective-permute-start.7 = (bf16[320,128]{1,0:T(8,128)(2,1)S(1)}, bf16[320,128]{1,0:T(8,128)(2,1)S(1)}, u32[]{:S(2)}, u32[]{:S(2)}) collective-permute-start(bf16[320,128]{1,0:T(8,128)(2,1)S(1)} %get-tuple-element.46.refs_2_.refs_3_), channel_id=1, source_target_pairs={{0,16},{4,20},{8,24},{12,28},{16,0},{20,4},{24,8},{28,12},{1,17},{... | collective-permute-start | bytes 245768 | tf_op jit(solution)/shard_map/ppermute | solution.py:505
  24.3 8.6 %copy-start.4 = (bf16[273,160]{1,0:T(8,128)(2,1)S(1)}, bf16[273,160]{1,0:T(8,128)(2,1)}, u32[]{:S(2)}) copy-start(bf16[273,160]{1,0:T(8,128)(2,1)} %constant.2.clone.spread) | copy-start | bytes 262084
  26.4 5.1 %collective-permute-start.11 = (bf16[320,128]{1,0:T(8,128)(2,1)S(1)}, bf16[320,128]{1,0:T(8,128)(2,1)S(1)}, u32[]{:S(2)}, u32[]{:S(2)}) collective-permute-start(bf16[320,128]{1,0:T(8,128)(2,1)S(1)} %get-tuple-element.56.own.c0), channel_id=1, source_target_pairs={{0,2},{1,3},{2,0},{3,1},{4,6},{5,7},{6,4},{7,5},{8,10},{9,11},{10,... | collective-permute-start | bytes 245768 | tf_op jit(solution)/shard_map/ppermute | solution.py:505
  28.0 6.0 %collective-permute-start.8 = (bf16[448,128]{1,0:T(8,128)(2,1)S(1)}, bf16[448,128]{1,0:T(8,128)(2,1)S(1)}, u32[]{:S(2)}, u32[]{:S(2)}) collective-permute-start(bf16[448,128]{1,0:T(8,128)(2,1)S(1)} %get-tuple-element.53), channel_id=1, source_target_pairs={{0,12},{4,8},{8,4},{12,0},{16,28},{20,24},{24,20},{28,16},{1,13},{... | collective-permute-start | bytes 344072 | tf_op jit(solution)/shard_map/ppermute | solution.py:505
  30.5 4.8 %collective-permute-start.9 = (bf16[448,128]{1,0:T(8,128)(2,1)S(1)}, bf16[448,128]{1,0:T(8,128)(2,1)S(1)}, u32[]{:S(2)}, u32[]{:S(2)}) collective-permute-start(bf16[448,128]{1,0:T(8,128)(2,1)S(1)} %get-tuple-element.54), channel_id=1, source_target_pairs={{0,8},{4,12},{8,0},{12,4},{16,24},{20,28},{24,16},{28,20},{1,9},{5... | collective-permute-start | bytes 344072 | tf_op jit(solution)/shard_map/ppermute | solution.py:505
  30.9 4.8 %collective-permute-start.10 = (bf16[448,128]{1,0:T(8,128)(2,1)S(1)}, bf16[448,128]{1,0:T(8,128)(2,1)S(1)}, u32[]{:S(2)}, u32[]{:S(2)}) collective-permute-start(bf16[448,128]{1,0:T(8,128)(2,1)S(1)} %get-tuple-element.55), channel_id=1, source_target_pairs={{0,4},{4,0},{8,12},{12,8},{16,20},{20,16},{24,28},{28,24},{1,5},{5... | collective-permute-start | bytes 344072 | tf_op jit(solution)/shard_map/ppermute | solution.py:505
  31.6 1.3 %collective-permute-start.12 = (bf16[320,128]{1,0:T(8,128)(2,1)S(1)}, bf16[320,128]{1,0:T(8,128)(2,1)S(1)}, u32[]{:S(2)}, u32[]{:S(2)}) collective-permute-start(bf16[320,128]{1,0:T(8,128)(2,1)S(1)} %shard_map.111), channel_id=1, source_target_pairs={{0,1},{1,0},{2,3},{3,2},{4,5},{5,4},{6,7},{7,6},{8,9},{9,8},{10,11... | collective-permute-start | bytes 245768 | tf_op jit(solution)/shard_map/ppermute | solution.py:505

commit v5 on v4

--- a/solution.py
+++ b/solution.py
@@ -65,6 +65,7 @@
 
 
 TILES = (384, 512)
+TILES_B = (896,)
 
 
 def key_sums(keys):
@@ -88,34 +89,46 @@
     else:
         o0, o1, o2, o3, early = refs[:5]
         refs = refs[5:]
-    x_v, wqk_v, wv_v, vt, qkt, sems = refs[:6]
     rows = x.shape[1]
     width = wv.shape[1] // 2
     keyed = wq.shape[1] // 2
-    get_x = pltpu.make_async_copy(x.at[0], x_v, sems.at[0])
-    keyed_cut = pl.ds(half * keyed, keyed)
-    get_k = pltpu.make_async_copy(wk.at[:, keyed_cut], wqk_v.at[:, pl.ds(0, keyed)], sems.at[1])
-    get_q = pltpu.make_async_copy(wq.at[:, keyed_cut], wqk_v.at[:, pl.ds(keyed, keyed)], sems.at[2])
-    copies, at = [], 0
-    for j, tile in enumerate(TILES):
-        source = wv.at[:, pl.ds(half * width + at, tile)]
-        copies.append(pltpu.make_async_copy(source, wv_v.at[:, pl.ds(at, tile)], sems.at[3 + j]))
-        at += tile
-    for copy in (get_x, get_k, get_q, *copies):
-        copy.start()
     place = lax.axis_index("blk")
     mine = lax.rem(place, GROUP)
     slab = width // GROUP
-    get_x.wait()
-    get_k.wait()
-    get_q.wait()
-    inputs = x_v[...]
-    qkt[...] = dot(inputs, wqk_v[...]).T.astype(bf16)
-    at = 0
-    for tile, copy in zip(TILES, copies):
-        copy.wait()
-        vt[at : at + tile, :] = dot(inputs, wv_v[:, at : at + tile]).T.astype(bf16)
-        at += tile
+    if half:
+        vt, qkt = refs
+        inputs = x[0]
+        both = jnp.concatenate([wk[:, keyed:], wq[:, keyed:]], 1)
+        qkt[...] = dot(inputs, both).T.astype(bf16)
+        at = 0
+        for tile in TILES_B:
+            weights = wv[:, width + at : width + at + tile]
+            vt[at : at + tile, :] = dot(inputs, weights).T.astype(bf16)
+            at += tile
+    else:
+        vt, qkt, x_v, wqk_v, wv_v, sems = refs
+        first, second = pl.ds(0, keyed), pl.ds(keyed, keyed)
+        needed = [
+            pltpu.make_async_copy(x.at[0], x_v, sems.at[0]),
+            pltpu.make_async_copy(wk.at[:, first], wqk_v.at[:, first], sems.at[1]),
+            pltpu.make_async_copy(wq.at[:, first], wqk_v.at[:, second], sems.at[2]),
+        ]
+        copies, at = [], 0
+        for j, tile in enumerate(TILES):
+            cut = pl.ds(at, tile)
+            copies.append(pltpu.make_async_copy(wv.at[:, cut], wv_v.at[:, cut], sems.at[3 + j]))
+            at += tile
+        for copy in (*needed, *copies):
+            copy.start()
+        for copy in needed:
+            copy.wait()
+        inputs = x_v[...]
+        qkt[...] = dot(inputs, wqk_v[...]).T.astype(bf16)
+        at = 0
+        for tile, copy in zip(TILES, copies):
+            copy.wait()
+            vt[at : at + tile, :] = dot(inputs, wv_v[:, at : at + tile]).T.astype(bf16)
+            at += tile
     part = keyed // GROUP
     for s, out in zip(ORDER, (o0, o1, o2, o3)):
         dest = mine ^ s
@@ -138,21 +151,20 @@
     keyed = wq.shape[1]
     total = (width + 2 * keyed) // GROUP // 2 + (2 * FEAT if half else 0)
     outs = [((total, rows), bf16)] * GROUP
-    scratch = [
-        pltpu.VMEM((rows, width), bf16),
-        pltpu.VMEM((width, keyed), bf16),
-        pltpu.VMEM((width, width // 2), bf16),
-        pltpu.VMEM((width // 2, rows), bf16),
-        pltpu.VMEM((keyed, rows), bf16),
-        pltpu.SemaphoreType.DMA((3 + len(TILES),)),
-    ]
+    scratch = [pltpu.VMEM((width // 2, rows), bf16), pltpu.VMEM((keyed, rows), bf16)]
     if not half:
         outs.append(((keyed // 2, rows), bf16))
+        scratch += [
+            pltpu.VMEM((rows, width), bf16),
+            pltpu.VMEM((width, keyed), bf16),
+            pltpu.VMEM((width, width // 2), bf16),
+            pltpu.SemaphoreType.DMA((3 + len(TILES),)),
+        ]
     flops = rows * width * (width + 2 * keyed)
     kernel = functools.partial(project_kernel, half)
     limit = LIMIT_B if half else LIMIT_A
     args = [x, wq, wk, wv, *others]
-    return call(kernel, outs, scratch, limit, flops, flops // rows, args, [pltpu.HBM] * 4)
+    return call(kernel, outs, scratch, limit, flops, flops // rows, args, [] if half else [pltpu.HBM] * 4)
 
 
 LIMIT_A = 53.6
@@ -427,9 +439,9 @@
 def hand_on_kernel(own, got, out):
     other = (lax.axis_index("req") ^ ROUTE[1]).astype(f32)
     kept = jnp.zeros(out.shape, f32)
+    step = (own.shape[0] - 2 * FEAT) // LOCAL
     for ref in (own, got):
-        at = (ref.shape[0] - 2 * FEAT) // LOCAL - REST + INFO
-        here = ref[at : at + 1, 0:1].astype(f32) == other
+        here = ref[step - FEAT : step, :].astype(f32)[INFO % FEAT :, 0:1] == other
         kept += jnp.where(here, ref[...].astype(f32), 0.0)
     out[...] = kept.astype(bf16)
 
@@ -445,7 +457,7 @@
     step = (c0.shape[0] - 2 * FEAT) // LOCAL
     at = step - REST + INFO
     for ref in (c0, c1, c2):
-        here = ref[at : at + 1, 0:1].astype(f32) == me
+        here = ref[step - FEAT : step, :].astype(f32)[INFO % FEAT :, 0:1] == me
         kept += jnp.where(here, ref[...].astype(f32), 0.0)
     size = state.shape[2] // LOCAL
     expand = state.shape[0]

time: 36.8 us -> 35.3 us (0.959)
  Pallas kernels: 12.4 us -> 11 us
    pallas_call x10, Pallas kernels: 11.5 us -> 10 us  [call(): pl.pallas_call(kernel, out_shape=[jax.ShapeDtypeStruct(shape, dtype) for...]
  transfers between devices with their start and end apart: 13 -> 13, of which waited for: 4 -> 4; matrix products, arithmetic and copies ran while one was open for 0% -> 0% of each run, Pallas kernels for 21% -> 18%
where the time goes in v5:
time: 35.3 us; the launch traced here: 35.1 us
  starting transfers between devices  18.6 us (53%)
  Pallas kernels  11 us (31%)
  waiting for transfers between devices  3.41 us (10%)
  between operations  2.1 us (6%)
    ppermute x13, starting transfers between devices, swap(): lax.ppermute(array, axis, [(i, i ^ by) for i in range(lax.axis_size(axis))])  18.6 us
    pallas_call x10, Pallas kernels, call(): pl.pallas_call(kernel, out_shape=[jax.ShapeDtypeStruct(shape, dtype) for...  10 us
    ppermute x13, waiting for transfers between devices, swap(): lax.ppermute(array, axis, [(i, i ^ by) for i in range(lax.axis_size(axis))])  3.41 us
    pallas_call x1, Pallas kernels, place_tokens(): pl.pallas_call(kernel, out_shape=jax.ShapeDtypeStruct((1, rows, width), b...  0.93 us
  transfers between devices with their start and end apart: 13, of which 4 were waited for; matrix products, arithmetic and copies ran while one was open for 0% of the time, Pallas kernels for 18%

profile of v5, /device:TPU:0, one launch (start us, length us, event | category | flops | bytes accessed | tf_op | source)
XLA Modules:
  0.0 35.1 jit_solution(5387404781704007319)
XLA Ops:
  0.7 3.0 %shard_map.103 = (bf16[288,128]{1,0:T(8,128)(2,1)S(1)}, bf16[288,128]{1,0:T(8,128)(2,1)S(1)}, bf16[288,128]{1,0:T(8,128)(2,1)S(1)}, bf16[288,128]{1,0:T(8,128)(2,1)S(1)}, bf16[128,128]{1,0:T(8,128)(2,1)S(1)}) custom-call(bf16[1,128,1792]{2,1,0:T(8,128)(2,1)} %refs_0_.4, bf16[1792,256]{1,0:T(8,128)(2,1)} %refs_1_.3, bf16[1792,256]{1,0:T(8,128)(2,1)} %refs_2_.3, ...), custom_call_target="tpu_custom_call" | custom-call | flops 528482304 | bytes 4128768 | tf_op jit(solution)/shard_map/pallas_call | solution.py:54
  3.7 4.1 %collective-permute-start.3 = (bf16[288,128]{1,0:T(8,128)(2,1)S(1)}, bf16[288,128]{1,0:T(8,128)(2,1)S(1)}, u32[]{:S(2)}, u32[]{:S(2)}) collective-permute-start(bf16[288,128]{1,0:T(8,128)(2,1)S(1)} %get-tuple-element.37), channel_id=1, source_target_pairs={{0,12},{4,8},{8,4},{12,0},{16,28},{20,24},{24,20},{28,16},{1,13},{... | collective-permute-start | bytes 221192 | tf_op jit(solution)/shard_map/ppermute | solution.py:517
  7.8 0.4 %collective-permute-start.4 = (bf16[288,128]{1,0:T(8,128)(2,1)S(1)}, bf16[288,128]{1,0:T(8,128)(2,1)S(1)}, u32[]{:S(2)}, u32[]{:S(2)}) collective-permute-start(bf16[288,128]{1,0:T(8,128)(2,1)S(1)} %get-tuple-element.38), channel_id=1, source_target_pairs={{0,8},{4,12},{8,0},{12,4},{16,24},{20,28},{24,16},{28,20},{1,9},{5... | collective-permute-start | bytes 221192 | tf_op jit(solution)/shard_map/ppermute | solution.py:517
  9.1 1.1 %shard_map.104 = (bf16[320,128]{1,0:T(8,128)(2,1)S(1)}, bf16[320,128]{1,0:T(8,128)(2,1)S(1)}, bf16[320,128]{1,0:T(8,128)(2,1)S(1)}, bf16[320,128]{1,0:T(8,128)(2,1)S(1)}) custom-call(bf16[1,128,1792]{2,1,0:T(8,128)(2,1)S(1)} %copy-done.3, bf16[1792,256]{1,0:T(8,128)(2,1)S(1)} %copy-done.1, bf16[1792,256]{1,0:T(8,128)(2,1)S(1)} %copy-done.2, ...), custom_call_target="tpu_custom_call" | custom-call | flops 528482304 | bytes 4128768 | tf_op jit(solution)/shard_map/pallas_call | solution.py:54
  10.2 2.9 %collective-permute-start = (bf16[320,128]{1,0:T(8,128)(2,1)S(1)}, bf16[320,128]{1,0:T(8,128)(2,1)S(1)}, u32[]{:S(2)}, u32[]{:S(2)}) collective-permute-start(bf16[320,128]{1,0:T(8,128)(2,1)S(1)} %get-tuple-element.33), channel_id=1, source_target_pairs={{0,12},{4,8},{8,4},{12,0},{16,28},{20,24},{24,20},{28,16},{1,13},{... | collective-permute-start | bytes 245768 | tf_op jit(solution)/shard_map/ppermute | solution.py:517
  13.0 0.4 %collective-permute-start.1 = (bf16[320,128]{1,0:T(8,128)(2,1)S(1)}, bf16[320,128]{1,0:T(8,128)(2,1)S(1)}, u32[]{:S(2)}, u32[]{:S(2)}) collective-permute-start(bf16[320,128]{1,0:T(8,128)(2,1)S(1)} %get-tuple-element.34), channel_id=1, source_target_pairs={{0,8},{4,12},{8,0},{12,4},{16,24},{20,28},{24,16},{28,20},{1,9},{5... | collective-permute-start | bytes 245768 | tf_op jit(solution)/shard_map/ppermute | solution.py:517
  13.7 0.8 %shard_map.105 = (bf16[2,128,512]{2,1,0:T(8,128)(2,1)S(1)}, bf16[64,512]{1,0:T(8,128)(2,1)S(1)}, bf16[288,128]{1,0:T(8,128)(2,1)S(1)}, f32[448,8]{1,0:T(8,128)S(1)}) custom-call(s32[1,1]{1,0:T(1,128)} %bitcast.4.refs_0_, bf16[288,128]{1,0:T(8,128)(2,1)S(1)} %get-tuple-element.36.refs_1_, bf16[288,128]{1,0:T(8,128)(2,1)S(1)} %collective-permute-done.3.refs_2_, ...), custom_call_target="tpu_custom_call" | custom-call | flops 100000000 | bytes 1000000 | tf_op jit(solution)/shard_map/pallas_call | solution.py:54
  14.5 3.0 %collective-permute-start.6 = (bf16[288,128]{1,0:T(8,128)(2,1)S(1)}, bf16[288,128]{1,0:T(8,128)(2,1)S(1)}, u32[]{:S(2)}, u32[]{:S(2)}) collective-permute-start(bf16[288,128]{1,0:T(8,128)(2,1)S(1)} %get-tuple-element.41.refs_6_.refs_2_), channel_id=1, source_target_pairs={{0,16},{4,20},{8,24},{12,28},{16,0},{20,4},{24,8},{28,12},{1,17},{... | collective-permute-start | bytes 221192 | tf_op jit(solution)/shard_map/ppermute | solution.py:517
  18.2 0.6 %shard_map.106 = (bf16[2,128,512]{2,1,0:T(8,128)(2,1)S(1)}, bf16[64,512]{1,0:T(8,128)(2,1)S(1)}, bf16[320,128]{1,0:T(8,128)(2,1)S(1)}) custom-call(s32[1,1]{1,0:T(1,128)} %bitcast.5.refs_0_, bf16[320,128]{1,0:T(8,128)(2,1)S(1)} %get-tuple-element.32.refs_1_, bf16[320,128]{1,0:T(8,128)(2,1)S(1)} %collective-permute-done.refs_2_, ...), custom_call_target="tpu_custom_call" | custom-call | flops 100000000 | bytes 1000000 | tf_op jit(solution)/shard_map/pallas_call | solution.py:54
  18.8 2.4 %collective-permute-start.7 = (bf16[320,128]{1,0:T(8,128)(2,1)S(1)}, bf16[320,128]{1,0:T(8,128)(2,1)S(1)}, u32[]{:S(2)}, u32[]{:S(2)}) collective-permute-start(bf16[320,128]{1,0:T(8,128)(2,1)S(1)} %get-tuple-element.46.refs_2_.refs_3_), channel_id=1, source_target_pairs={{0,16},{4,20},{8,24},{12,28},{16,0},{20,4},{24,8},{28,12},{1,17},{... | collective-permute-start | bytes 245768 | tf_op jit(solution)/shard_map/ppermute | solution.py:517
  21.1 0.9 %shard_map.107.refs_1_ = f32[2,128,512]{2,1,0:T(8,128)S(1)} custom-call(bf16[2,128,512]{2,1,0:T(8,128)(2,1)S(1)} %get-tuple-element.44.refs_0_, bf16[64,512]{1,0:T(8,128)(2,1)S(1)} %get-tuple-element.45.refs_1_.refs_4_, bf16[320,128]{1,0:T(8,128)(2,1)S(1)} %get-tuple-element.46.refs_2_.refs_3_), custom_call_target="tpu_custom_call" | custom-call | flops 1000 | bytes 1000 | tf_op jit(solution)/shard_map/pallas_call | solution.py:54
  22.1 0.7 %shard_map.108 = (bf16[224,128]{1,0:T(8,128)(2,1)S(1)}, bf16[224,128]{1,0:T(8,128)(2,1)S(1)}, bf16[224,128]{1,0:T(8,128)(2,1)S(1)}, bf16[224,128]{1,0:T(8,128)(2,1)S(1)}, bf16[288,128]{1,0:T(8,128)(2,1)S(1)}) custom-call(s32[1,1]{1,0:T(1,128)} %bitcast.6.refs_0_, f32[2,128,512]{2,1,0:T(8,128)S(1)} %shard_map.107.refs_1_, ...), custom_call_target="tpu_custom_call" | custom-call | flops 50000000 | bytes 20000000 | tf_op jit(solution)/shard_map/pallas_call | solution.py:54
  22.8 0.9 %shard_map.109.refs_2_ = f32[2,128,512]{2,1,0:T(8,128)S(1)} custom-call(bf16[2,128,512]{2,1,0:T(8,128)(2,1)S(1)} %get-tuple-element.42.refs_0_, bf16[64,512]{1,0:T(8,128)(2,1)S(1)} %get-tuple-element.43.refs_1_.refs_5_, bf16[288,128]{1,0:T(8,128)(2,1)S(1)} %get-tuple-element.47.refs_2_.refs_7_), custom_call_target="tpu_custom_call" | custom-call | flops 5000000000 | bytes 1000 | tf_op jit(solution)/shard_map/pallas_call | solution.py:54
  23.8 0.4 %collective-permute-done.7.refs_4_ = bf16[320,128]{1,0:T(8,128)(2,1)S(1)} collective-permute-done((bf16[320,128]{1,0:T(8,128)(2,1)S(1)}, bf16[320,128]{1,0:T(8,128)(2,1)S(1)}, u32[]{:S(2)}, u32[]{:S(2)}) %collective-permute-start.7) | collective-permute-done | bytes 81952 | tf_op jit(solution)/shard_map/ppermute | solution.py:517
  24.2 0.7 %shard_map.110 = (bf16[448,128]{1,0:T(8,128)(2,1)S(1)}, bf16[448,128]{1,0:T(8,128)(2,1)S(1)}, bf16[448,128]{1,0:T(8,128)(2,1)S(1)}, bf16[448,128]{1,0:T(8,128)(2,1)S(1)}, bf16[320,128]{1,0:T(8,128)(2,1)S(1)}) custom-call(s32[1]{0:T(128)S(6)} %copy.12.refs_0_, s32[1,1]{1,0:T(1,128)} %bitcast.7.refs_1_, f32[2,128,512]{2,1,0:T(8,128)S(1)} %shard_map.109.refs_2_, ...), custom_call_target="tpu_custom_call" | custom-call | flops 50000000 | bytes 20000000 | tf_op jit(solution)/shard_map/pallas_call | solution.py:54
  24.9 1.6 %collective-permute-start.11 = (bf16[320,128]{1,0:T(8,128)(2,1)S(1)}, bf16[320,128]{1,0:T(8,128)(2,1)S(1)}, u32[]{:S(2)}, u32[]{:S(2)}) collective-permute-start(bf16[320,128]{1,0:T(8,128)(2,1)S(1)} %get-tuple-element.56.own.c0), channel_id=1, source_target_pairs={{0,2},{1,3},{2,0},{3,1},{4,6},{5,7},{6,4},{7,5},{8,10},{9,11},{10,... | collective-permute-start | bytes 245768 | tf_op jit(solution)/shard_map/ppermute | solution.py:517
  26.5 2.5 %collective-permute-start.8 = (bf16[448,128]{1,0:T(8,128)(2,1)S(1)}, bf16[448,128]{1,0:T(8,128)(2,1)S(1)}, u32[]{:S(2)}, u32[]{:S(2)}) collective-permute-start(bf16[448,128]{1,0:T(8,128)(2,1)S(1)} %get-tuple-element.53), channel_id=1, source_target_pairs={{0,12},{4,8},{8,4},{12,0},{16,28},{20,24},{24,20},{28,16},{1,13},{... | collective-permute-start | bytes 344072 | tf_op jit(solution)/shard_map/ppermute | solution.py:517
  29.0 0.4 %collective-permute-start.9 = (bf16[448,128]{1,0:T(8,128)(2,1)S(1)}, bf16[448,128]{1,0:T(8,128)(2,1)S(1)}, u32[]{:S(2)}, u32[]{:S(2)}) collective-permute-start(bf16[448,128]{1,0:T(8,128)(2,1)S(1)} %get-tuple-element.54), channel_id=1, source_target_pairs={{0,8},{4,12},{8,0},{12,4},{16,24},{20,28},{24,16},{28,20},{1,9},{5... | collective-permute-start | bytes 344072 | tf_op jit(solution)/shard_map/ppermute | solution.py:517
  29.4 0.5 %collective-permute-start.10 = (bf16[448,128]{1,0:T(8,128)(2,1)S(1)}, bf16[448,128]{1,0:T(8,128)(2,1)S(1)}, u32[]{:S(2)}, u32[]{:S(2)}) collective-permute-start(bf16[448,128]{1,0:T(8,128)(2,1)S(1)} %get-tuple-element.55), channel_id=1, source_target_pairs={{0,4},{4,0},{8,12},{12,8},{16,20},{20,16},{24,28},{28,24},{1,5},{5... | collective-permute-start | bytes 344072 | tf_op jit(solution)/shard_map/ppermute | solution.py:517
  30.1 1.3 %collective-permute-done.12.refs_4_.c2 = bf16[320,128]{1,0:T(8,128)(2,1)S(1)} collective-permute-done((bf16[320,128]{1,0:T(8,128)(2,1)S(1)}, bf16[320,128]{1,0:T(8,128)(2,1)S(1)}, u32[]{:S(2)}, u32[]{:S(2)}) %collective-permute-start.12) | collective-permute-done | bytes 81952 | tf_op jit(solution)/shard_map/ppermute | solution.py:517
  31.4 1.1 %shard_map.113 = (f32[273,1,224]{2,1,0:T(1,128)}, f32[1,16,273]{2,1,0:T(8,128)}) custom-call(bf16[320,128]{1,0:T(8,128)(2,1)S(1)} %get-tuple-element.56.own.c0, bf16[320,128]{1,0:T(8,128)(2,1)S(1)} %collective-permute-done.11.got.c1, bf16[320,128]{1,0:T(8,128)(2,1)S(1)} %collective-permute-done.12.refs_4_.c2, bf16[273,160]{1,0:T(8,128)(2,1)S(1)} %copy-done.4), custom_call_target="tpu_custom_call" | custom-call | flops 40000000 | bytes 1000000 | tf_op jit(solution)/shard_map/pallas_call | solution.py:54
  32.5 1.3 %collective-permute-done.9.refs_2_ = bf16[448,128]{1,0:T(8,128)(2,1)S(1)} collective-permute-done((bf16[448,128]{1,0:T(8,128)(2,1)S(1)}, bf16[448,128]{1,0:T(8,128)(2,1)S(1)}, u32[]{:S(2)}, u32[]{:S(2)}) %collective-permute-start.9) | collective-permute-done | bytes 114720 | tf_op jit(solution)/shard_map/ppermute | solution.py:517
  33.8 0.4 %collective-permute-done.10.refs_3_ = bf16[448,128]{1,0:T(8,128)(2,1)S(1)} collective-permute-done((bf16[448,128]{1,0:T(8,128)(2,1)S(1)}, bf16[448,128]{1,0:T(8,128)(2,1)S(1)}, u32[]{:S(2)}, u32[]{:S(2)}) %collective-permute-start.10) | collective-permute-done | bytes 114720 | tf_op jit(solution)/shard_map/ppermute | solution.py:517
  34.2 0.9 %shard_map.112 = bf16[1,128,1792]{2,1,0:T(8,128)(2,1)} custom-call(bf16[448,128]{1,0:T(8,128)(2,1)S(1)} %get-tuple-element.52.refs_0_, bf16[448,128]{1,0:T(8,128)(2,1)S(1)} %collective-permute-done.8.refs_1_, bf16[448,128]{1,0:T(8,128)(2,1)S(1)} %collective-permute-done.9.refs_2_, bf16[448,128]{1,0:T(8,128)(2,1)S(1)} %collective-permute-done.10.refs_3_, ...), custom_call_target="tpu_custom_call" | custom-call | flops 1000 | bytes 1000000 | tf_op jit(solution)/shard_map/pallas_call | solution.py:421
  (25 shorter events, 0.6 us)
Async XLA Ops:
  0.6 8.5 %copy-start = (bf16[1792,1792]{1,0:T(8,128)(2,1)S(1)}, bf16[1792,1792]{1,0:T(8,128)(2,1)}, u32[]{:S(2)}) copy-start(bf16[1792,1792]{1,0:T(8,128)(2,1)} %refs_3_.3) | copy-start | bytes 19267588
  0.6 8.5 %copy-start.2 = (bf16[1792,256]{1,0:T(8,128)(2,1)S(1)}, bf16[1792,256]{1,0:T(8,128)(2,1)}, u32[]{:S(2)}) copy-start(bf16[1792,256]{1,0:T(8,128)(2,1)} %refs_2_.3) | copy-start | bytes 2752516
  0.7 8.5 %copy-start.1 = (bf16[1792,256]{1,0:T(8,128)(2,1)S(1)}, bf16[1792,256]{1,0:T(8,128)(2,1)}, u32[]{:S(2)}) copy-start(bf16[1792,256]{1,0:T(8,128)(2,1)} %refs_1_.3) | copy-start | bytes 2752516
  0.7 8.5 %copy-start.3 = (bf16[1,128,1792]{2,1,0:T(8,128)(2,1)S(1)}, bf16[1,128,1792]{2,1,0:T(8,128)(2,1)}, u32[]{:S(2)}) copy-start(bf16[1,128,1792]{2,1,0:T(8,128)(2,1)} %refs_0_.4) | copy-start | bytes 1376260
  3.7 10.0 %copy-start.5 = (f32[3,1792]{1,0:T(4,128)S(1)}, f32[3,1792]{1,0:T(4,128)}, u32[]{:S(2)}) copy-start(f32[3,1792]{1,0:T(4,128)} %refs_5_.1) | copy-start | bytes 64516
  3.7 9.8 %collective-permute-start.3 = (bf16[288,128]{1,0:T(8,128)(2,1)S(1)}, bf16[288,128]{1,0:T(8,128)(2,1)S(1)}, u32[]{:S(2)}, u32[]{:S(2)}) collective-permute-start(bf16[288,128]{1,0:T(8,128)(2,1)S(1)} %get-tuple-element.37), channel_id=1, source_target_pairs={{0,12},{4,8},{8,4},{12,0},{16,28},{20,24},{24,20},{28,16},{1,13},{... | collective-permute-start | bytes 221192 | tf_op jit(solution)/shard_map/ppermute | solution.py:517
  7.8 5.9 %collective-permute-start.4 = (bf16[288,128]{1,0:T(8,128)(2,1)S(1)}, bf16[288,128]{1,0:T(8,128)(2,1)S(1)}, u32[]{:S(2)}, u32[]{:S(2)}) collective-permute-start(bf16[288,128]{1,0:T(8,128)(2,1)S(1)} %get-tuple-element.38), channel_id=1, source_target_pairs={{0,8},{4,12},{8,0},{12,4},{16,24},{20,28},{24,16},{28,20},{1,9},{5... | collective-permute-start | bytes 221192 | tf_op jit(solution)/shard_map/ppermute | solution.py:517
  8.2 5.5 %collective-permute-start.5 = (bf16[288,128]{1,0:T(8,128)(2,1)S(1)}, bf16[288,128]{1,0:T(8,128)(2,1)S(1)}, u32[]{:S(2)}, u32[]{:S(2)}) collective-permute-start(bf16[288,128]{1,0:T(8,128)(2,1)S(1)} %get-tuple-element.39), channel_id=1, source_target_pairs={{0,4},{4,0},{8,12},{12,8},{16,20},{20,16},{24,28},{28,24},{1,5},{5... | collective-permute-start | bytes 221192 | tf_op jit(solution)/shard_map/ppermute | solution.py:517
  10.2 8.0 %collective-permute-start = (bf16[320,128]{1,0:T(8,128)(2,1)S(1)}, bf16[320,128]{1,0:T(8,128)(2,1)S(1)}, u32[]{:S(2)}, u32[]{:S(2)}) collective-permute-start(bf16[320,128]{1,0:T(8,128)(2,1)S(1)} %get-tuple-element.33), channel_id=1, source_target_pairs={{0,12},{4,8},{8,4},{12,0},{16,28},{20,24},{24,20},{28,16},{1,13},{... | collective-permute-start | bytes 245768 | tf_op jit(solution)/shard_map/ppermute | solution.py:517
  13.0 5.2 %collective-permute-start.1 = (bf16[320,128]{1,0:T(8,128)(2,1)S(1)}, bf16[320,128]{1,0:T(8,128)(2,1)S(1)}, u32[]{:S(2)}, u32[]{:S(2)}) collective-permute-start(bf16[320,128]{1,0:T(8,128)(2,1)S(1)} %get-tuple-element.34), channel_id=1, source_target_pairs={{0,8},{4,12},{8,0},{12,4},{16,24},{20,28},{24,16},{28,20},{1,9},{5... | collective-permute-start | bytes 245768 | tf_op jit(solution)/shard_map/ppermute | solution.py:517
  13.5 4.7 %collective-permute-start.2 = (bf16[320,128]{1,0:T(8,128)(2,1)S(1)}, bf16[320,128]{1,0:T(8,128)(2,1)S(1)}, u32[]{:S(2)}, u32[]{:S(2)}) collective-permute-start(bf16[320,128]{1,0:T(8,128)(2,1)S(1)} %get-tuple-element.35), channel_id=1, source_target_pairs={{0,4},{4,0},{8,12},{12,8},{16,20},{20,16},{24,28},{28,24},{1,5},{5... | collective-permute-start | bytes 245768 | tf_op jit(solution)/shard_map/ppermute | solution.py:517
  14.5 7.5 %collective-permute-start.6 = (bf16[288,128]{1,0:T(8,128)(2,1)S(1)}, bf16[288,128]{1,0:T(8,128)(2,1)S(1)}, u32[]{:S(2)}, u32[]{:S(2)}) collective-permute-start(bf16[288,128]{1,0:T(8,128)(2,1)S(1)} %get-tuple-element.41.refs_6_.refs_2_), channel_id=1, source_target_pairs={{0,16},{4,20},{8,24},{12,28},{16,0},{20,4},{24,8},{28,12},{1,17},{... | collective-permute-start | bytes 221192 | tf_op jit(solution)/shard_map/ppermute | solution.py:517
  18.8 5.4 %collective-permute-start.7 = (bf16[320,128]{1,0:T(8,128)(2,1)S(1)}, bf16[320,128]{1,0:T(8,128)(2,1)S(1)}, u32[]{:S(2)}, u32[]{:S(2)}) collective-permute-start(bf16[320,128]{1,0:T(8,128)(2,1)S(1)} %get-tuple-element.46.refs_2_.refs_3_), channel_id=1, source_target_pairs={{0,16},{4,20},{8,24},{12,28},{16,0},{20,4},{24,8},{28,12},{1,17},{... | collective-permute-start | bytes 245768 | tf_op jit(solution)/shard_map/ppermute | solution.py:517
  22.8 8.6 %copy-start.4 = (bf16[273,160]{1,0:T(8,128)(2,1)S(1)}, bf16[273,160]{1,0:T(8,128)(2,1)}, u32[]{:S(2)}) copy-start(bf16[273,160]{1,0:T(8,128)(2,1)} %constant.2.clone.spread) | copy-start | bytes 262084
  24.9 5.1 %collective-permute-start.11 = (bf16[320,128]{1,0:T(8,128)(2,1)S(1)}, bf16[320,128]{1,0:T(8,128)(2,1)S(1)}, u32[]{:S(2)}, u32[]{:S(2)}) collective-permute-start(bf16[320,128]{1,0:T(8,128)(2,1)S(1)} %get-tuple-element.56.own.c0), channel_id=1, source_target_pairs={{0,2},{1,3},{2,0},{3,1},{4,6},{5,7},{6,4},{7,5},{8,10},{9,11},{10,... | collective-permute-start | bytes 245768 | tf_op jit(solution)/shard_map/ppermute | solution.py:517
  26.5 6.0 %collective-permute-start.8 = (bf16[448,128]{1,0:T(8,128)(2,1)S(1)}, bf16[448,128]{1,0:T(8,128)(2,1)S(1)}, u32[]{:S(2)}, u32[]{:S(2)}) collective-permute-start(bf16[448,128]{1,0:T(8,128)(2,1)S(1)} %get-tuple-element.53), channel_id=1, source_target_pairs={{0,12},{4,8},{8,4},{12,0},{16,28},{20,24},{24,20},{28,16},{1,13},{... | collective-permute-start | bytes 344072 | tf_op jit(solution)/shard_map/ppermute | solution.py:517
  29.0 4.8 %collective-permute-start.9 = (bf16[448,128]{1,0:T(8,128)(2,1)S(1)}, bf16[448,128]{1,0:T(8,128)(2,1)S(1)}, u32[]{:S(2)}, u32[]{:S(2)}) collective-permute-start(bf16[448,128]{1,0:T(8,128)(2,1)S(1)} %get-tuple-element.54), channel_id=1, source_target_pairs={{0,8},{4,12},{8,0},{12,4},{16,24},{20,28},{24,16},{28,20},{1,9},{5... | collective-permute-start | bytes 344072 | tf_op jit(solution)/shard_map/ppermute | solution.py:517
  29.4 4.8 %collective-permute-start.10 = (bf16[448,128]{1,0:T(8,128)(2,1)S(1)}, bf16[448,128]{1,0:T(8,128)(2,1)S(1)}, u32[]{:S(2)}, u32[]{:S(2)}) collective-permute-start(bf16[448,128]{1,0:T(8,128)(2,1)S(1)} %get-tuple-element.55), channel_id=1, source_target_pairs={{0,4},{4,0},{8,12},{12,8},{16,20},{20,16},{24,28},{28,24},{1,5},{5... | collective-permute-start | bytes 344072 | tf_op jit(solution)/shard_map/ppermute | solution.py:517
  30.1 1.3 %collective-permute-start.12 = (bf16[320,128]{1,0:T(8,128)(2,1)S(1)}, bf16[320,128]{1,0:T(8,128)(2,1)S(1)}, u32[]{:S(2)}, u32[]{:S(2)}) collective-permute-start(bf16[320,128]{1,0:T(8,128)(2,1)S(1)} %shard_map.111), channel_id=1, source_target_pairs={{0,1},{1,0},{2,3},{3,2},{4,5},{5,4},{6,7},{7,6},{8,9},{9,8},{10,11... | collective-permute-start | bytes 245768 | tf_op jit(solution)/shard_map/ppermute | solution.py:517

commit v6 on v5

--- a/solution.py
+++ b/solution.py
@@ -21,6 +21,7 @@
 INFO = 31
 LOCAL = HEADS // GROUP // 2
 ORDER = (0, 3, 2, 1)
+RETURN = (0, 3, 1, 2)
 f32 = jnp.float32
 bf16 = jnp.bfloat16
 NT = (((1,), (1,)), ((), ()))
@@ -350,7 +351,7 @@
         result = (top * inverse).astype(bf16)
         for b in range(GROUP):
             scr[b, h * size : (h + 1) * size, :] = result[:, b * rows : (b + 1) * rows]
-    for j, (s, out) in enumerate(zip(ORDER, (r0, r1, r2, r3))):
+    for j, (s, out) in enumerate(zip(RETURN, (r0, r1, r2, r3))):
         if half:
             out[0 : LOCAL * size, :] = firsts[j][...]
         out[half * LOCAL * size :, :] = scr[mine ^ s]
@@ -392,7 +393,7 @@
     mine = lax.rem(lax.axis_index("blk"), GROUP)
     half = width // 2
     slab = half // GROUP
-    for s, ref in zip(ORDER, (r0, r1, r2, r3)):
+    for s, ref in zip(RETURN, (r0, r1, r2, r3)):
         start = pl.multiple_of(slab * (mine ^ s), 32)
         scr[pl.ds(start, slab), :] = ref[0:slab, :]
         scr[pl.ds(pl.multiple_of(half + start, 32), slab), :] = ref[slab:, :]
@@ -509,8 +510,8 @@
     return call(expand_kernel, outs, [], 32, 40_000_000, 1_000_000, [*candidates, spread])
 
 
-def across(arrays):
-    return [swap(array, "blk", s) if s else array for s, array in zip(ORDER, arrays)]
+def across(arrays, order):
+    return [swap(array, "blk", s) if s else array for s, array in zip(order, arrays)]
 
 
 def swap(array, axis, by):
@@ -524,9 +525,9 @@
     given = (tokens_in, query_weight, key_weight, value_weight)
     length, slot = prompt_lengths.reshape(1, 1), decode_map
     *parts, early = project(0, *given)
-    sent = [across(parts)]
+    sent = [across(parts, ORDER)]
     parts = project(1, *given, length, early)
-    sent.append(across(parts))
+    sent.append(across(parts, ORDER))
     *first, taps = group_state(0, length, sent[0], conv_weight, [])
     second = group_state(1, length, sent[1], taps, [first[2]])
     got = [swap(held[2], "blk", GROUP) for held in (first, second)]
@@ -536,7 +537,7 @@
     aug, qk, own = second
     num = local_part(aug, qk, 5_000_000_000, [early[4]])
     *parts, total = finish(1, length, slot, num, own, got[1], qk, taps, [early[4], *early[:4]])
-    results = across(parts)
+    results = across(parts, RETURN)
     beside = swap(total, "req", ROUTE[0])
     theirs = swap(hand_on(total, beside, []), "req", ROUTE[1])
     state, norm = expand_state([total, beside, theirs], width // lax.axis_size("blk"))

time: 35.3 us -> 35.4 us (level)
  no operation moved by 1% of the time
where the time goes in v6:
time: 35.4 us; the launch traced here: 35.2 us
  starting transfers between devices  18.6 us (53%)
  Pallas kernels  11 us (31%)
  waiting for transfers between devices  3.48 us (10%)
  between operations  2.1 us (6%)
    ppermute x13, starting transfers between devices, swap(): lax.ppermute(array, axis, [(i, i ^ by) for i in range(lax.axis_size(axis))])  18.6 us
    pallas_call x10, Pallas kernels, call(): pl.pallas_call(kernel, out_shape=[jax.ShapeDtypeStruct(shape, dtype) for...  10 us
    ppermute x13, waiting for transfers between devices, swap(): lax.ppermute(array, axis, [(i, i ^ by) for i in range(lax.axis_size(axis))])  3.48 us
    pallas_call x1, Pallas kernels, place_tokens(): pl.pallas_call(kernel, out_shape=jax.ShapeDtypeStruct((1, rows, width), b...  0.93 us
  transfers between devices with their start and end apart: 13, of which 4 were waited for; matrix products, arithmetic and copies ran while one was open for 0% of the time, Pallas kernels for 18%

profile of v6, /device:TPU:0, one launch (start us, length us, event | category | flops | bytes accessed | tf_op | source)
XLA Modules:
  0.0 35.2 jit_solution(16138239754553489769)
XLA Ops:
  0.7 3.0 %shard_map.103 = (bf16[288,128]{1,0:T(8,128)(2,1)S(1)}, bf16[288,128]{1,0:T(8,128)(2,1)S(1)}, bf16[288,128]{1,0:T(8,128)(2,1)S(1)}, bf16[288,128]{1,0:T(8,128)(2,1)S(1)}, bf16[128,128]{1,0:T(8,128)(2,1)S(1)}) custom-call(bf16[1,128,1792]{2,1,0:T(8,128)(2,1)} %refs_0_.4, bf16[1792,256]{1,0:T(8,128)(2,1)} %refs_1_.3, bf16[1792,256]{1,0:T(8,128)(2,1)} %refs_2_.3, ...), custom_call_target="tpu_custom_call" | custom-call | flops 528482304 | bytes 4128768 | tf_op jit(solution)/shard_map/pallas_call | solution.py:55
  3.7 4.1 %collective-permute-start.3 = (bf16[288,128]{1,0:T(8,128)(2,1)S(1)}, bf16[288,128]{1,0:T(8,128)(2,1)S(1)}, u32[]{:S(2)}, u32[]{:S(2)}) collective-permute-start(bf16[288,128]{1,0:T(8,128)(2,1)S(1)} %get-tuple-element.37), channel_id=1, source_target_pairs={{0,12},{4,8},{8,4},{12,0},{16,28},{20,24},{24,20},{28,16},{1,13},{... | collective-permute-start | bytes 221192 | tf_op jit(solution)/shard_map/ppermute | solution.py:518
  7.8 0.4 %collective-permute-start.4 = (bf16[288,128]{1,0:T(8,128)(2,1)S(1)}, bf16[288,128]{1,0:T(8,128)(2,1)S(1)}, u32[]{:S(2)}, u32[]{:S(2)}) collective-permute-start(bf16[288,128]{1,0:T(8,128)(2,1)S(1)} %get-tuple-element.38), channel_id=1, source_target_pairs={{0,8},{4,12},{8,0},{12,4},{16,24},{20,28},{24,16},{28,20},{1,9},{5... | collective-permute-start | bytes 221192 | tf_op jit(solution)/shard_map/ppermute | solution.py:518
  9.1 1.1 %shard_map.104 = (bf16[320,128]{1,0:T(8,128)(2,1)S(1)}, bf16[320,128]{1,0:T(8,128)(2,1)S(1)}, bf16[320,128]{1,0:T(8,128)(2,1)S(1)}, bf16[320,128]{1,0:T(8,128)(2,1)S(1)}) custom-call(bf16[1,128,1792]{2,1,0:T(8,128)(2,1)S(1)} %copy-done.3, bf16[1792,256]{1,0:T(8,128)(2,1)S(1)} %copy-done.1, bf16[1792,256]{1,0:T(8,128)(2,1)S(1)} %copy-done.2, ...), custom_call_target="tpu_custom_call" | custom-call | flops 528482304 | bytes 4128768 | tf_op jit(solution)/shard_map/pallas_call | solution.py:55
  10.2 2.9 %collective-permute-start = (bf16[320,128]{1,0:T(8,128)(2,1)S(1)}, bf16[320,128]{1,0:T(8,128)(2,1)S(1)}, u32[]{:S(2)}, u32[]{:S(2)}) collective-permute-start(bf16[320,128]{1,0:T(8,128)(2,1)S(1)} %get-tuple-element.33), channel_id=1, source_target_pairs={{0,12},{4,8},{8,4},{12,0},{16,28},{20,24},{24,20},{28,16},{1,13},{... | collective-permute-start | bytes 245768 | tf_op jit(solution)/shard_map/ppermute | solution.py:518
  13.0 0.4 %collective-permute-start.1 = (bf16[320,128]{1,0:T(8,128)(2,1)S(1)}, bf16[320,128]{1,0:T(8,128)(2,1)S(1)}, u32[]{:S(2)}, u32[]{:S(2)}) collective-permute-start(bf16[320,128]{1,0:T(8,128)(2,1)S(1)} %get-tuple-element.34), channel_id=1, source_target_pairs={{0,8},{4,12},{8,0},{12,4},{16,24},{20,28},{24,16},{28,20},{1,9},{5... | collective-permute-start | bytes 245768 | tf_op jit(solution)/shard_map/ppermute | solution.py:518
  13.7 0.8 %shard_map.105 = (bf16[2,128,512]{2,1,0:T(8,128)(2,1)S(1)}, bf16[64,512]{1,0:T(8,128)(2,1)S(1)}, bf16[288,128]{1,0:T(8,128)(2,1)S(1)}, f32[448,8]{1,0:T(8,128)S(1)}) custom-call(s32[1,1]{1,0:T(1,128)} %bitcast.4.refs_0_, bf16[288,128]{1,0:T(8,128)(2,1)S(1)} %get-tuple-element.36.refs_1_, bf16[288,128]{1,0:T(8,128)(2,1)S(1)} %collective-permute-done.3.refs_2_, ...), custom_call_target="tpu_custom_call" | custom-call | flops 100000000 | bytes 1000000 | tf_op jit(solution)/shard_map/pallas_call | solution.py:55
  14.5 3.0 %collective-permute-start.6 = (bf16[288,128]{1,0:T(8,128)(2,1)S(1)}, bf16[288,128]{1,0:T(8,128)(2,1)S(1)}, u32[]{:S(2)}, u32[]{:S(2)}) collective-permute-start(bf16[288,128]{1,0:T(8,128)(2,1)S(1)} %get-tuple-element.41.refs_6_.refs_2_), channel_id=1, source_target_pairs={{0,16},{4,20},{8,24},{12,28},{16,0},{20,4},{24,8},{28,12},{1,17},{... | collective-permute-start | bytes 221192 | tf_op jit(solution)/shard_map/ppermute | solution.py:518
  18.2 0.6 %shard_map.106 = (bf16[2,128,512]{2,1,0:T(8,128)(2,1)S(1)}, bf16[64,512]{1,0:T(8,128)(2,1)S(1)}, bf16[320,128]{1,0:T(8,128)(2,1)S(1)}) custom-call(s32[1,1]{1,0:T(1,128)} %bitcast.5.refs_0_, bf16[320,128]{1,0:T(8,128)(2,1)S(1)} %get-tuple-element.32.refs_1_, bf16[320,128]{1,0:T(8,128)(2,1)S(1)} %collective-permute-done.refs_2_, ...), custom_call_target="tpu_custom_call" | custom-call | flops 100000000 | bytes 1000000 | tf_op jit(solution)/shard_map/pallas_call | solution.py:55
  18.8 2.4 %collective-permute-start.7 = (bf16[320,128]{1,0:T(8,128)(2,1)S(1)}, bf16[320,128]{1,0:T(8,128)(2,1)S(1)}, u32[]{:S(2)}, u32[]{:S(2)}) collective-permute-start(bf16[320,128]{1,0:T(8,128)(2,1)S(1)} %get-tuple-element.46.refs_2_.refs_3_), channel_id=1, source_target_pairs={{0,16},{4,20},{8,24},{12,28},{16,0},{20,4},{24,8},{28,12},{1,17},{... | collective-permute-start | bytes 245768 | tf_op jit(solution)/shard_map/ppermute | solution.py:518
  21.1 0.9 %shard_map.107.refs_1_ = f32[2,128,512]{2,1,0:T(8,128)S(1)} custom-call(bf16[2,128,512]{2,1,0:T(8,128)(2,1)S(1)} %get-tuple-element.44.refs_0_, bf16[64,512]{1,0:T(8,128)(2,1)S(1)} %get-tuple-element.45.refs_1_.refs_4_, bf16[320,128]{1,0:T(8,128)(2,1)S(1)} %get-tuple-element.46.refs_2_.refs_3_), custom_call_target="tpu_custom_call" | custom-call | flops 1000 | bytes 1000 | tf_op jit(solution)/shard_map/pallas_call | solution.py:55
  22.1 0.7 %shard_map.108 = (bf16[224,128]{1,0:T(8,128)(2,1)S(1)}, bf16[224,128]{1,0:T(8,128)(2,1)S(1)}, bf16[224,128]{1,0:T(8,128)(2,1)S(1)}, bf16[224,128]{1,0:T(8,128)(2,1)S(1)}, bf16[288,128]{1,0:T(8,128)(2,1)S(1)}) custom-call(s32[1,1]{1,0:T(1,128)} %bitcast.6.refs_0_, f32[2,128,512]{2,1,0:T(8,128)S(1)} %shard_map.107.refs_1_, ...), custom_call_target="tpu_custom_call" | custom-call | flops 50000000 | bytes 20000000 | tf_op jit(solution)/shard_map/pallas_call | solution.py:55
  22.8 0.9 %shard_map.109.refs_2_ = f32[2,128,512]{2,1,0:T(8,128)S(1)} custom-call(bf16[2,128,512]{2,1,0:T(8,128)(2,1)S(1)} %get-tuple-element.42.refs_0_, bf16[64,512]{1,0:T(8,128)(2,1)S(1)} %get-tuple-element.43.refs_1_.refs_5_, bf16[288,128]{1,0:T(8,128)(2,1)S(1)} %get-tuple-element.47.refs_2_.refs_7_), custom_call_target="tpu_custom_call" | custom-call | flops 5000000000 | bytes 1000 | tf_op jit(solution)/shard_map/pallas_call | solution.py:55
  23.8 0.4 %collective-permute-done.7.refs_4_ = bf16[320,128]{1,0:T(8,128)(2,1)S(1)} collective-permute-done((bf16[320,128]{1,0:T(8,128)(2,1)S(1)}, bf16[320,128]{1,0:T(8,128)(2,1)S(1)}, u32[]{:S(2)}, u32[]{:S(2)}) %collective-permute-start.7) | collective-permute-done | bytes 81952 | tf_op jit(solution)/shard_map/ppermute | solution.py:518
  24.2 0.7 %shard_map.110 = (bf16[448,128]{1,0:T(8,128)(2,1)S(1)}, bf16[448,128]{1,0:T(8,128)(2,1)S(1)}, bf16[448,128]{1,0:T(8,128)(2,1)S(1)}, bf16[448,128]{1,0:T(8,128)(2,1)S(1)}, bf16[320,128]{1,0:T(8,128)(2,1)S(1)}) custom-call(s32[1]{0:T(128)S(6)} %copy.12.refs_0_, s32[1,1]{1,0:T(1,128)} %bitcast.7.refs_1_, f32[2,128,512]{2,1,0:T(8,128)S(1)} %shard_map.109.refs_2_, ...), custom_call_target="tpu_custom_call" | custom-call | flops 50000000 | bytes 20000000 | tf_op jit(solution)/shard_map/pallas_call | solution.py:55
  24.9 1.6 %collective-permute-start.11 = (bf16[320,128]{1,0:T(8,128)(2,1)S(1)}, bf16[320,128]{1,0:T(8,128)(2,1)S(1)}, u32[]{:S(2)}, u32[]{:S(2)}) collective-permute-start(bf16[320,128]{1,0:T(8,128)(2,1)S(1)} %get-tuple-element.56.own.c0), channel_id=1, source_target_pairs={{0,2},{1,3},{2,0},{3,1},{4,6},{5,7},{6,4},{7,5},{8,10},{9,11},{10,... | collective-permute-start | bytes 245768 | tf_op jit(solution)/shard_map/ppermute | solution.py:518
  26.5 2.5 %collective-permute-start.8 = (bf16[448,128]{1,0:T(8,128)(2,1)S(1)}, bf16[448,128]{1,0:T(8,128)(2,1)S(1)}, u32[]{:S(2)}, u32[]{:S(2)}) collective-permute-start(bf16[448,128]{1,0:T(8,128)(2,1)S(1)} %get-tuple-element.53), channel_id=1, source_target_pairs={{0,12},{4,8},{8,4},{12,0},{16,28},{20,24},{24,20},{28,16},{1,13},{... | collective-permute-start | bytes 344072 | tf_op jit(solution)/shard_map/ppermute | solution.py:518
  29.0 0.5 %collective-permute-start.9 = (bf16[448,128]{1,0:T(8,128)(2,1)S(1)}, bf16[448,128]{1,0:T(8,128)(2,1)S(1)}, u32[]{:S(2)}, u32[]{:S(2)}) collective-permute-start(bf16[448,128]{1,0:T(8,128)(2,1)S(1)} %get-tuple-element.54), channel_id=1, source_target_pairs={{0,4},{4,0},{8,12},{12,8},{16,20},{20,16},{24,28},{28,24},{1,5},{5... | collective-permute-start | bytes 344072 | tf_op jit(solution)/shard_map/ppermute | solution.py:518
  29.5 0.5 %collective-permute-start.10 = (bf16[448,128]{1,0:T(8,128)(2,1)S(1)}, bf16[448,128]{1,0:T(8,128)(2,1)S(1)}, u32[]{:S(2)}, u32[]{:S(2)}) collective-permute-start(bf16[448,128]{1,0:T(8,128)(2,1)S(1)} %get-tuple-element.55), channel_id=1, source_target_pairs={{0,8},{4,12},{8,0},{12,4},{16,24},{20,28},{24,16},{28,20},{1,9},{5... | collective-permute-start | bytes 344072 | tf_op jit(solution)/shard_map/ppermute | solution.py:518
  30.1 1.3 %collective-permute-done.12.refs_4_.c2 = bf16[320,128]{1,0:T(8,128)(2,1)S(1)} collective-permute-done((bf16[320,128]{1,0:T(8,128)(2,1)S(1)}, bf16[320,128]{1,0:T(8,128)(2,1)S(1)}, u32[]{:S(2)}, u32[]{:S(2)}) %collective-permute-start.12) | collective-permute-done | bytes 81952 | tf_op jit(solution)/shard_map/ppermute | solution.py:518
  31.4 1.1 %shard_map.113 = (f32[273,1,224]{2,1,0:T(1,128)}, f32[1,16,273]{2,1,0:T(8,128)}) custom-call(bf16[320,128]{1,0:T(8,128)(2,1)S(1)} %get-tuple-element.56.own.c0, bf16[320,128]{1,0:T(8,128)(2,1)S(1)} %collective-permute-done.11.got.c1, bf16[320,128]{1,0:T(8,128)(2,1)S(1)} %collective-permute-done.12.refs_4_.c2, bf16[273,160]{1,0:T(8,128)(2,1)S(1)} %copy-done.4), custom_call_target="tpu_custom_call" | custom-call | flops 40000000 | bytes 1000000 | tf_op jit(solution)/shard_map/pallas_call | solution.py:55
  32.5 1.3 %collective-permute-done.9.refs_2_ = bf16[448,128]{1,0:T(8,128)(2,1)S(1)} collective-permute-done((bf16[448,128]{1,0:T(8,128)(2,1)S(1)}, bf16[448,128]{1,0:T(8,128)(2,1)S(1)}, u32[]{:S(2)}, u32[]{:S(2)}) %collective-permute-start.9) | collective-permute-done | bytes 114720 | tf_op jit(solution)/shard_map/ppermute | solution.py:518
  33.8 0.5 %collective-permute-done.10.refs_3_ = bf16[448,128]{1,0:T(8,128)(2,1)S(1)} collective-permute-done((bf16[448,128]{1,0:T(8,128)(2,1)S(1)}, bf16[448,128]{1,0:T(8,128)(2,1)S(1)}, u32[]{:S(2)}, u32[]{:S(2)}) %collective-permute-start.10) | collective-permute-done | bytes 114720 | tf_op jit(solution)/shard_map/ppermute | solution.py:518
  34.3 0.9 %shard_map.112 = bf16[1,128,1792]{2,1,0:T(8,128)(2,1)} custom-call(bf16[448,128]{1,0:T(8,128)(2,1)S(1)} %get-tuple-element.52.refs_0_, bf16[448,128]{1,0:T(8,128)(2,1)S(1)} %collective-permute-done.8.refs_1_, bf16[448,128]{1,0:T(8,128)(2,1)S(1)} %collective-permute-done.9.refs_2_, bf16[448,128]{1,0:T(8,128)(2,1)S(1)} %collective-permute-done.10.refs_3_, ...), custom_call_target="tpu_custom_call" | custom-call | flops 1000 | bytes 1000000 | tf_op jit(solution)/shard_map/pallas_call | solution.py:422
  (25 shorter events, 0.6 us)
Async XLA Ops:
  0.6 8.5 %copy-start = (bf16[1792,1792]{1,0:T(8,128)(2,1)S(1)}, bf16[1792,1792]{1,0:T(8,128)(2,1)}, u32[]{:S(2)}) copy-start(bf16[1792,1792]{1,0:T(8,128)(2,1)} %refs_3_.3) | copy-start | bytes 19267588
  0.6 8.5 %copy-start.2 = (bf16[1792,256]{1,0:T(8,128)(2,1)S(1)}, bf16[1792,256]{1,0:T(8,128)(2,1)}, u32[]{:S(2)}) copy-start(bf16[1792,256]{1,0:T(8,128)(2,1)} %refs_2_.3) | copy-start | bytes 2752516
  0.7 8.5 %copy-start.1 = (bf16[1792,256]{1,0:T(8,128)(2,1)S(1)}, bf16[1792,256]{1,0:T(8,128)(2,1)}, u32[]{:S(2)}) copy-start(bf16[1792,256]{1,0:T(8,128)(2,1)} %refs_1_.3) | copy-start | bytes 2752516
  0.7 8.5 %copy-start.3 = (bf16[1,128,1792]{2,1,0:T(8,128)(2,1)S(1)}, bf16[1,128,1792]{2,1,0:T(8,128)(2,1)}, u32[]{:S(2)}) copy-start(bf16[1,128,1792]{2,1,0:T(8,128)(2,1)} %refs_0_.4) | copy-start | bytes 1376260
  3.7 10.0 %copy-start.5 = (f32[3,1792]{1,0:T(4,128)S(1)}, f32[3,1792]{1,0:T(4,128)}, u32[]{:S(2)}) copy-start(f32[3,1792]{1,0:T(4,128)} %refs_5_.1) | copy-start | bytes 64516
  3.7 9.8 %collective-permute-start.3 = (bf16[288,128]{1,0:T(8,128)(2,1)S(1)}, bf16[288,128]{1,0:T(8,128)(2,1)S(1)}, u32[]{:S(2)}, u32[]{:S(2)}) collective-permute-start(bf16[288,128]{1,0:T(8,128)(2,1)S(1)} %get-tuple-element.37), channel_id=1, source_target_pairs={{0,12},{4,8},{8,4},{12,0},{16,28},{20,24},{24,20},{28,16},{1,13},{... | collective-permute-start | bytes 221192 | tf_op jit(solution)/shard_map/ppermute | solution.py:518
  7.8 5.9 %collective-permute-start.4 = (bf16[288,128]{1,0:T(8,128)(2,1)S(1)}, bf16[288,128]{1,0:T(8,128)(2,1)S(1)}, u32[]{:S(2)}, u32[]{:S(2)}) collective-permute-start(bf16[288,128]{1,0:T(8,128)(2,1)S(1)} %get-tuple-element.38), channel_id=1, source_target_pairs={{0,8},{4,12},{8,0},{12,4},{16,24},{20,28},{24,16},{28,20},{1,9},{5... | collective-permute-start | bytes 221192 | tf_op jit(solution)/shard_map/ppermute | solution.py:518
  8.2 5.5 %collective-permute-start.5 = (bf16[288,128]{1,0:T(8,128)(2,1)S(1)}, bf16[288,128]{1,0:T(8,128)(2,1)S(1)}, u32[]{:S(2)}, u32[]{:S(2)}) collective-permute-start(bf16[288,128]{1,0:T(8,128)(2,1)S(1)} %get-tuple-element.39), channel_id=1, source_target_pairs={{0,4},{4,0},{8,12},{12,8},{16,20},{20,16},{24,28},{28,24},{1,5},{5... | collective-permute-start | bytes 221192 | tf_op jit(solution)/shard_map/ppermute | solution.py:518
  10.2 8.0 %collective-permute-start = (bf16[320,128]{1,0:T(8,128)(2,1)S(1)}, bf16[320,128]{1,0:T(8,128)(2,1)S(1)}, u32[]{:S(2)}, u32[]{:S(2)}) collective-permute-start(bf16[320,128]{1,0:T(8,128)(2,1)S(1)} %get-tuple-element.33), channel_id=1, source_target_pairs={{0,12},{4,8},{8,4},{12,0},{16,28},{20,24},{24,20},{28,16},{1,13},{... | collective-permute-start | bytes 245768 | tf_op jit(solution)/shard_map/ppermute | solution.py:518
  13.0 5.2 %collective-permute-start.1 = (bf16[320,128]{1,0:T(8,128)(2,1)S(1)}, bf16[320,128]{1,0:T(8,128)(2,1)S(1)}, u32[]{:S(2)}, u32[]{:S(2)}) collective-permute-start(bf16[320,128]{1,0:T(8,128)(2,1)S(1)} %get-tuple-element.34), channel_id=1, source_target_pairs={{0,8},{4,12},{8,0},{12,4},{16,24},{20,28},{24,16},{28,20},{1,9},{5... | collective-permute-start | bytes 245768 | tf_op jit(solution)/shard_map/ppermute | solution.py:518
  13.5 4.7 %collective-permute-start.2 = (bf16[320,128]{1,0:T(8,128)(2,1)S(1)}, bf16[320,128]{1,0:T(8,128)(2,1)S(1)}, u32[]{:S(2)}, u32[]{:S(2)}) collective-permute-start(bf16[320,128]{1,0:T(8,128)(2,1)S(1)} %get-tuple-element.35), channel_id=1, source_target_pairs={{0,4},{4,0},{8,12},{12,8},{16,20},{20,16},{24,28},{28,24},{1,5},{5... | collective-permute-start | bytes 245768 | tf_op jit(solution)/shard_map/ppermute | solution.py:518
  14.5 7.5 %collective-permute-start.6 = (bf16[288,128]{1,0:T(8,128)(2,1)S(1)}, bf16[288,128]{1,0:T(8,128)(2,1)S(1)}, u32[]{:S(2)}, u32[]{:S(2)}) collective-permute-start(bf16[288,128]{1,0:T(8,128)(2,1)S(1)} %get-tuple-element.41.refs_6_.refs_2_), channel_id=1, source_target_pairs={{0,16},{4,20},{8,24},{12,28},{16,0},{20,4},{24,8},{28,12},{1,17},{... | collective-permute-start | bytes 221192 | tf_op jit(solution)/shard_map/ppermute | solution.py:518
  18.8 5.4 %collective-permute-start.7 = (bf16[320,128]{1,0:T(8,128)(2,1)S(1)}, bf16[320,128]{1,0:T(8,128)(2,1)S(1)}, u32[]{:S(2)}, u32[]{:S(2)}) collective-permute-start(bf16[320,128]{1,0:T(8,128)(2,1)S(1)} %get-tuple-element.46.refs_2_.refs_3_), channel_id=1, source_target_pairs={{0,16},{4,20},{8,24},{12,28},{16,0},{20,4},{24,8},{28,12},{1,17},{... | collective-permute-start | bytes 245768 | tf_op jit(solution)/shard_map/ppermute | solution.py:518
  22.8 8.6 %copy-start.4 = (bf16[273,160]{1,0:T(8,128)(2,1)S(1)}, bf16[273,160]{1,0:T(8,128)(2,1)}, u32[]{:S(2)}) copy-start(bf16[273,160]{1,0:T(8,128)(2,1)} %constant.2.clone.spread) | copy-start | bytes 262084
  24.9 5.1 %collective-permute-start.11 = (bf16[320,128]{1,0:T(8,128)(2,1)S(1)}, bf16[320,128]{1,0:T(8,128)(2,1)S(1)}, u32[]{:S(2)}, u32[]{:S(2)}) collective-permute-start(bf16[320,128]{1,0:T(8,128)(2,1)S(1)} %get-tuple-element.56.own.c0), channel_id=1, source_target_pairs={{0,2},{1,3},{2,0},{3,1},{4,6},{5,7},{6,4},{7,5},{8,10},{9,11},{10,... | collective-permute-start | bytes 245768 | tf_op jit(solution)/shard_map/ppermute | solution.py:518
  26.5 6.0 %collective-permute-start.8 = (bf16[448,128]{1,0:T(8,128)(2,1)S(1)}, bf16[448,128]{1,0:T(8,128)(2,1)S(1)}, u32[]{:S(2)}, u32[]{:S(2)}) collective-permute-start(bf16[448,128]{1,0:T(8,128)(2,1)S(1)} %get-tuple-element.53), channel_id=1, source_target_pairs={{0,12},{4,8},{8,4},{12,0},{16,28},{20,24},{24,20},{28,16},{1,13},{... | collective-permute-start | bytes 344072 | tf_op jit(solution)/shard_map/ppermute | solution.py:518
  29.0 4.8 %collective-permute-start.9 = (bf16[448,128]{1,0:T(8,128)(2,1)S(1)}, bf16[448,128]{1,0:T(8,128)(2,1)S(1)}, u32[]{:S(2)}, u32[]{:S(2)}) collective-permute-start(bf16[448,128]{1,0:T(8,128)(2,1)S(1)} %get-tuple-element.54), channel_id=1, source_target_pairs={{0,4},{4,0},{8,12},{12,8},{16,20},{20,16},{24,28},{28,24},{1,5},{5... | collective-permute-start | bytes 344072 | tf_op jit(solution)/shard_map/ppermute | solution.py:518
  29.5 4.8 %collective-permute-start.10 = (bf16[448,128]{1,0:T(8,128)(2,1)S(1)}, bf16[448,128]{1,0:T(8,128)(2,1)S(1)}, u32[]{:S(2)}, u32[]{:S(2)}) collective-permute-start(bf16[448,128]{1,0:T(8,128)(2,1)S(1)} %get-tuple-element.55), channel_id=1, source_target_pairs={{0,8},{4,12},{8,0},{12,4},{16,24},{20,28},{24,16},{28,20},{1,9},{5... | collective-permute-start | bytes 344072 | tf_op jit(solution)/shard_map/ppermute | solution.py:518
  30.1 1.3 %collective-permute-start.12 = (bf16[320,128]{1,0:T(8,128)(2,1)S(1)}, bf16[320,128]{1,0:T(8,128)(2,1)S(1)}, u32[]{:S(2)}, u32[]{:S(2)}) collective-permute-start(bf16[320,128]{1,0:T(8,128)(2,1)S(1)} %shard_map.111), channel_id=1, source_target_pairs={{0,1},{1,0},{2,3},{3,2},{4,5},{5,4},{6,7},{7,6},{8,9},{9,8},{10,11... | collective-permute-start | bytes 245768 | tf_op jit(solution)/shard_map/ppermute | solution.py:518

commit v7 on v6

--- a/solution.py
+++ b/solution.py
@@ -85,20 +85,21 @@
     x, wq, wk, wv = refs[:4]
     refs = refs[4:]
     if half:
-        length, early, o0, o1, o2, o3 = refs[:6]
+        length, early, conv, o0, o1, o2, o3, taps = refs[:8]
+        refs = refs[8:]
+    else:
+        o0, o1, o2, o3, early, x_v = refs[:6]
         refs = refs[6:]
-    else:
-        o0, o1, o2, o3, early = refs[:5]
-        refs = refs[5:]
-    rows = x.shape[1]
+    rows = early.shape[1]
     width = wv.shape[1] // 2
     keyed = wq.shape[1] // 2
     place = lax.axis_index("blk")
     mine = lax.rem(place, GROUP)
     slab = width // GROUP
     if half:
-        vt, qkt = refs
-        inputs = x[0]
+        vt, qkt, taps_v = refs
+        inputs = x[...]
+        own_taps(conv, mine, taps, taps_v)
         both = jnp.concatenate([wk[:, keyed:], wq[:, keyed:]], 1)
         qkt[...] = dot(inputs, both).T.astype(bf16)
         at = 0
@@ -107,7 +108,7 @@
             vt[at : at + tile, :] = dot(inputs, weights).T.astype(bf16)
             at += tile
     else:
-        vt, qkt, x_v, wqk_v, wv_v, sems = refs
+        vt, qkt, wqk_v, wv_v, sems = refs
         first, second = pl.ds(0, keyed), pl.ds(keyed, keyed)
         needed = [
             pltpu.make_async_copy(x.at[0], x_v, sems.at[0]),
@@ -148,15 +149,18 @@
 
 
 def project(half, x, wq, wk, wv, *others):
-    _, rows, width = x.shape
+    rows, width = x.shape[-2:]
     keyed = wq.shape[1]
     total = (width + 2 * keyed) // GROUP // 2 + (2 * FEAT if half else 0)
     outs = [((total, rows), bf16)] * GROUP
     scratch = [pltpu.VMEM((width // 2, rows), bf16), pltpu.VMEM((keyed, rows), bf16)]
-    if not half:
-        outs.append(((keyed // 2, rows), bf16))
+    if half:
+        slab = width // GROUP
+        outs.append(((slab, 8), f32))
+        scratch.append(pltpu.VMEM(((slab // 2 // LANES + 2) * LANES, 8), f32))
+    else:
+        outs += [((keyed // 2, rows), bf16), ((rows, width), bf16)]
         scratch += [
-            pltpu.VMEM((rows, width), bf16),
             pltpu.VMEM((width, keyed), bf16),
             pltpu.VMEM((width, width // 2), bf16),
             pltpu.SemaphoreType.DMA((3 + len(TILES),)),
@@ -168,7 +172,7 @@
     return call(kernel, outs, scratch, limit, flops, flops // rows, args, [] if half else [pltpu.HBM] * 4)
 
 
-LIMIT_A = 53.6
+LIMIT_A = 53.1
 LIMIT_B = 16
 
 
@@ -189,11 +193,7 @@
 
 def state_kernel(half, *refs):
     length, p0, p1, p2, p3 = refs[:5]
-    if half:
-        taps, aug, qk, state, held = refs[5:]
-    else:
-        conv, aug, qk, state, taps, held, taps_v = refs[5:]
-        own_taps(conv, lax.rem(lax.axis_index("blk"), GROUP), taps, taps_v)
+    taps, aug, qk, state, held = refs[5:]
     rows = p0.shape[1]
     place = lax.axis_index("blk")
     mine, group = lax.rem(place, GROUP), place // GROUP
@@ -259,10 +259,6 @@
         (((total - extra) // LOCAL * LOCAL + extra, LANES), bf16),
     ]
     scratch = [pltpu.VMEM((GROUP, total - extra, rows), bf16)]
-    if not half:
-        slab = taps.shape[1] // GROUP
-        outs.append(((slab, 8), f32))
-        scratch.append(pltpu.VMEM(((slab // 2 // LANES + 2) * LANES, 8), f32))
     kernel = functools.partial(state_kernel, half)
     args = [length, *payloads, taps]
     return call(kernel, outs, scratch, 32, 100_000_000, 1_000_000, args, after=after)
@@ -524,11 +520,11 @@
     width = tokens_in.shape[2]
     given = (tokens_in, query_weight, key_weight, value_weight)
     length, slot = prompt_lengths.reshape(1, 1), decode_map
-    *parts, early = project(0, *given)
+    *parts, early, inputs = project(0, *given)
     sent = [across(parts, ORDER)]
-    parts = project(1, *given, length, early)
+    *parts, taps = project(1, inputs, *given[1:], length, early, conv_weight)
     sent.append(across(parts, ORDER))
-    *first, taps = group_state(0, length, sent[0], conv_weight, [])
+    first = group_state(0, length, sent[0], taps, [])
     second = group_state(1, length, sent[1], taps, [first[2]])
     got = [swap(held[2], "blk", GROUP) for held in (first, second)]
     aug, qk, own = first

time: 35.4 us -> 35.1 us (level)
  transfers between devices with their start and end apart: 13 -> 13, of which waited for: 4 -> 4; matrix products, arithmetic and copies ran while one was open for 0% -> 0% of each run, Pallas kernels for 18% -> 17%
where the time goes in v7:
time: 35.1 us; the launch traced here: 34.9 us
  starting transfers between devices  18.9 us (54%)
  Pallas kernels  10.7 us (30%)
  waiting for transfers between devices  3.24 us (9%)
  between operations  2.08 us (6%)
    ppermute x13, starting transfers between devices, swap(): lax.ppermute(array, axis, [(i, i ^ by) for i in range(lax.axis_size(axis))])  18.9 us
    pallas_call x10, Pallas kernels, call(): pl.pallas_call(kernel, out_shape=[jax.ShapeDtypeStruct(shape, dtype) for...  9.77 us
    ppermute x13, waiting for transfers between devices, swap(): lax.ppermute(array, axis, [(i, i ^ by) for i in range(lax.axis_size(axis))])  3.24 us
    pallas_call x1, Pallas kernels, place_tokens(): pl.pallas_call(kernel, out_shape=jax.ShapeDtypeStruct((1, rows, width), b...  0.93 us
  transfers between devices with their start and end apart: 13, of which 4 were waited for; matrix products, arithmetic and copies ran while one was open for 0% of the time, Pallas kernels for 17%

profile of v7, /device:TPU:0, one launch (start us, length us, event | category | flops | bytes accessed | tf_op | source)
XLA Modules:
  0.0 34.9 jit_solution(18090827794346348416)
XLA Ops:
  0.7 3.0 %shard_map.103 = (bf16[288,128]{1,0:T(8,128)(2,1)S(1)}, bf16[288,128]{1,0:T(8,128)(2,1)S(1)}, bf16[288,128]{1,0:T(8,128)(2,1)S(1)}, bf16[288,128]{1,0:T(8,128)(2...) custom-call(bf16[1,128,1792]{2,1,0:T(8,128)(2,1)} %refs_0_.2, bf16[1792,256]{1,0:T(8,128)(2,1)} %refs_1_.3, ...), custom_call_target="tpu_custom_call" | custom-call | flops 528482304 | bytes 4128768 | tf_op jit(solution)/shard_map/pallas_call | solution.py:55
  3.7 4.1 %collective-permute-start.3 = (bf16[288,128]{1,0:T(8,128)(2,1)S(1)}, bf16[288,128]{1,0:T(8,128)(2,1)S(1)}, u32[]{:S(2)}, u32[]{:S(2)}) collective-permute-start(bf16[288,128]{1,0:T(8,128)(2,1)S(1)} %get-tuple-element.40), channel_id=1, source_target_pairs={{0,12},{4,8},{8,4},{12,0},{16,28},{20,24},{24,20},{28,16},{1,13},{... | collective-permute-start | bytes 221192 | tf_op jit(solution)/shard_map/ppermute | solution.py:514
  7.8 0.4 %collective-permute-start.4 = (bf16[288,128]{1,0:T(8,128)(2,1)S(1)}, bf16[288,128]{1,0:T(8,128)(2,1)S(1)}, u32[]{:S(2)}, u32[]{:S(2)}) collective-permute-start(bf16[288,128]{1,0:T(8,128)(2,1)S(1)} %get-tuple-element.41), channel_id=1, source_target_pairs={{0,8},{4,12},{8,0},{12,4},{16,24},{20,28},{24,16},{28,20},{1,9},{5... | collective-permute-start | bytes 221192 | tf_op jit(solution)/shard_map/ppermute | solution.py:514
  9.1 1.1 %shard_map.104 = (bf16[320,128]{1,0:T(8,128)(2,1)S(1)}, bf16[320,128]{1,0:T(8,128)(2,1)S(1)}, bf16[320,128]{1,0:T(8,128)(2,1)S(1)}, bf16[320,128]{1,0:T(8,128)(2,1)S(1)}, f32[448,8]{1,0:T(8,128)S(1)}) custom-call(bf16[128,1792]{1,0:T(8,128)(2,1)S(1)} %get-tuple-element.32.refs_0_, bf16[1792,256]{1,0:T(8,128)(2,1)S(1)} %copy-done.1, ...), custom_call_target="tpu_custom_call" | custom-call | flops 528482304 | bytes 4128768 | tf_op jit(solution)/shard_map/pallas_call | solution.py:55
  10.2 2.9 %collective-permute-start = (bf16[320,128]{1,0:T(8,128)(2,1)S(1)}, bf16[320,128]{1,0:T(8,128)(2,1)S(1)}, u32[]{:S(2)}, u32[]{:S(2)}) collective-permute-start(bf16[320,128]{1,0:T(8,128)(2,1)S(1)} %get-tuple-element.35), channel_id=1, source_target_pairs={{0,12},{4,8},{8,4},{12,0},{16,28},{20,24},{24,20},{28,16},{1,13},{... | collective-permute-start | bytes 245768 | tf_op jit(solution)/shard_map/ppermute | solution.py:514
  13.0 0.4 %collective-permute-start.1 = (bf16[320,128]{1,0:T(8,128)(2,1)S(1)}, bf16[320,128]{1,0:T(8,128)(2,1)S(1)}, u32[]{:S(2)}, u32[]{:S(2)}) collective-permute-start(bf16[320,128]{1,0:T(8,128)(2,1)S(1)} %get-tuple-element.36), channel_id=1, source_target_pairs={{0,8},{4,12},{8,0},{12,4},{16,24},{20,28},{24,16},{28,20},{1,9},{5... | collective-permute-start | bytes 245768 | tf_op jit(solution)/shard_map/ppermute | solution.py:514
  13.5 0.2 collective-permute-start.2
  13.7 0.6 %shard_map.105 = (bf16[2,128,512]{2,1,0:T(8,128)(2,1)S(1)}, bf16[64,512]{1,0:T(8,128)(2,1)S(1)}, bf16[288,128]{1,0:T(8,128)(2,1)S(1)}) custom-call(s32[1,1]{1,0:T(1,128)} %bitcast.4.refs_0_, bf16[288,128]{1,0:T(8,128)(2,1)S(1)} %get-tuple-element.39.refs_1_, bf16[288,128]{1,0:T(8,128)(2,1)S(1)} %collective-permute-done.3.refs_2_, ...), custom_call_target="tpu_custom_call" | custom-call | flops 100000000 | bytes 1000000 | tf_op jit(solution)/shard_map/pallas_call | solution.py:55
  14.3 2.9 %collective-permute-start.6 = (bf16[288,128]{1,0:T(8,128)(2,1)S(1)}, bf16[288,128]{1,0:T(8,128)(2,1)S(1)}, u32[]{:S(2)}, u32[]{:S(2)}) collective-permute-start(bf16[288,128]{1,0:T(8,128)(2,1)S(1)} %get-tuple-element.43.refs_6_.refs_2_), channel_id=1, source_target_pairs={{0,16},{4,20},{8,24},{12,28},{16,0},{20,4},{24,8},{28,12},{1,17},{... | collective-permute-start | bytes 221192 | tf_op jit(solution)/shard_map/ppermute | solution.py:514
  17.9 0.6 %shard_map.106 = (bf16[2,128,512]{2,1,0:T(8,128)(2,1)S(1)}, bf16[64,512]{1,0:T(8,128)(2,1)S(1)}, bf16[320,128]{1,0:T(8,128)(2,1)S(1)}) custom-call(s32[1,1]{1,0:T(1,128)} %bitcast.5.refs_0_, bf16[320,128]{1,0:T(8,128)(2,1)S(1)} %get-tuple-element.34.refs_1_, bf16[320,128]{1,0:T(8,128)(2,1)S(1)} %collective-permute-done.refs_2_, ...), custom_call_target="tpu_custom_call" | custom-call | flops 100000000 | bytes 1000000 | tf_op jit(solution)/shard_map/pallas_call | solution.py:55
  18.5 2.6 %collective-permute-start.7 = (bf16[320,128]{1,0:T(8,128)(2,1)S(1)}, bf16[320,128]{1,0:T(8,128)(2,1)S(1)}, u32[]{:S(2)}, u32[]{:S(2)}) collective-permute-start(bf16[320,128]{1,0:T(8,128)(2,1)S(1)} %get-tuple-element.48.refs_2_.refs_3_), channel_id=1, source_target_pairs={{0,16},{4,20},{8,24},{12,28},{16,0},{20,4},{24,8},{28,12},{1,17},{... | collective-permute-start | bytes 245768 | tf_op jit(solution)/shard_map/ppermute | solution.py:514
  21.1 0.9 %shard_map.107.refs_1_ = f32[2,128,512]{2,1,0:T(8,128)S(1)} custom-call(bf16[2,128,512]{2,1,0:T(8,128)(2,1)S(1)} %get-tuple-element.46.refs_0_, bf16[64,512]{1,0:T(8,128)(2,1)S(1)} %get-tuple-element.47.refs_1_.refs_4_, bf16[320,128]{1,0:T(8,128)(2,1)S(1)} %get-tuple-element.48.refs_2_.refs_3_), custom_call_target="tpu_custom_call" | custom-call | flops 1000 | bytes 1000 | tf_op jit(solution)/shard_map/pallas_call | solution.py:55
  22.1 0.7 %shard_map.108 = (bf16[224,128]{1,0:T(8,128)(2,1)S(1)}, bf16[224,128]{1,0:T(8,128)(2,1)S(1)}, bf16[224,128]{1,0:T(8,128)(2,1)S(1)}, bf16[224,128]{1,0:T(8,128)(2,1)S(1)}, bf16[288,128]{1,0:T(8,128)(2,1)S(1)}) custom-call(s32[1,1]{1,0:T(1,128)} %bitcast.6.refs_0_, f32[2,128,512]{2,1,0:T(8,128)S(1)} %shard_map.107.refs_1_, ...), custom_call_target="tpu_custom_call" | custom-call | flops 50000000 | bytes 20000000 | tf_op jit(solution)/shard_map/pallas_call | solution.py:55
  22.8 0.9 %shard_map.109.refs_2_ = f32[2,128,512]{2,1,0:T(8,128)S(1)} custom-call(bf16[2,128,512]{2,1,0:T(8,128)(2,1)S(1)} %get-tuple-element.44.refs_0_, bf16[64,512]{1,0:T(8,128)(2,1)S(1)} %get-tuple-element.45.refs_1_.refs_5_, bf16[288,128]{1,0:T(8,128)(2,1)S(1)} %get-tuple-element.49.refs_2_.refs_7_), custom_call_target="tpu_custom_call" | custom-call | flops 5000000000 | bytes 1000 | tf_op jit(solution)/shard_map/pallas_call | solution.py:55
  23.9 0.7 %shard_map.110 = (bf16[448,128]{1,0:T(8,128)(2,1)S(1)}, bf16[448,128]{1,0:T(8,128)(2,1)S(1)}, bf16[448,128]{1,0:T(8,128)(2,1)S(1)}, bf16[448,128]{1,0:T(8,128)(2,1)S(1)}, bf16[320,128]{1,0:T(8,128)(2,1)S(1)}) custom-call(s32[1]{0:T(128)S(6)} %copy.12.refs_0_, s32[1,1]{1,0:T(1,128)} %bitcast.7.refs_1_, f32[2,128,512]{2,1,0:T(8,128)S(1)} %shard_map.109.refs_2_, ...), custom_call_target="tpu_custom_call" | custom-call | flops 50000000 | bytes 20000000 | tf_op jit(solution)/shard_map/pallas_call | solution.py:55
  24.6 1.6 %collective-permute-start.11 = (bf16[320,128]{1,0:T(8,128)(2,1)S(1)}, bf16[320,128]{1,0:T(8,128)(2,1)S(1)}, u32[]{:S(2)}, u32[]{:S(2)}) collective-permute-start(bf16[320,128]{1,0:T(8,128)(2,1)S(1)} %get-tuple-element.58.own.c0), channel_id=1, source_target_pairs={{0,2},{1,3},{2,0},{3,1},{4,6},{5,7},{6,4},{7,5},{8,10},{9,11},{10,... | collective-permute-start | bytes 245768 | tf_op jit(solution)/shard_map/ppermute | solution.py:514
  26.2 2.5 %collective-permute-start.8 = (bf16[448,128]{1,0:T(8,128)(2,1)S(1)}, bf16[448,128]{1,0:T(8,128)(2,1)S(1)}, u32[]{:S(2)}, u32[]{:S(2)}) collective-permute-start(bf16[448,128]{1,0:T(8,128)(2,1)S(1)} %get-tuple-element.55), channel_id=1, source_target_pairs={{0,12},{4,8},{8,4},{12,0},{16,28},{20,24},{24,20},{28,16},{1,13},{... | collective-permute-start | bytes 344072 | tf_op jit(solution)/shard_map/ppermute | solution.py:514
  28.7 0.5 %collective-permute-start.9 = (bf16[448,128]{1,0:T(8,128)(2,1)S(1)}, bf16[448,128]{1,0:T(8,128)(2,1)S(1)}, u32[]{:S(2)}, u32[]{:S(2)}) collective-permute-start(bf16[448,128]{1,0:T(8,128)(2,1)S(1)} %get-tuple-element.56), channel_id=1, source_target_pairs={{0,4},{4,0},{8,12},{12,8},{16,20},{20,16},{24,28},{28,24},{1,5},{5... | collective-permute-start | bytes 344072 | tf_op jit(solution)/shard_map/ppermute | solution.py:514
  29.2 0.4 %collective-permute-start.10 = (bf16[448,128]{1,0:T(8,128)(2,1)S(1)}, bf16[448,128]{1,0:T(8,128)(2,1)S(1)}, u32[]{:S(2)}, u32[]{:S(2)}) collective-permute-start(bf16[448,128]{1,0:T(8,128)(2,1)S(1)} %get-tuple-element.57), channel_id=1, source_target_pairs={{0,8},{4,12},{8,0},{12,4},{16,24},{20,28},{24,16},{28,20},{1,9},{5... | collective-permute-start | bytes 344072 | tf_op jit(solution)/shard_map/ppermute | solution.py:514
  29.8 1.3 %collective-permute-done.12.refs_4_.c2 = bf16[320,128]{1,0:T(8,128)(2,1)S(1)} collective-permute-done((bf16[320,128]{1,0:T(8,128)(2,1)S(1)}, bf16[320,128]{1,0:T(8,128)(2,1)S(1)}, u32[]{:S(2)}, u32[]{:S(2)}) %collective-permute-start.12) | collective-permute-done | bytes 81952 | tf_op jit(solution)/shard_map/ppermute | solution.py:514
  31.1 1.1 %shard_map.113 = (f32[273,1,224]{2,1,0:T(1,128)}, f32[1,16,273]{2,1,0:T(8,128)}) custom-call(bf16[320,128]{1,0:T(8,128)(2,1)S(1)} %get-tuple-element.58.own.c0, bf16[320,128]{1,0:T(8,128)(2,1)S(1)} %collective-permute-done.11.got.c1, bf16[320,128]{1,0:T(8,128)(2,1)S(1)} %collective-permute-done.12.refs_4_.c2, bf16[273,160]{1,0:T(8,128)(2,1)S(1)} %copy-done.3), custom_call_target="tpu_custom_call" | custom-call | flops 40000000 | bytes 1000000 | tf_op jit(solution)/shard_map/pallas_call | solution.py:55
  32.2 1.3 %collective-permute-done.9.refs_2_ = bf16[448,128]{1,0:T(8,128)(2,1)S(1)} collective-permute-done((bf16[448,128]{1,0:T(8,128)(2,1)S(1)}, bf16[448,128]{1,0:T(8,128)(2,1)S(1)}, u32[]{:S(2)}, u32[]{:S(2)}) %collective-permute-start.9) | collective-permute-done | bytes 114720 | tf_op jit(solution)/shard_map/ppermute | solution.py:514
  33.5 0.5 %collective-permute-done.10.refs_3_ = bf16[448,128]{1,0:T(8,128)(2,1)S(1)} collective-permute-done((bf16[448,128]{1,0:T(8,128)(2,1)S(1)}, bf16[448,128]{1,0:T(8,128)(2,1)S(1)}, u32[]{:S(2)}, u32[]{:S(2)}) %collective-permute-start.10) | collective-permute-done | bytes 114720 | tf_op jit(solution)/shard_map/ppermute | solution.py:514
  34.0 0.9 %shard_map.112 = bf16[1,128,1792]{2,1,0:T(8,128)(2,1)} custom-call(bf16[448,128]{1,0:T(8,128)(2,1)S(1)} %get-tuple-element.54.refs_0_, bf16[448,128]{1,0:T(8,128)(2,1)S(1)} %collective-permute-done.8.refs_1_, bf16[448,128]{1,0:T(8,128)(2,1)S(1)} %collective-permute-done.9.refs_2_, bf16[448,128]{1,0:T(8,128)(2,1)S(1)} %collective-permute-done.10.refs_3_, ...), custom_call_target="tpu_custom_call" | custom-call | flops 1000 | bytes 1000000 | tf_op jit(solution)/shard_map/pallas_call | solution.py:418
  (23 shorter events, 0.5 us)
Async XLA Ops:
  0.6 8.4 %copy-start = (bf16[1792,1792]{1,0:T(8,128)(2,1)S(1)}, bf16[1792,1792]{1,0:T(8,128)(2,1)}, u32[]{:S(2)}) copy-start(bf16[1792,1792]{1,0:T(8,128)(2,1)} %refs_3_.3) | copy-start | bytes 19267588
  0.6 8.4 %copy-start.2 = (bf16[1792,256]{1,0:T(8,128)(2,1)S(1)}, bf16[1792,256]{1,0:T(8,128)(2,1)}, u32[]{:S(2)}) copy-start(bf16[1792,256]{1,0:T(8,128)(2,1)} %refs_2_.3) | copy-start | bytes 2752516
  0.7 8.4 %copy-start.1 = (bf16[1792,256]{1,0:T(8,128)(2,1)S(1)}, bf16[1792,256]{1,0:T(8,128)(2,1)}, u32[]{:S(2)}) copy-start(bf16[1792,256]{1,0:T(8,128)(2,1)} %refs_1_.3) | copy-start | bytes 2752516
  0.7 8.4 %copy-start.4 = (f32[3,1792]{1,0:T(4,128)S(1)}, f32[3,1792]{1,0:T(4,128)}, u32[]{:S(2)}) copy-start(f32[3,1792]{1,0:T(4,128)} %refs_6_.1) | copy-start | bytes 64516
  3.7 9.7 %collective-permute-start.3 = (bf16[288,128]{1,0:T(8,128)(2,1)S(1)}, bf16[288,128]{1,0:T(8,128)(2,1)S(1)}, u32[]{:S(2)}, u32[]{:S(2)}) collective-permute-start(bf16[288,128]{1,0:T(8,128)(2,1)S(1)} %get-tuple-element.40), channel_id=1, source_target_pairs={{0,12},{4,8},{8,4},{12,0},{16,28},{20,24},{24,20},{28,16},{1,13},{... | collective-permute-start | bytes 221192 | tf_op jit(solution)/shard_map/ppermute | solution.py:514
  7.8 5.9 %collective-permute-start.4 = (bf16[288,128]{1,0:T(8,128)(2,1)S(1)}, bf16[288,128]{1,0:T(8,128)(2,1)S(1)}, u32[]{:S(2)}, u32[]{:S(2)}) collective-permute-start(bf16[288,128]{1,0:T(8,128)(2,1)S(1)} %get-tuple-element.41), channel_id=1, source_target_pairs={{0,8},{4,12},{8,0},{12,4},{16,24},{20,28},{24,16},{28,20},{1,9},{5... | collective-permute-start | bytes 221192 | tf_op jit(solution)/shard_map/ppermute | solution.py:514
  8.2 5.5 %collective-permute-start.5 = (bf16[288,128]{1,0:T(8,128)(2,1)S(1)}, bf16[288,128]{1,0:T(8,128)(2,1)S(1)}, u32[]{:S(2)}, u32[]{:S(2)}) collective-permute-start(bf16[288,128]{1,0:T(8,128)(2,1)S(1)} %get-tuple-element.42), channel_id=1, source_target_pairs={{0,4},{4,0},{8,12},{12,8},{16,20},{20,16},{24,28},{28,24},{1,5},{5... | collective-permute-start | bytes 221192 | tf_op jit(solution)/shard_map/ppermute | solution.py:514
  10.2 7.7 %collective-permute-start = (bf16[320,128]{1,0:T(8,128)(2,1)S(1)}, bf16[320,128]{1,0:T(8,128)(2,1)S(1)}, u32[]{:S(2)}, u32[]{:S(2)}) collective-permute-start(bf16[320,128]{1,0:T(8,128)(2,1)S(1)} %get-tuple-element.35), channel_id=1, source_target_pairs={{0,12},{4,8},{8,4},{12,0},{16,28},{20,24},{24,20},{28,16},{1,13},{... | collective-permute-start | bytes 245768 | tf_op jit(solution)/shard_map/ppermute | solution.py:514
  13.0 4.9 %collective-permute-start.1 = (bf16[320,128]{1,0:T(8,128)(2,1)S(1)}, bf16[320,128]{1,0:T(8,128)(2,1)S(1)}, u32[]{:S(2)}, u32[]{:S(2)}) collective-permute-start(bf16[320,128]{1,0:T(8,128)(2,1)S(1)} %get-tuple-element.36), channel_id=1, source_target_pairs={{0,8},{4,12},{8,0},{12,4},{16,24},{20,28},{24,16},{28,20},{1,9},{5... | collective-permute-start | bytes 245768 | tf_op jit(solution)/shard_map/ppermute | solution.py:514
  13.5 4.4 %collective-permute-start.2 = (bf16[320,128]{1,0:T(8,128)(2,1)S(1)}, bf16[320,128]{1,0:T(8,128)(2,1)S(1)}, u32[]{:S(2)}, u32[]{:S(2)}) collective-permute-start(bf16[320,128]{1,0:T(8,128)(2,1)S(1)} %get-tuple-element.37), channel_id=1, source_target_pairs={{0,4},{4,0},{8,12},{12,8},{16,20},{20,16},{24,28},{28,24},{1,5},{5... | collective-permute-start | bytes 245768 | tf_op jit(solution)/shard_map/ppermute | solution.py:514
  14.3 7.8 %collective-permute-start.6 = (bf16[288,128]{1,0:T(8,128)(2,1)S(1)}, bf16[288,128]{1,0:T(8,128)(2,1)S(1)}, u32[]{:S(2)}, u32[]{:S(2)}) collective-permute-start(bf16[288,128]{1,0:T(8,128)(2,1)S(1)} %get-tuple-element.43.refs_6_.refs_2_), channel_id=1, source_target_pairs={{0,16},{4,20},{8,24},{12,28},{16,0},{20,4},{24,8},{28,12},{1,17},{... | collective-permute-start | bytes 221192 | tf_op jit(solution)/shard_map/ppermute | solution.py:514
  18.5 5.4 %collective-permute-start.7 = (bf16[320,128]{1,0:T(8,128)(2,1)S(1)}, bf16[320,128]{1,0:T(8,128)(2,1)S(1)}, u32[]{:S(2)}, u32[]{:S(2)}) collective-permute-start(bf16[320,128]{1,0:T(8,128)(2,1)S(1)} %get-tuple-element.48.refs_2_.refs_3_), channel_id=1, source_target_pairs={{0,16},{4,20},{8,24},{12,28},{16,0},{20,4},{24,8},{28,12},{1,17},{... | collective-permute-start | bytes 245768 | tf_op jit(solution)/shard_map/ppermute | solution.py:514
  22.8 8.3 %copy-start.3 = (bf16[273,160]{1,0:T(8,128)(2,1)S(1)}, bf16[273,160]{1,0:T(8,128)(2,1)}, u32[]{:S(2)}) copy-start(bf16[273,160]{1,0:T(8,128)(2,1)} %constant.2.clone.spread) | copy-start | bytes 262084
  24.6 5.1 %collective-permute-start.11 = (bf16[320,128]{1,0:T(8,128)(2,1)S(1)}, bf16[320,128]{1,0:T(8,128)(2,1)S(1)}, u32[]{:S(2)}, u32[]{:S(2)}) collective-permute-start(bf16[320,128]{1,0:T(8,128)(2,1)S(1)} %get-tuple-element.58.own.c0), channel_id=1, source_target_pairs={{0,2},{1,3},{2,0},{3,1},{4,6},{5,7},{6,4},{7,5},{8,10},{9,11},{10,... | collective-permute-start | bytes 245768 | tf_op jit(solution)/shard_map/ppermute | solution.py:514
  26.2 6.0 %collective-permute-start.8 = (bf16[448,128]{1,0:T(8,128)(2,1)S(1)}, bf16[448,128]{1,0:T(8,128)(2,1)S(1)}, u32[]{:S(2)}, u32[]{:S(2)}) collective-permute-start(bf16[448,128]{1,0:T(8,128)(2,1)S(1)} %get-tuple-element.55), channel_id=1, source_target_pairs={{0,12},{4,8},{8,4},{12,0},{16,28},{20,24},{24,20},{28,16},{1,13},{... | collective-permute-start | bytes 344072 | tf_op jit(solution)/shard_map/ppermute | solution.py:514
  28.7 4.8 %collective-permute-start.9 = (bf16[448,128]{1,0:T(8,128)(2,1)S(1)}, bf16[448,128]{1,0:T(8,128)(2,1)S(1)}, u32[]{:S(2)}, u32[]{:S(2)}) collective-permute-start(bf16[448,128]{1,0:T(8,128)(2,1)S(1)} %get-tuple-element.56), channel_id=1, source_target_pairs={{0,4},{4,0},{8,12},{12,8},{16,20},{20,16},{24,28},{28,24},{1,5},{5... | collective-permute-start | bytes 344072 | tf_op jit(solution)/shard_map/ppermute | solution.py:514
  29.2 4.8 %collective-permute-start.10 = (bf16[448,128]{1,0:T(8,128)(2,1)S(1)}, bf16[448,128]{1,0:T(8,128)(2,1)S(1)}, u32[]{:S(2)}, u32[]{:S(2)}) collective-permute-start(bf16[448,128]{1,0:T(8,128)(2,1)S(1)} %get-tuple-element.57), channel_id=1, source_target_pairs={{0,8},{4,12},{8,0},{12,4},{16,24},{20,28},{24,16},{28,20},{1,9},{5... | collective-permute-start | bytes 344072 | tf_op jit(solution)/shard_map/ppermute | solution.py:514
  29.8 1.3 %collective-permute-start.12 = (bf16[320,128]{1,0:T(8,128)(2,1)S(1)}, bf16[320,128]{1,0:T(8,128)(2,1)S(1)}, u32[]{:S(2)}, u32[]{:S(2)}) collective-permute-start(bf16[320,128]{1,0:T(8,128)(2,1)S(1)} %shard_map.111), channel_id=1, source_target_pairs={{0,1},{1,0},{2,3},{3,2},{4,5},{5,4},{6,7},{7,6},{8,9},{9,8},{10,11... | collective-permute-start | bytes 245768 | tf_op jit(solution)/shard_map/ppermute | solution.py:514

commit v8 on v7

--- a/solution.py
+++ b/solution.py
@@ -21,7 +21,7 @@
 INFO = 31
 LOCAL = HEADS // GROUP // 2
 ORDER = (0, 3, 2, 1)
-RETURN = (0, 3, 1, 2)
+RETURN = (0, 3, 2, 1)
 f32 = jnp.float32
 bf16 = jnp.bfloat16
 NT = (((1,), (1,)), ((), ()))

time: 35.1 us -> 35 us (level)
  no operation moved by 1% of the time
where the time goes in v8:
time: 35 us; the launch traced here: 34.8 us
  starting transfers between devices  18.9 us (54%)
  Pallas kernels  10.7 us (31%)
  waiting for transfers between devices  3.12 us (9%)
  between operations  2.08 us (6%)
    ppermute x13, starting transfers between devices, swap(): lax.ppermute(array, axis, [(i, i ^ by) for i in range(lax.axis_size(axis))])  18.9 us
    pallas_call x10, Pallas kernels, call(): pl.pallas_call(kernel, out_shape=[jax.ShapeDtypeStruct(shape, dtype) for...  9.77 us
    ppermute x13, waiting for transfers between devices, swap(): lax.ppermute(array, axis, [(i, i ^ by) for i in range(lax.axis_size(axis))])  3.12 us
    pallas_call x1, Pallas kernels, place_tokens(): pl.pallas_call(kernel, out_shape=jax.ShapeDtypeStruct((1, rows, width), b...  0.93 us
  transfers between devices with their start and end apart: 13, of which 4 were waited for; matrix products, arithmetic and copies ran while one was open for 0% of the time, Pallas kernels for 17%

profile of v8, /device:TPU:0, one launch (start us, length us, event | category | flops | bytes accessed | tf_op | source)
XLA Modules:
  0.0 34.8 jit_solution(8612177442975554930)
XLA Ops:
  0.7 3.0 %shard_map.103 = (bf16[288,128]{1,0:T(8,128)(2,1)S(1)}, bf16[288,128]{1,0:T(8,128)(2,1)S(1)}, bf16[288,128]{1,0:T(8,128)(2,1)S(1)}, bf16[288,128]{1,0:T(8,128)(2...) custom-call(bf16[1,128,1792]{2,1,0:T(8,128)(2,1)} %refs_0_.2, bf16[1792,256]{1,0:T(8,128)(2,1)} %refs_1_.3, ...), custom_call_target="tpu_custom_call" | custom-call | flops 528482304 | bytes 4128768 | tf_op jit(solution)/shard_map/pallas_call | solution.py:55
  3.7 4.1 %collective-permute-start.3 = (bf16[288,128]{1,0:T(8,128)(2,1)S(1)}, bf16[288,128]{1,0:T(8,128)(2,1)S(1)}, u32[]{:S(2)}, u32[]{:S(2)}) collective-permute-start(bf16[288,128]{1,0:T(8,128)(2,1)S(1)} %get-tuple-element.40), channel_id=1, source_target_pairs={{0,12},{4,8},{8,4},{12,0},{16,28},{20,24},{24,20},{28,16},{1,13},{... | collective-permute-start | bytes 221192 | tf_op jit(solution)/shard_map/ppermute | solution.py:514
  7.8 0.4 %collective-permute-start.4 = (bf16[288,128]{1,0:T(8,128)(2,1)S(1)}, bf16[288,128]{1,0:T(8,128)(2,1)S(1)}, u32[]{:S(2)}, u32[]{:S(2)}) collective-permute-start(bf16[288,128]{1,0:T(8,128)(2,1)S(1)} %get-tuple-element.41), channel_id=1, source_target_pairs={{0,8},{4,12},{8,0},{12,4},{16,24},{20,28},{24,16},{28,20},{1,9},{5... | collective-permute-start | bytes 221192 | tf_op jit(solution)/shard_map/ppermute | solution.py:514
  9.1 1.1 %shard_map.104 = (bf16[320,128]{1,0:T(8,128)(2,1)S(1)}, bf16[320,128]{1,0:T(8,128)(2,1)S(1)}, bf16[320,128]{1,0:T(8,128)(2,1)S(1)}, bf16[320,128]{1,0:T(8,128)(2,1)S(1)}, f32[448,8]{1,0:T(8,128)S(1)}) custom-call(bf16[128,1792]{1,0:T(8,128)(2,1)S(1)} %get-tuple-element.32.refs_0_, bf16[1792,256]{1,0:T(8,128)(2,1)S(1)} %copy-done.1, ...), custom_call_target="tpu_custom_call" | custom-call | flops 528482304 | bytes 4128768 | tf_op jit(solution)/shard_map/pallas_call | solution.py:55
  10.2 2.9 %collective-permute-start = (bf16[320,128]{1,0:T(8,128)(2,1)S(1)}, bf16[320,128]{1,0:T(8,128)(2,1)S(1)}, u32[]{:S(2)}, u32[]{:S(2)}) collective-permute-start(bf16[320,128]{1,0:T(8,128)(2,1)S(1)} %get-tuple-element.35), channel_id=1, source_target_pairs={{0,12},{4,8},{8,4},{12,0},{16,28},{20,24},{24,20},{28,16},{1,13},{... | collective-permute-start | bytes 245768 | tf_op jit(solution)/shard_map/ppermute | solution.py:514
  13.0 0.4 %collective-permute-start.1 = (bf16[320,128]{1,0:T(8,128)(2,1)S(1)}, bf16[320,128]{1,0:T(8,128)(2,1)S(1)}, u32[]{:S(2)}, u32[]{:S(2)}) collective-permute-start(bf16[320,128]{1,0:T(8,128)(2,1)S(1)} %get-tuple-element.36), channel_id=1, source_target_pairs={{0,8},{4,12},{8,0},{12,4},{16,24},{20,28},{24,16},{28,20},{1,9},{5... | collective-permute-start | bytes 245768 | tf_op jit(solution)/shard_map/ppermute | solution.py:514
  13.5 0.2 collective-permute-start.2
  13.7 0.6 %shard_map.105 = (bf16[2,128,512]{2,1,0:T(8,128)(2,1)S(1)}, bf16[64,512]{1,0:T(8,128)(2,1)S(1)}, bf16[288,128]{1,0:T(8,128)(2,1)S(1)}) custom-call(s32[1,1]{1,0:T(1,128)} %bitcast.4.refs_0_, bf16[288,128]{1,0:T(8,128)(2,1)S(1)} %get-tuple-element.39.refs_1_, bf16[288,128]{1,0:T(8,128)(2,1)S(1)} %collective-permute-done.3.refs_2_, ...), custom_call_target="tpu_custom_call" | custom-call | flops 100000000 | bytes 1000000 | tf_op jit(solution)/shard_map/pallas_call | solution.py:55
  14.3 2.9 %collective-permute-start.6 = (bf16[288,128]{1,0:T(8,128)(2,1)S(1)}, bf16[288,128]{1,0:T(8,128)(2,1)S(1)}, u32[]{:S(2)}, u32[]{:S(2)}) collective-permute-start(bf16[288,128]{1,0:T(8,128)(2,1)S(1)} %get-tuple-element.43.refs_6_.refs_2_), channel_id=1, source_target_pairs={{0,16},{4,20},{8,24},{12,28},{16,0},{20,4},{24,8},{28,12},{1,17},{... | collective-permute-start | bytes 221192 | tf_op jit(solution)/shard_map/ppermute | solution.py:514
  17.9 0.6 %shard_map.106 = (bf16[2,128,512]{2,1,0:T(8,128)(2,1)S(1)}, bf16[64,512]{1,0:T(8,128)(2,1)S(1)}, bf16[320,128]{1,0:T(8,128)(2,1)S(1)}) custom-call(s32[1,1]{1,0:T(1,128)} %bitcast.5.refs_0_, bf16[320,128]{1,0:T(8,128)(2,1)S(1)} %get-tuple-element.34.refs_1_, bf16[320,128]{1,0:T(8,128)(2,1)S(1)} %collective-permute-done.refs_2_, ...), custom_call_target="tpu_custom_call" | custom-call | flops 100000000 | bytes 1000000 | tf_op jit(solution)/shard_map/pallas_call | solution.py:55
  18.5 2.6 %collective-permute-start.7 = (bf16[320,128]{1,0:T(8,128)(2,1)S(1)}, bf16[320,128]{1,0:T(8,128)(2,1)S(1)}, u32[]{:S(2)}, u32[]{:S(2)}) collective-permute-start(bf16[320,128]{1,0:T(8,128)(2,1)S(1)} %get-tuple-element.48.refs_2_.refs_3_), channel_id=1, source_target_pairs={{0,16},{4,20},{8,24},{12,28},{16,0},{20,4},{24,8},{28,12},{1,17},{... | collective-permute-start | bytes 245768 | tf_op jit(solution)/shard_map/ppermute | solution.py:514
  21.1 0.9 %shard_map.107.refs_1_ = f32[2,128,512]{2,1,0:T(8,128)S(1)} custom-call(bf16[2,128,512]{2,1,0:T(8,128)(2,1)S(1)} %get-tuple-element.46.refs_0_, bf16[64,512]{1,0:T(8,128)(2,1)S(1)} %get-tuple-element.47.refs_1_.refs_4_, bf16[320,128]{1,0:T(8,128)(2,1)S(1)} %get-tuple-element.48.refs_2_.refs_3_), custom_call_target="tpu_custom_call" | custom-call | flops 1000 | bytes 1000 | tf_op jit(solution)/shard_map/pallas_call | solution.py:55
  22.1 0.7 %shard_map.108 = (bf16[224,128]{1,0:T(8,128)(2,1)S(1)}, bf16[224,128]{1,0:T(8,128)(2,1)S(1)}, bf16[224,128]{1,0:T(8,128)(2,1)S(1)}, bf16[224,128]{1,0:T(8,128)(2,1)S(1)}, bf16[288,128]{1,0:T(8,128)(2,1)S(1)}) custom-call(s32[1,1]{1,0:T(1,128)} %bitcast.6.refs_0_, f32[2,128,512]{2,1,0:T(8,128)S(1)} %shard_map.107.refs_1_, ...), custom_call_target="tpu_custom_call" | custom-call | flops 50000000 | bytes 20000000 | tf_op jit(solution)/shard_map/pallas_call | solution.py:55
  22.8 0.9 %shard_map.109.refs_2_ = f32[2,128,512]{2,1,0:T(8,128)S(1)} custom-call(bf16[2,128,512]{2,1,0:T(8,128)(2,1)S(1)} %get-tuple-element.44.refs_0_, bf16[64,512]{1,0:T(8,128)(2,1)S(1)} %get-tuple-element.45.refs_1_.refs_5_, bf16[288,128]{1,0:T(8,128)(2,1)S(1)} %get-tuple-element.49.refs_2_.refs_7_), custom_call_target="tpu_custom_call" | custom-call | flops 5000000000 | bytes 1000 | tf_op jit(solution)/shard_map/pallas_call | solution.py:55
  23.9 0.7 %shard_map.110 = (bf16[448,128]{1,0:T(8,128)(2,1)S(1)}, bf16[448,128]{1,0:T(8,128)(2,1)S(1)}, bf16[448,128]{1,0:T(8,128)(2,1)S(1)}, bf16[448,128]{1,0:T(8,128)(2,1)S(1)}, bf16[320,128]{1,0:T(8,128)(2,1)S(1)}) custom-call(s32[1]{0:T(128)S(6)} %copy.12.refs_0_, s32[1,1]{1,0:T(1,128)} %bitcast.7.refs_1_, f32[2,128,512]{2,1,0:T(8,128)S(1)} %shard_map.109.refs_2_, ...), custom_call_target="tpu_custom_call" | custom-call | flops 50000000 | bytes 20000000 | tf_op jit(solution)/shard_map/pallas_call | solution.py:55
  24.6 1.6 %collective-permute-start.11 = (bf16[320,128]{1,0:T(8,128)(2,1)S(1)}, bf16[320,128]{1,0:T(8,128)(2,1)S(1)}, u32[]{:S(2)}, u32[]{:S(2)}) collective-permute-start(bf16[320,128]{1,0:T(8,128)(2,1)S(1)} %get-tuple-element.58.own.c0), channel_id=1, source_target_pairs={{0,2},{1,3},{2,0},{3,1},{4,6},{5,7},{6,4},{7,5},{8,10},{9,11},{10,... | collective-permute-start | bytes 245768 | tf_op jit(solution)/shard_map/ppermute | solution.py:514
  26.2 2.5 %collective-permute-start.8 = (bf16[448,128]{1,0:T(8,128)(2,1)S(1)}, bf16[448,128]{1,0:T(8,128)(2,1)S(1)}, u32[]{:S(2)}, u32[]{:S(2)}) collective-permute-start(bf16[448,128]{1,0:T(8,128)(2,1)S(1)} %get-tuple-element.55), channel_id=1, source_target_pairs={{0,12},{4,8},{8,4},{12,0},{16,28},{20,24},{24,20},{28,16},{1,13},{... | collective-permute-start | bytes 344072 | tf_op jit(solution)/shard_map/ppermute | solution.py:514
  28.7 0.4 %collective-permute-start.9 = (bf16[448,128]{1,0:T(8,128)(2,1)S(1)}, bf16[448,128]{1,0:T(8,128)(2,1)S(1)}, u32[]{:S(2)}, u32[]{:S(2)}) collective-permute-start(bf16[448,128]{1,0:T(8,128)(2,1)S(1)} %get-tuple-element.56), channel_id=1, source_target_pairs={{0,8},{4,12},{8,0},{12,4},{16,24},{20,28},{24,16},{28,20},{1,9},{5... | collective-permute-start | bytes 344072 | tf_op jit(solution)/shard_map/ppermute | solution.py:514
  29.1 0.6 %collective-permute-start.10 = (bf16[448,128]{1,0:T(8,128)(2,1)S(1)}, bf16[448,128]{1,0:T(8,128)(2,1)S(1)}, u32[]{:S(2)}, u32[]{:S(2)}) collective-permute-start(bf16[448,128]{1,0:T(8,128)(2,1)S(1)} %get-tuple-element.57), channel_id=1, source_target_pairs={{0,4},{4,0},{8,12},{12,8},{16,20},{20,16},{24,28},{28,24},{1,5},{5... | collective-permute-start | bytes 344072 | tf_op jit(solution)/shard_map/ppermute | solution.py:514
  29.8 1.3 %collective-permute-done.12.refs_4_.c2 = bf16[320,128]{1,0:T(8,128)(2,1)S(1)} collective-permute-done((bf16[320,128]{1,0:T(8,128)(2,1)S(1)}, bf16[320,128]{1,0:T(8,128)(2,1)S(1)}, u32[]{:S(2)}, u32[]{:S(2)}) %collective-permute-start.12) | collective-permute-done | bytes 81952 | tf_op jit(solution)/shard_map/ppermute | solution.py:514
  31.1 1.1 %shard_map.113 = (f32[273,1,224]{2,1,0:T(1,128)}, f32[1,16,273]{2,1,0:T(8,128)}) custom-call(bf16[320,128]{1,0:T(8,128)(2,1)S(1)} %get-tuple-element.58.own.c0, bf16[320,128]{1,0:T(8,128)(2,1)S(1)} %collective-permute-done.11.got.c1, bf16[320,128]{1,0:T(8,128)(2,1)S(1)} %collective-permute-done.12.refs_4_.c2, bf16[273,160]{1,0:T(8,128)(2,1)S(1)} %copy-done.3), custom_call_target="tpu_custom_call" | custom-call | flops 40000000 | bytes 1000000 | tf_op jit(solution)/shard_map/pallas_call | solution.py:55
  32.2 1.3 %collective-permute-done.9.refs_2_ = bf16[448,128]{1,0:T(8,128)(2,1)S(1)} collective-permute-done((bf16[448,128]{1,0:T(8,128)(2,1)S(1)}, bf16[448,128]{1,0:T(8,128)(2,1)S(1)}, u32[]{:S(2)}, u32[]{:S(2)}) %collective-permute-start.9) | collective-permute-done | bytes 114720 | tf_op jit(solution)/shard_map/ppermute | solution.py:514
  33.5 0.4 %collective-permute-done.10.refs_3_ = bf16[448,128]{1,0:T(8,128)(2,1)S(1)} collective-permute-done((bf16[448,128]{1,0:T(8,128)(2,1)S(1)}, bf16[448,128]{1,0:T(8,128)(2,1)S(1)}, u32[]{:S(2)}, u32[]{:S(2)}) %collective-permute-start.10) | collective-permute-done | bytes 114720 | tf_op jit(solution)/shard_map/ppermute | solution.py:514
  33.9 0.9 %shard_map.112 = bf16[1,128,1792]{2,1,0:T(8,128)(2,1)} custom-call(bf16[448,128]{1,0:T(8,128)(2,1)S(1)} %get-tuple-element.54.refs_0_, bf16[448,128]{1,0:T(8,128)(2,1)S(1)} %collective-permute-done.8.refs_1_, bf16[448,128]{1,0:T(8,128)(2,1)S(1)} %collective-permute-done.9.refs_2_, bf16[448,128]{1,0:T(8,128)(2,1)S(1)} %collective-permute-done.10.refs_3_, ...), custom_call_target="tpu_custom_call" | custom-call | flops 1000 | bytes 1000000 | tf_op jit(solution)/shard_map/pallas_call | solution.py:418
  (23 shorter events, 0.5 us)
Async XLA Ops:
  0.6 8.4 %copy-start = (bf16[1792,1792]{1,0:T(8,128)(2,1)S(1)}, bf16[1792,1792]{1,0:T(8,128)(2,1)}, u32[]{:S(2)}) copy-start(bf16[1792,1792]{1,0:T(8,128)(2,1)} %refs_3_.3) | copy-start | bytes 19267588
  0.6 8.4 %copy-start.2 = (bf16[1792,256]{1,0:T(8,128)(2,1)S(1)}, bf16[1792,256]{1,0:T(8,128)(2,1)}, u32[]{:S(2)}) copy-start(bf16[1792,256]{1,0:T(8,128)(2,1)} %refs_2_.3) | copy-start | bytes 2752516
  0.7 8.4 %copy-start.1 = (bf16[1792,256]{1,0:T(8,128)(2,1)S(1)}, bf16[1792,256]{1,0:T(8,128)(2,1)}, u32[]{:S(2)}) copy-start(bf16[1792,256]{1,0:T(8,128)(2,1)} %refs_1_.3) | copy-start | bytes 2752516
  0.7 8.4 %copy-start.4 = (f32[3,1792]{1,0:T(4,128)S(1)}, f32[3,1792]{1,0:T(4,128)}, u32[]{:S(2)}) copy-start(f32[3,1792]{1,0:T(4,128)} %refs_6_.1) | copy-start | bytes 64516
  3.7 9.7 %collective-permute-start.3 = (bf16[288,128]{1,0:T(8,128)(2,1)S(1)}, bf16[288,128]{1,0:T(8,128)(2,1)S(1)}, u32[]{:S(2)}, u32[]{:S(2)}) collective-permute-start(bf16[288,128]{1,0:T(8,128)(2,1)S(1)} %get-tuple-element.40), channel_id=1, source_target_pairs={{0,12},{4,8},{8,4},{12,0},{16,28},{20,24},{24,20},{28,16},{1,13},{... | collective-permute-start | bytes 221192 | tf_op jit(solution)/shard_map/ppermute | solution.py:514
  7.8 5.9 %collective-permute-start.4 = (bf16[288,128]{1,0:T(8,128)(2,1)S(1)}, bf16[288,128]{1,0:T(8,128)(2,1)S(1)}, u32[]{:S(2)}, u32[]{:S(2)}) collective-permute-start(bf16[288,128]{1,0:T(8,128)(2,1)S(1)} %get-tuple-element.41), channel_id=1, source_target_pairs={{0,8},{4,12},{8,0},{12,4},{16,24},{20,28},{24,16},{28,20},{1,9},{5... | collective-permute-start | bytes 221192 | tf_op jit(solution)/shard_map/ppermute | solution.py:514
  8.2 5.5 %collective-permute-start.5 = (bf16[288,128]{1,0:T(8,128)(2,1)S(1)}, bf16[288,128]{1,0:T(8,128)(2,1)S(1)}, u32[]{:S(2)}, u32[]{:S(2)}) collective-permute-start(bf16[288,128]{1,0:T(8,128)(2,1)S(1)} %get-tuple-element.42), channel_id=1, source_target_pairs={{0,4},{4,0},{8,12},{12,8},{16,20},{20,16},{24,28},{28,24},{1,5},{5... | collective-permute-start | bytes 221192 | tf_op jit(solution)/shard_map/ppermute | solution.py:514
  10.2 7.7 %collective-permute-start = (bf16[320,128]{1,0:T(8,128)(2,1)S(1)}, bf16[320,128]{1,0:T(8,128)(2,1)S(1)}, u32[]{:S(2)}, u32[]{:S(2)}) collective-permute-start(bf16[320,128]{1,0:T(8,128)(2,1)S(1)} %get-tuple-element.35), channel_id=1, source_target_pairs={{0,12},{4,8},{8,4},{12,0},{16,28},{20,24},{24,20},{28,16},{1,13},{... | collective-permute-start | bytes 245768 | tf_op jit(solution)/shard_map/ppermute | solution.py:514
  13.0 4.9 %collective-permute-start.1 = (bf16[320,128]{1,0:T(8,128)(2,1)S(1)}, bf16[320,128]{1,0:T(8,128)(2,1)S(1)}, u32[]{:S(2)}, u32[]{:S(2)}) collective-permute-start(bf16[320,128]{1,0:T(8,128)(2,1)S(1)} %get-tuple-element.36), channel_id=1, source_target_pairs={{0,8},{4,12},{8,0},{12,4},{16,24},{20,28},{24,16},{28,20},{1,9},{5... | collective-permute-start | bytes 245768 | tf_op jit(solution)/shard_map/ppermute | solution.py:514
  13.5 4.4 %collective-permute-start.2 = (bf16[320,128]{1,0:T(8,128)(2,1)S(1)}, bf16[320,128]{1,0:T(8,128)(2,1)S(1)}, u32[]{:S(2)}, u32[]{:S(2)}) collective-permute-start(bf16[320,128]{1,0:T(8,128)(2,1)S(1)} %get-tuple-element.37), channel_id=1, source_target_pairs={{0,4},{4,0},{8,12},{12,8},{16,20},{20,16},{24,28},{28,24},{1,5},{5... | collective-permute-start | bytes 245768 | tf_op jit(solution)/shard_map/ppermute | solution.py:514
  14.3 7.8 %collective-permute-start.6 = (bf16[288,128]{1,0:T(8,128)(2,1)S(1)}, bf16[288,128]{1,0:T(8,128)(2,1)S(1)}, u32[]{:S(2)}, u32[]{:S(2)}) collective-permute-start(bf16[288,128]{1,0:T(8,128)(2,1)S(1)} %get-tuple-element.43.refs_6_.refs_2_), channel_id=1, source_target_pairs={{0,16},{4,20},{8,24},{12,28},{16,0},{20,4},{24,8},{28,12},{1,17},{... | collective-permute-start | bytes 221192 | tf_op jit(solution)/shard_map/ppermute | solution.py:514
  18.5 5.4 %collective-permute-start.7 = (bf16[320,128]{1,0:T(8,128)(2,1)S(1)}, bf16[320,128]{1,0:T(8,128)(2,1)S(1)}, u32[]{:S(2)}, u32[]{:S(2)}) collective-permute-start(bf16[320,128]{1,0:T(8,128)(2,1)S(1)} %get-tuple-element.48.refs_2_.refs_3_), channel_id=1, source_target_pairs={{0,16},{4,20},{8,24},{12,28},{16,0},{20,4},{24,8},{28,12},{1,17},{... | collective-permute-start | bytes 245768 | tf_op jit(solution)/shard_map/ppermute | solution.py:514
  22.8 8.3 %copy-start.3 = (bf16[273,160]{1,0:T(8,128)(2,1)S(1)}, bf16[273,160]{1,0:T(8,128)(2,1)}, u32[]{:S(2)}) copy-start(bf16[273,160]{1,0:T(8,128)(2,1)} %constant.2.clone.spread) | copy-start | bytes 262084
  24.6 5.1 %collective-permute-start.11 = (bf16[320,128]{1,0:T(8,128)(2,1)S(1)}, bf16[320,128]{1,0:T(8,128)(2,1)S(1)}, u32[]{:S(2)}, u32[]{:S(2)}) collective-permute-start(bf16[320,128]{1,0:T(8,128)(2,1)S(1)} %get-tuple-element.58.own.c0), channel_id=1, source_target_pairs={{0,2},{1,3},{2,0},{3,1},{4,6},{5,7},{6,4},{7,5},{8,10},{9,11},{10,... | collective-permute-start | bytes 245768 | tf_op jit(solution)/shard_map/ppermute | solution.py:514
  26.2 6.0 %collective-permute-start.8 = (bf16[448,128]{1,0:T(8,128)(2,1)S(1)}, bf16[448,128]{1,0:T(8,128)(2,1)S(1)}, u32[]{:S(2)}, u32[]{:S(2)}) collective-permute-start(bf16[448,128]{1,0:T(8,128)(2,1)S(1)} %get-tuple-element.55), channel_id=1, source_target_pairs={{0,12},{4,8},{8,4},{12,0},{16,28},{20,24},{24,20},{28,16},{1,13},{... | collective-permute-start | bytes 344072 | tf_op jit(solution)/shard_map/ppermute | solution.py:514
  28.7 4.8 %collective-permute-start.9 = (bf16[448,128]{1,0:T(8,128)(2,1)S(1)}, bf16[448,128]{1,0:T(8,128)(2,1)S(1)}, u32[]{:S(2)}, u32[]{:S(2)}) collective-permute-start(bf16[448,128]{1,0:T(8,128)(2,1)S(1)} %get-tuple-element.56), channel_id=1, source_target_pairs={{0,8},{4,12},{8,0},{12,4},{16,24},{20,28},{24,16},{28,20},{1,9},{5... | collective-permute-start | bytes 344072 | tf_op jit(solution)/shard_map/ppermute | solution.py:514
  29.1 4.8 %collective-permute-start.10 = (bf16[448,128]{1,0:T(8,128)(2,1)S(1)}, bf16[448,128]{1,0:T(8,128)(2,1)S(1)}, u32[]{:S(2)}, u32[]{:S(2)}) collective-permute-start(bf16[448,128]{1,0:T(8,128)(2,1)S(1)} %get-tuple-element.57), channel_id=1, source_target_pairs={{0,4},{4,0},{8,12},{12,8},{16,20},{20,16},{24,28},{28,24},{1,5},{5... | collective-permute-start | bytes 344072 | tf_op jit(solution)/shard_map/ppermute | solution.py:514
  29.8 1.3 %collective-permute-start.12 = (bf16[320,128]{1,0:T(8,128)(2,1)S(1)}, bf16[320,128]{1,0:T(8,128)(2,1)S(1)}, u32[]{:S(2)}, u32[]{:S(2)}) collective-permute-start(bf16[320,128]{1,0:T(8,128)(2,1)S(1)} %shard_map.111), channel_id=1, source_target_pairs={{0,1},{1,0},{2,3},{3,2},{4,5},{5,4},{6,7},{7,6},{8,9},{9,8},{10,11... | collective-permute-start | bytes 245768 | tf_op jit(solution)/shard_map/ppermute | solution.py:514
